TPU v7x, 256 devices: a whole 4x4x8 slice. The times are simulated.
256 devices in a mesh: level: 8 (over y, core), grp: 32 (over z, x).
Axes of the slice: x: 4, y: 4, z: 8, core: 2. Of those that a mesh axis runs over, the one named last changes fastest.
Arguments:
- right_side: bfloat16 [8, 1024, 128, 256], P('level', 'grp'), may hold values from -6 to 6
- diag_inverse: bfloat16 [8, 1024, 128, 128], P('level', 'grp'), as said below
- below_block: bfloat16 [8, 1024, 64, 128], P('level', 'grp'), may hold values from -0.75 to 0.75
- parent_device: int32 [8, 1024, 1], replicated, may hold values from 0 to 31; in each aligned block of 32 rows (0 to 31, 32 to 63, ..., all dimensions but the last counted through in order) at most 2 rows name the same one
- parent_slot: int32 [8, 1024], replicated, may hold values from 0 to 31
- row_index: int32 [8, 64, 1024], replicated, may hold values from 0 to 127, as said below
Outputs:
- solution: bfloat16 [8, 1024, 128, 256], P('level', 'grp')
- outgoing: bfloat16 [8, 1024, 64, 256], P('level', 'grp')
Inputs may be any that keep to these rules, and one draw needn't show every extreme that they name: `parent_device`: among the 32 supernodes of one device, at most 2 have parents on one device; exactly 2 do on some devices. `row_index`: for each supernode, its 64 rows are distinct and increasing. `diag_inverse`: lower triangular with a positive diagonal.
All inputs are finite; a program needn't handle non-finite values.
Results may differ from a plain program's by a relative error of at most 0.009.
Values may be sent and summed in bfloat16 or wider, within the bound.
No kernel may reach another device: no remote copies, remote signals or barrier semaphores. Data moves between devices by JAX's collectives and lax.ppermute only.
A program may use at most 128 MiB of HBM per device.

v0:
```python
import jax
import jax.numpy as jnp
from jax import lax
from jax.sharding import PartitionSpec as P

CAP = 2


def from_behind(value, axis, by):
    peers = lax.axis_size(axis)
    pairs = [(i, i + by) for i in range(peers) if 0 <= i + by < peers]
    return lax.ppermute(value, axis, pairs)


def ranking(owners):
    count = owners.shape[-1]
    same = owners[..., :, None] == owners[..., None, :]
    earlier = lax.broadcasted_iota(jnp.int32, (count, count), 1) < lax.broadcasted_iota(
        jnp.int32, (count, count), 0
    )
    return jnp.sum(jnp.logical_and(same, earlier).astype(jnp.int32), axis=-1)


def shards(right_side, diag_inverse, below_block, parent_device, parent_slot, row_index):
    level_count = lax.axis_size("level")
    group = lax.axis_size("grp")
    level_id = lax.axis_index("level")
    member = lax.axis_index("grp")
    nodes_dev = right_side.shape[1]
    block = right_side.shape[2]
    columns = right_side.shape[3]
    update_rows = below_block.shape[2]

    def routing_for(sender_level):
        devices = lax.dynamic_index_in_dim(parent_device[:, :, 0], sender_level, 0, keepdims=False)
        own = lax.dynamic_slice_in_dim(devices, member * nodes_dev, nodes_dev)
        slots_all = lax.dynamic_index_in_dim(parent_slot, sender_level, 0, keepdims=False)
        rows_all = lax.dynamic_index_in_dim(row_index, sender_level, 0, keepdims=False)
        sender_dev = devices.reshape(group, nodes_dev)
        sender_slot = slots_all.reshape(group, nodes_dev)
        sender_rows = jnp.transpose(rows_all.reshape(update_rows, group, nodes_dev), (1, 2, 0))
        sender_rank = ranking(sender_dev)
        anchor = lax.broadcasted_iota(jnp.int32, (group, nodes_dev), 0)
        position = jnp.where(sender_dev == member, anchor * CAP + sender_rank, group * CAP).reshape(
            -1
        )
        target_slot = (
            jnp.full((group * CAP,), nodes_dev, jnp.int32)
            .at[position]
            .set(sender_slot.reshape(-1), mode="drop")
        )
        target_rows = (
            jnp.zeros((group * CAP, update_rows), jnp.int32)
            .at[position]
            .set(sender_rows.reshape(-1, update_rows), mode="drop")
        )
        return (own, (target_slot[:, None] * block + target_rows).reshape(-1))

    def pack(update, owners):
        slots = owners * CAP + ranking(owners)
        buffer = jnp.zeros((group * CAP, update_rows, update.shape[-1]), jnp.bfloat16)
        return buffer.at[slots].set(update)

    def place(received, target):
        span = received.shape[-1]
        inflow = (
            jnp.zeros((nodes_dev * block, span), jnp.float32)
            .at[target]
            .add(received.astype(jnp.float32).reshape(-1, span), mode="drop")
        )
        return inflow.reshape(nodes_dev, block, span)

    def solve_level(inverse, below, loads, arrived):
        reduced = (loads.astype(jnp.float32) - arrived).astype(jnp.bfloat16)
        solved = jnp.einsum(
            "nij,njc->nic", inverse, reduced, preferred_element_type=jnp.float32
        ).astype(jnp.bfloat16)
        update = jnp.einsum(
            "nri,nic->nrc", below, solved, preferred_element_type=jnp.float32
        ).astype(jnp.bfloat16)
        return (solved, update)

    tiles = 1
    inverse = diag_inverse[0]
    below = below_block[0]
    source = right_side[0]
    previous = jnp.maximum(level_id - 1, 0)
    own_local = routing_for(level_id)[0]
    prev_local, target = routing_for(previous)

    def compute(pending):
        return solve_level(inverse, below, source, pending)

    steps_total = level_count + tiles - 1

    def advance(step, carry):
        pending, solved_all, updates_all = carry
        solved, update = compute(pending)
        solved_all = solved
        updates_all = update
        routed = lax.all_to_all(
            pack(update, own_local), "grp", split_axis=0, concat_axis=0, tiled=True
        )
        received = from_behind(routed, "level", 1)
        pending = place(received, target)
        return (pending, solved_all, updates_all)

    start_state = (
        jnp.zeros((nodes_dev, block, columns), jnp.float32),
        jnp.zeros((nodes_dev, block, columns), jnp.bfloat16),
        jnp.zeros((nodes_dev, update_rows, columns), jnp.bfloat16),
    )
    pending, solved_all, updates_all = lax.fori_loop(0, steps_total - 1, advance, start_state)
    solved, update = compute(pending)
    solved_all = solved
    updates_all = update
    return (solved_all[None], updates_all[None])


def solution(mesh):
    return jax.shard_map(
        shards,
        mesh=mesh,
        in_specs=(
            P("level", "grp", None, None),
            P("level", "grp", None, None),
            P("level", "grp", None, None),
            P(),
            P(),
            P(),
        ),
        out_specs=(P("level", "grp", None, None), P("level", "grp", None, None)),
        check_vma=False,
    )
```

profile of v0, /device:TPU:10, one launch (start us, length us, event | category | flops | bytes accessed | tf_op | source)
XLA Modules:
  0.0 869.8 jit_solution(10616530588567499038)
XLA Ops:
  7.4 4.3 scatter_custom_fusion.2
  12.8 4.1 copy.15
  19.3 837.7 %while.11 = (s32[]{:T(128)}, f32[32,128,256]{2,1,0:T(8,128)}, s32[4096]{0:T(1024)S(1)}, s32[32]{0:T(128)S(1)}, s32[32]{0:T(128)S(1)}, /*index=5*/bf16[32,128,256...) while((s32[]{:T(128)}, f32[32,128,256]{2,1,0:T(8,128)}, ...), condition=%wide.region_7.8_spmd, body=%wide.region_4.0_spmd.sunk | while | flops 409481376 | bytes 41452188 | solution.py:113
  19.3 5.6 copy.21
  24.9 4.6 fusion.41
  31.0 4.6 scatter_fusion
  35.6 62.3 %all_to_all.7 = bf16[64,64,256]{2,1,0:T(8,128)(2,1)} all-to-all(bf16[64,64,256]{2,1,0:T(8,128)(2,1)} %scatter_fusion), channel_id=1, replica_groups=mesh['level'=8,'grp'=32] {'grp'}, dimensions={0} | all-to-all | bytes 4194304 | tf_op jit(solution)/shard_map/while/body/eval_jaxpr/all_to_all | solution.py:101
  99.8 25.7 %collective-permute-done = bf16[64,64,256]{2,1,0:T(8,128)(2,1)} collective-permute-done((bf16[64,64,256]{2,1,0:T(8,128)(2,1)}, bf16[64,64,256]{2,1,0:T(8,128)(2,1)}, u32[]{:S(2)}, u32[]{:S(2)}) %collective-permute-start) | collective-permute-done | bytes 2097184 | tf_op jit(solution)/shard_map/while/body/eval_jaxpr/ppermute | solution.py:12
  125.5 23.1 %scatter_custom_fusion.12 = f32[4096,256]{1,0:T(8,128)} fusion(s32[4096]{0:T(1024)S(1)} %bitcast.73, bf16[4096,256]{1,0:T(8,128)(2,1)} %bitcast.63, f32[]{:T(128)} %constant.79.clone.1..sunk), kind=kCustom, calls=%fused_computation.4.clone.1 | custom fusion | flops 2097152 | bytes 6291460 | tf_op jit(solution)/shard_map/while/body/eval_jaxpr/scatter-add | solution.py:69
  148.6 5.6 copy.21
  154.2 4.6 fusion.41
  160.3 4.6 scatter_fusion
  164.9 55.6 %all_to_all.7 = bf16[64,64,256]{2,1,0:T(8,128)(2,1)} all-to-all(bf16[64,64,256]{2,1,0:T(8,128)(2,1)} %scatter_fusion), channel_id=1, replica_groups=mesh['level'=8,'grp'=32] {'grp'}, dimensions={0} | all-to-all | bytes 4194304 | tf_op jit(solution)/shard_map/while/body/eval_jaxpr/all_to_all | solution.py:101
  222.4 25.7 %collective-permute-done = bf16[64,64,256]{2,1,0:T(8,128)(2,1)} collective-permute-done((bf16[64,64,256]{2,1,0:T(8,128)(2,1)}, bf16[64,64,256]{2,1,0:T(8,128)(2,1)}, u32[]{:S(2)}, u32[]{:S(2)}) %collective-permute-start) | collective-permute-done | bytes 2097184 | tf_op jit(solution)/shard_map/while/body/eval_jaxpr/ppermute | solution.py:12
  248.1 23.1 %scatter_custom_fusion.12 = f32[4096,256]{1,0:T(8,128)} fusion(s32[4096]{0:T(1024)S(1)} %bitcast.73, bf16[4096,256]{1,0:T(8,128)(2,1)} %bitcast.63, f32[]{:T(128)} %constant.79.clone.1..sunk), kind=kCustom, calls=%fused_computation.4.clone.1 | custom fusion | flops 2097152 | bytes 6291460 | tf_op jit(solution)/shard_map/while/body/eval_jaxpr/scatter-add | solution.py:69
  271.2 5.6 copy.21
  276.8 4.6 fusion.41
  282.9 4.6 scatter_fusion
  287.5 55.3 %all_to_all.7 = bf16[64,64,256]{2,1,0:T(8,128)(2,1)} all-to-all(bf16[64,64,256]{2,1,0:T(8,128)(2,1)} %scatter_fusion), channel_id=1, replica_groups=mesh['level'=8,'grp'=32] {'grp'}, dimensions={0} | all-to-all | bytes 4194304 | tf_op jit(solution)/shard_map/while/body/eval_jaxpr/all_to_all | solution.py:101
  344.7 25.7 %collective-permute-done = bf16[64,64,256]{2,1,0:T(8,128)(2,1)} collective-permute-done((bf16[64,64,256]{2,1,0:T(8,128)(2,1)}, bf16[64,64,256]{2,1,0:T(8,128)(2,1)}, u32[]{:S(2)}, u32[]{:S(2)}) %collective-permute-start) | collective-permute-done | bytes 2097184 | tf_op jit(solution)/shard_map/while/body/eval_jaxpr/ppermute | solution.py:12
  370.4 23.1 %scatter_custom_fusion.12 = f32[4096,256]{1,0:T(8,128)} fusion(s32[4096]{0:T(1024)S(1)} %bitcast.73, bf16[4096,256]{1,0:T(8,128)(2,1)} %bitcast.63, f32[]{:T(128)} %constant.79.clone.1..sunk), kind=kCustom, calls=%fused_computation.4.clone.1 | custom fusion | flops 2097152 | bytes 6291460 | tf_op jit(solution)/shard_map/while/body/eval_jaxpr/scatter-add | solution.py:69
  393.5 5.6 copy.21
  399.1 4.6 fusion.41
  405.2 4.6 scatter_fusion
  409.8 52.4 %all_to_all.7 = bf16[64,64,256]{2,1,0:T(8,128)(2,1)} all-to-all(bf16[64,64,256]{2,1,0:T(8,128)(2,1)} %scatter_fusion), channel_id=1, replica_groups=mesh['level'=8,'grp'=32] {'grp'}, dimensions={0} | all-to-all | bytes 4194304 | tf_op jit(solution)/shard_map/while/body/eval_jaxpr/all_to_all | solution.py:101
  464.1 25.7 %collective-permute-done = bf16[64,64,256]{2,1,0:T(8,128)(2,1)} collective-permute-done((bf16[64,64,256]{2,1,0:T(8,128)(2,1)}, bf16[64,64,256]{2,1,0:T(8,128)(2,1)}, u32[]{:S(2)}, u32[]{:S(2)}) %collective-permute-start) | collective-permute-done | bytes 2097184 | tf_op jit(solution)/shard_map/while/body/eval_jaxpr/ppermute | solution.py:12
  489.9 23.1 %scatter_custom_fusion.12 = f32[4096,256]{1,0:T(8,128)} fusion(s32[4096]{0:T(1024)S(1)} %bitcast.73, bf16[4096,256]{1,0:T(8,128)(2,1)} %bitcast.63, f32[]{:T(128)} %constant.79.clone.1..sunk), kind=kCustom, calls=%fused_computation.4.clone.1 | custom fusion | flops 2097152 | bytes 6291460 | tf_op jit(solution)/shard_map/while/body/eval_jaxpr/scatter-add | solution.py:69
  512.9 5.6 copy.21
  518.5 4.6 fusion.41
  524.6 4.6 scatter_fusion
  529.2 50.1 %all_to_all.7 = bf16[64,64,256]{2,1,0:T(8,128)(2,1)} all-to-all(bf16[64,64,256]{2,1,0:T(8,128)(2,1)} %scatter_fusion), channel_id=1, replica_groups=mesh['level'=8,'grp'=32] {'grp'}, dimensions={0} | all-to-all | bytes 4194304 | tf_op jit(solution)/shard_map/while/body/eval_jaxpr/all_to_all | solution.py:101
  581.2 25.7 %collective-permute-done = bf16[64,64,256]{2,1,0:T(8,128)(2,1)} collective-permute-done((bf16[64,64,256]{2,1,0:T(8,128)(2,1)}, bf16[64,64,256]{2,1,0:T(8,128)(2,1)}, u32[]{:S(2)}, u32[]{:S(2)}) %collective-permute-start) | collective-permute-done | bytes 2097184 | tf_op jit(solution)/shard_map/while/body/eval_jaxpr/ppermute | solution.py:12
  606.9 23.1 %scatter_custom_fusion.12 = f32[4096,256]{1,0:T(8,128)} fusion(s32[4096]{0:T(1024)S(1)} %bitcast.73, bf16[4096,256]{1,0:T(8,128)(2,1)} %bitcast.63, f32[]{:T(128)} %constant.79.clone.1..sunk), kind=kCustom, calls=%fused_computation.4.clone.1 | custom fusion | flops 2097152 | bytes 6291460 | tf_op jit(solution)/shard_map/while/body/eval_jaxpr/scatter-add | solution.py:69
  630.0 5.6 copy.21
  635.6 4.6 fusion.41
  641.7 4.6 scatter_fusion
  646.3 47.6 %all_to_all.7 = bf16[64,64,256]{2,1,0:T(8,128)(2,1)} all-to-all(bf16[64,64,256]{2,1,0:T(8,128)(2,1)} %scatter_fusion), channel_id=1, replica_groups=mesh['level'=8,'grp'=32] {'grp'}, dimensions={0} | all-to-all | bytes 4194304 | tf_op jit(solution)/shard_map/while/body/eval_jaxpr/all_to_all | solution.py:101
  695.9 25.7 %collective-permute-done = bf16[64,64,256]{2,1,0:T(8,128)(2,1)} collective-permute-done((bf16[64,64,256]{2,1,0:T(8,128)(2,1)}, bf16[64,64,256]{2,1,0:T(8,128)(2,1)}, u32[]{:S(2)}, u32[]{:S(2)}) %collective-permute-start) | collective-permute-done | bytes 2097184 | tf_op jit(solution)/shard_map/while/body/eval_jaxpr/ppermute | solution.py:12
  721.6 23.1 %scatter_custom_fusion.12 = f32[4096,256]{1,0:T(8,128)} fusion(s32[4096]{0:T(1024)S(1)} %bitcast.73, bf16[4096,256]{1,0:T(8,128)(2,1)} %bitcast.63, f32[]{:T(128)} %constant.79.clone.1..sunk), kind=kCustom, calls=%fused_computation.4.clone.1 | custom fusion | flops 2097152 | bytes 6291460 | tf_op jit(solution)/shard_map/while/body/eval_jaxpr/scatter-add | solution.py:69
  744.7 5.6 copy.21
  750.2 4.6 fusion.41
  756.4 4.6 scatter_fusion
  761.0 45.4 %all_to_all.7 = bf16[64,64,256]{2,1,0:T(8,128)(2,1)} all-to-all(bf16[64,64,256]{2,1,0:T(8,128)(2,1)} %scatter_fusion), channel_id=1, replica_groups=mesh['level'=8,'grp'=32] {'grp'}, dimensions={0} | all-to-all | bytes 4194304 | tf_op jit(solution)/shard_map/while/body/eval_jaxpr/all_to_all | solution.py:101
  808.3 25.7 %collective-permute-done = bf16[64,64,256]{2,1,0:T(8,128)(2,1)} collective-permute-done((bf16[64,64,256]{2,1,0:T(8,128)(2,1)}, bf16[64,64,256]{2,1,0:T(8,128)(2,1)}, u32[]{:S(2)}, u32[]{:S(2)}) %collective-permute-start) | collective-permute-done | bytes 2097184 | tf_op jit(solution)/shard_map/while/body/eval_jaxpr/ppermute | solution.py:12
  834.0 23.1 %scatter_custom_fusion.12 = f32[4096,256]{1,0:T(8,128)} fusion(s32[4096]{0:T(1024)S(1)} %bitcast.73, bf16[4096,256]{1,0:T(8,128)(2,1)} %bitcast.63, f32[]{:T(128)} %constant.79.clone.1..sunk), kind=kCustom, calls=%fused_computation.4.clone.1 | custom fusion | flops 2097152 | bytes 6291460 | tf_op jit(solution)/shard_map/while/body/eval_jaxpr/scatter-add | solution.py:69
  857.1 5.2 fusion.14
  862.3 4.1 copy.17
  866.4 3.4 fusion.15
  (50 shorter events, 34.6 us)
Async XLA Ops:
  0.6 2.6 copy-start
  97.9 27.7 %collective-permute-start = (bf16[64,64,256]{2,1,0:T(8,128)(2,1)}, bf16[64,64,256]{2,1,0:T(8,128)(2,1)}, u32[]{:S(2)}, u32[]{:S(2)}) collective-permute-start(bf16[64,64,256]{2,1,0:T(8,128)(2,1)} %all_to_all.7), channel_id=1, source_target_pairs={{0,32},{32,64},{64,96},{96,128},{128,160},{160,192},{192,224},{1,3... | collective-permute-start | bytes 6291464 | tf_op jit(solution)/shard_map/while/body/eval_jaxpr/ppermute | solution.py:12
  220.5 27.7 %collective-permute-start = (bf16[64,64,256]{2,1,0:T(8,128)(2,1)}, bf16[64,64,256]{2,1,0:T(8,128)(2,1)}, u32[]{:S(2)}, u32[]{:S(2)}) collective-permute-start(bf16[64,64,256]{2,1,0:T(8,128)(2,1)} %all_to_all.7), channel_id=1, source_target_pairs={{0,32},{32,64},{64,96},{96,128},{128,160},{160,192},{192,224},{1,3... | collective-permute-start | bytes 6291464 | tf_op jit(solution)/shard_map/while/body/eval_jaxpr/ppermute | solution.py:12
  342.8 27.7 %collective-permute-start = (bf16[64,64,256]{2,1,0:T(8,128)(2,1)}, bf16[64,64,256]{2,1,0:T(8,128)(2,1)}, u32[]{:S(2)}, u32[]{:S(2)}) collective-permute-start(bf16[64,64,256]{2,1,0:T(8,128)(2,1)} %all_to_all.7), channel_id=1, source_target_pairs={{0,32},{32,64},{64,96},{96,128},{128,160},{160,192},{192,224},{1,3... | collective-permute-start | bytes 6291464 | tf_op jit(solution)/shard_map/while/body/eval_jaxpr/ppermute | solution.py:12
  462.2 27.7 %collective-permute-start = (bf16[64,64,256]{2,1,0:T(8,128)(2,1)}, bf16[64,64,256]{2,1,0:T(8,128)(2,1)}, u32[]{:S(2)}, u32[]{:S(2)}) collective-permute-start(bf16[64,64,256]{2,1,0:T(8,128)(2,1)} %all_to_all.7), channel_id=1, source_target_pairs={{0,32},{32,64},{64,96},{96,128},{128,160},{160,192},{192,224},{1,3... | collective-permute-start | bytes 6291464 | tf_op jit(solution)/shard_map/while/body/eval_jaxpr/ppermute | solution.py:12
  579.3 27.7 %collective-permute-start = (bf16[64,64,256]{2,1,0:T(8,128)(2,1)}, bf16[64,64,256]{2,1,0:T(8,128)(2,1)}, u32[]{:S(2)}, u32[]{:S(2)}) collective-permute-start(bf16[64,64,256]{2,1,0:T(8,128)(2,1)} %all_to_all.7), channel_id=1, source_target_pairs={{0,32},{32,64},{64,96},{96,128},{128,160},{160,192},{192,224},{1,3... | collective-permute-start | bytes 6291464 | tf_op jit(solution)/shard_map/while/body/eval_jaxpr/ppermute | solution.py:12
  693.9 27.7 %collective-permute-start = (bf16[64,64,256]{2,1,0:T(8,128)(2,1)}, bf16[64,64,256]{2,1,0:T(8,128)(2,1)}, u32[]{:S(2)}, u32[]{:S(2)}) collective-permute-start(bf16[64,64,256]{2,1,0:T(8,128)(2,1)} %all_to_all.7), channel_id=1, source_target_pairs={{0,32},{32,64},{64,96},{96,128},{128,160},{160,192},{192,224},{1,3... | collective-permute-start | bytes 6291464 | tf_op jit(solution)/shard_map/while/body/eval_jaxpr/ppermute | solution.py:12
  806.3 27.7 %collective-permute-start = (bf16[64,64,256]{2,1,0:T(8,128)(2,1)}, bf16[64,64,256]{2,1,0:T(8,128)(2,1)}, u32[]{:S(2)}, u32[]{:S(2)}) collective-permute-start(bf16[64,64,256]{2,1,0:T(8,128)(2,1)} %all_to_all.7), channel_id=1, source_target_pairs={{0,32},{32,64},{64,96},{96,128},{128,160},{160,192},{192,224},{1,3... | collective-permute-start | bytes 6291464 | tf_op jit(solution)/shard_map/while/body/eval_jaxpr/ppermute | solution.py:12
  862.3 4.1 copy-start.1
where the time goes:
time: 873 us; the launch traced here: 870 us
  blocking collectives  369 us (42%)
  waiting for transfers between devices  180 us (21%)
  other arithmetic  163 us (19%)
  local copies, waits for them, and re-layouts  103 us (12%)
  matrix products  40.7 us (5%)
  starting transfers between devices  13.4 us (2%)
    all_to_all x7, blocking collectives, advance(): lax.all_to_all(pack(update, own_local), 'grp', split_axis=0, concat_axis=...  369 us
    ppermute x7, waiting for transfers between devices, from_behind(): return lax.ppermute(value, axis, pairs)  180 us
    scatter-add x7, other arithmetic, place(): inflow = jnp.zeros((nodes_dev * block, span), jnp.float32).at[target].add...  161 us
    another operation x14, local copies, waits for them, and re-layouts  49.8 us
    dot_general x8, matrix products, solve_level(): jnp.einsum('nri,nic->nrc', below, solved, preferred_element_type=jnp.floa...  35.4 us
    scatter x7, local copies, waits for them, and re-layouts, pack(): return buffer.at[slots].set(update)  32.1 us
  transfers between devices with their start and end apart: 7, of which 7 were waited for; matrix products, arithmetic and copies ran while one was open for 0% of the time, Pallas kernels for 0%

commit v1 on v0

v1 whole, which is shorter than its diff:
```python
import functools

import jax
import jax.numpy as jnp
from jax import lax
from jax.experimental import pallas as pl
from jax.experimental.pallas import tpu as pltpu
from jax.sharding import PartitionSpec as P

VMEM = 48 * 1024 * 1024
F32 = jnp.float32
BF16 = jnp.bfloat16


def dot(a, b):
    return jnp.dot(a, b, preferred_element_type=F32)


def dot_nt(a, b):
    return lax.dot_general(a, b, (((1,), (1,)), ((), ())), preferred_element_type=F32)


def low_lanes(shape, half):
    return lax.broadcasted_iota(jnp.int32, shape, len(shape) - 1) < half


def prepare_kernel(rhs_ref, inv_ref, below_ref, gain_ref, load_ref):
    nodes = rhs_ref.shape[0]
    levels, _, span, _ = load_ref.shape
    for pair in range(nodes // 2):
        halves = []
        for node in (2 * pair, 2 * pair + 1):
            inv, below = inv_ref[node], below_ref[node]
            gain_ref[node] = dot(below, inv).astype(BF16)
            solved = dot(inv, rhs_ref[node]).astype(BF16)
            halves.append(dot(below, solved))
        both = jnp.concatenate(halves, axis=0).T.astype(BF16)
        load_ref[:, pair] = both.reshape(levels, span, both.shape[1])


def operator_kernel(slot_ref, rows_ref, gain_ref, op_ref):
    senders, rows, lanes = op_ref.shape
    nodes, _, block = gain_ref.shape
    low = low_lanes((rows, lanes), rows)
    for s in range(senders):
        hot = (
            lax.broadcasted_iota(jnp.int32, (block, lanes), 0) == rows_ref[s : s + 1, :]
        ).astype(BF16)
        first = dot(gain_ref[jnp.minimum(slot_ref[2 * s], nodes - 1)], hot)
        second = dot(gain_ref[jnp.minimum(slot_ref[2 * s + 1], nodes - 1)], hot)
        op_ref[s] = jnp.where(low, first, second).astype(BF16)


def pack(values, take_ref, level, send_ref):
    senders, span, lanes = send_ref.shape
    low = low_lanes((span, lanes), lanes // 2)
    for d in range(senders):
        first = values[take_ref[level, 2 * d]]
        second = values[take_ref[level, 2 * d + 1]]
        send_ref[d] = jnp.where(low, first, second)


def both_halves(pair_value, odd, low, half):
    turned = pltpu.roll(pair_value, half, 1)
    return jnp.where(low, turned, pair_value) if odd else jnp.where(low, pair_value, turned)


def first_kernel(take_ref, load_ref, send_ref, values):
    _, pairs, span, lanes = load_ref.shape
    low = low_lanes((span, lanes), lanes // 2)
    for pair in range(pairs):
        value = load_ref[0, pair].astype(F32)
        for odd in (0, 1):
            values[2 * pair + odd] = both_halves(value, odd, low, lanes // 2).astype(BF16)
    values[2 * pairs] = jnp.zeros((span, lanes), BF16)
    pack(values, take_ref, 0, send_ref)


def hop_kernel(level, take_ref, slot_ref, got_ref, op_ref, load_ref, send_ref, total, values):
    senders, span, lanes = got_ref.shape
    _, pairs, _, _ = load_ref.shape
    half = lanes // 2
    low = low_lanes((span, lanes), half)
    low_op = low_lanes((half, lanes), half)
    total[...] = jnp.zeros_like(total)
    for s in range(senders):
        op = op_ref[0, s]
        zero = jnp.zeros_like(op)
        split = jnp.concatenate(
            [jnp.where(low_op, op, zero), jnp.where(low_op, zero, op)], axis=0
        )
        part = dot_nt(got_ref[s], split)
        one = slot_ref[level - 1, 2 * s]
        two = slot_ref[level - 1, 2 * s + 1]
        total[one] += jnp.where(low, part, 0.0)
        total[two] += jnp.where(low, 0.0, part)
    for pair in range(pairs):
        value = load_ref[0, pair].astype(F32)
        for odd in (0, 1):
            node = 2 * pair + odd
            come = total[node]
            come = come + pltpu.roll(come, half, 1)
            values[node] = (both_halves(value, odd, low, half) - come).astype(BF16)
    values[2 * pairs] = jnp.zeros((span, lanes), BF16)
    pack(values, take_ref, level, send_ref)


def finish_kernel(
    steps, slot_ref, rows_ref, got_ref, rhs_ref, inv_ref, below_ref, sol_ref, out_ref, inflow
):
    step = pl.program_id(0)
    chunks, senders, span, lanes = got_ref.shape
    block = rhs_ref.shape[1]
    half = lanes // 2

    @pl.when(step == 0)
    def _():
        inflow[...] = jnp.zeros_like(inflow)

    @pl.when(step < steps)
    def _():
        low = low_lanes((block, lanes), half)
        for s in range(senders):
            rows = rows_ref[pl.ds(step * senders + s, 1), :]
            hot = lax.broadcasted_iota(jnp.int32, (block, lanes), 0) == rows
            hot = jnp.concatenate(
                [jnp.logical_and(hot, low), jnp.logical_and(hot, jnp.logical_not(low))], axis=0
            )
            got = got_ref[:, s].reshape(chunks * span, lanes)
            part = dot_nt(hot.astype(BF16), got)
            one = slot_ref[2 * (step * senders + s)]
            two = slot_ref[2 * (step * senders + s) + 1]
            inflow[one] += part[:block]
            inflow[two] += part[block:]

    @pl.when(step >= steps)
    def _():
        nodes = rhs_ref.shape[0]
        base = (step - steps) * nodes
        for n in range(nodes):
            reduced = (rhs_ref[n].astype(F32) - inflow[base + n]).astype(BF16)
            solved = dot(inv_ref[n], reduced).astype(BF16)
            sol_ref[0, n] = solved
            out_ref[0, n] = dot(below_ref[n], solved).astype(BF16)


def params(*semantics):
    return pltpu.CompilerParams(vmem_limit_bytes=VMEM, dimension_semantics=semantics or None)


SMEM_SPEC = pl.BlockSpec(memory_space=pltpu.SMEM)
VMEM_SPEC = pl.BlockSpec(memory_space=pltpu.VMEM)


def shards(right_side, diag_inverse, below_block, parent_device, parent_slot, row_index):
    levels = lax.axis_size("level")
    group = lax.axis_size("grp")
    level_id = lax.axis_index("level")
    member = lax.axis_index("grp")
    _, nodes, block, columns = right_side.shape
    rows = below_block.shape[2]
    span = columns // levels
    lanes = 2 * rows
    pairs = nodes // 2
    hops = levels - 1

    devices = parent_device[:hops, :, 0].reshape(hops, group, nodes)
    slots = parent_slot[:hops].reshape(hops, group, nodes)
    place = lax.broadcasted_iota(jnp.int32, (hops, group, nodes), 2)

    def ends(named):
        first = jnp.min(jnp.where(named, place, nodes), axis=-1)
        last = jnp.max(jnp.where(named, place, -1), axis=-1)
        return first, jnp.where(last > first, last, nodes)

    first, last = ends(devices == member)
    own = lax.dynamic_index_in_dim(devices, member, 1, keepdims=True)
    take = jnp.stack(ends(own == lax.broadcasted_iota(jnp.int32, (hops, group, nodes), 1)), -1)
    take = take.reshape(hops, 2 * group)

    def slot_of(which):
        hit = place == which[..., None]
        found = jnp.sum(jnp.where(hit, slots, 0), axis=-1)
        return jnp.where(which < nodes, found, nodes)

    slot = jnp.stack([slot_of(first), slot_of(last)], -1).reshape(hops, 2 * group)

    before = jnp.maximum(level_id - 1, 0)
    home_slot = lax.dynamic_index_in_dim(slot, before, 0, keepdims=False)
    home_slot = jnp.where(level_id > 0, home_slot, nodes)
    landing = lax.dynamic_index_in_dim(row_index, before, 0, keepdims=False)
    landing = landing.reshape(rows, group, nodes)

    def rows_of(which):
        which = lax.dynamic_index_in_dim(which, before, 0, keepdims=False)[None, :, None]
        hit = lax.broadcasted_iota(jnp.int32, (rows, group, nodes), 2) == which
        found = jnp.sum(jnp.where(hit, landing, 0), axis=-1)
        return jnp.where(which[..., 0] < nodes, found, -1)

    home_rows = jnp.concatenate([rows_of(first), rows_of(last)], axis=0).T

    step = 4
    gain, load = pl.pallas_call(
        prepare_kernel,
        grid=(nodes // step,),
        in_specs=[
            pl.BlockSpec((step, block, columns), lambda i: (i, 0, 0)),
            pl.BlockSpec((step, block, block), lambda i: (i, 0, 0)),
            pl.BlockSpec((step, rows, block), lambda i: (i, 0, 0)),
        ],
        out_specs=[
            pl.BlockSpec((step, rows, block), lambda i: (i, 0, 0)),
            pl.BlockSpec((levels, step // 2, span, lanes), lambda i: (0, i, 0, 0)),
        ],
        out_shape=[
            jax.ShapeDtypeStruct((nodes, rows, block), BF16),
            jax.ShapeDtypeStruct((levels, pairs, span, lanes), BF16),
        ],
        compiler_params=params("arbitrary"),
        name="prepare",
    )(right_side[0], diag_inverse[0], below_block[0])

    operators = pl.pallas_call(
        operator_kernel,
        in_specs=[SMEM_SPEC, VMEM_SPEC, VMEM_SPEC],
        out_specs=VMEM_SPEC,
        out_shape=jax.ShapeDtypeStruct((group, rows, lanes), BF16),
        compiler_params=params(),
        name="operators",
    )(home_slot, home_rows, gain)
    operators = lax.all_gather(operators, "level", axis=0)
    loads = lax.all_to_all(load, "level", split_axis=0, concat_axis=0, tiled=True)

    def load_spec(level):
        return pl.BlockSpec((1, pairs, span, lanes), lambda i: (level, 0, 0, 0))

    message = jax.ShapeDtypeStruct((group, span, lanes), BF16)
    message_spec = pl.BlockSpec((group, span, lanes), lambda i: (0, 0, 0))
    values_shape = pltpu.VMEM((nodes + 1, span, lanes), BF16)
    arrived = [jnp.zeros((group, span, lanes), BF16)]
    for level in range(hops):
        if level == 0:
            send = pl.pallas_call(
                first_kernel,
                grid=(1,),
                in_specs=[SMEM_SPEC, load_spec(0)],
                out_specs=message_spec,
                out_shape=message,
                scratch_shapes=[values_shape],
                compiler_params=params("arbitrary"),
                name="first",
            )(take, loads)
        else:
            send = pl.pallas_call(
                functools.partial(hop_kernel, level),
                grid=(1,),
                in_specs=[
                    SMEM_SPEC,
                    SMEM_SPEC,
                    message_spec,
                    pl.BlockSpec((1, group, rows, lanes), lambda i, level=level: (level, 0, 0, 0)),
                    load_spec(level),
                ],
                out_specs=message_spec,
                out_shape=message,
                scratch_shapes=[pltpu.VMEM((nodes + 1, span, lanes), F32), values_shape],
                compiler_params=params("arbitrary"),
                name="hop",
            )(take, slot, arrived[-1], operators, loads)
        arrived.append(lax.all_to_all(send, "grp", split_axis=0, concat_axis=0, tiled=True))

    home = lax.all_to_all(jnp.stack(arrived), "level", split_axis=0, concat_axis=0, tiled=True)

    steps = group // step
    turns = nodes // step
    lead = lambda i: jnp.minimum(i, steps - 1)
    tail = lambda i: jnp.maximum(i - steps, 0)
    return pl.pallas_call(
        functools.partial(finish_kernel, steps),
        grid=(steps + turns,),
        in_specs=[
            SMEM_SPEC,
            VMEM_SPEC,
            pl.BlockSpec((levels, step, span, lanes), lambda i: (0, lead(i), 0, 0)),
            pl.BlockSpec((step, block, columns), lambda i: (tail(i), 0, 0)),
            pl.BlockSpec((step, block, block), lambda i: (tail(i), 0, 0)),
            pl.BlockSpec((step, rows, block), lambda i: (tail(i), 0, 0)),
        ],
        out_specs=[
            pl.BlockSpec((1, step, block, columns), lambda i: (0, tail(i), 0, 0)),
            pl.BlockSpec((1, step, rows, columns), lambda i: (0, tail(i), 0, 0)),
        ],
        out_shape=[
            jax.ShapeDtypeStruct((1, nodes, block, columns), BF16),
            jax.ShapeDtypeStruct((1, nodes, rows, columns), BF16),
        ],
        scratch_shapes=[pltpu.VMEM((nodes + 1, block, columns), F32)],
        compiler_params=params("arbitrary"),
        name="finish",
    )(home_slot, home_rows, home, right_side[0], diag_inverse[0], below_block[0])


def solution(mesh):
    return jax.shard_map(
        shards,
        mesh=mesh,
        in_specs=(
            P("level", "grp", None, None),
            P("level", "grp", None, None),
            P("level", "grp", None, None),
            P(),
            P(),
            P(),
        ),
        out_specs=(P("level", "grp", None, None), P("level", "grp", None, None)),
        check_vma=False,
    )
```

time: 873 us -> 237 us (0.27)
  the two profiles are of different devices: /device:TPU:10 before, /device:TPU:25 now
where the time goes in v1:
time: 237 us; the launch traced here: 233 us
  blocking collectives  83.2 us (35%)
  waiting for transfers between devices  45 us (19%)
  starting transfers between devices  29.9 us (13%)
  Pallas kernels  28.8 us (12%)
  local copies, waits for them, and re-layouts  28.3 us (12%)
  between operations  14.3 us (6%)
  other arithmetic  3.55 us (1%)
    all_to_all x3, blocking collectives, shards(): lax.all_to_all(send, 'grp', split_axis=0, concat_axis=0, tiled=True)  44.7 us
    all_to_all x1, blocking collectives, shards(): lax.all_to_all(jnp.stack(arrived), 'level', split_axis=0, concat_axis=0,...  38.5 us
    all_to_all x4, waiting for transfers between devices, shards(): lax.all_to_all(send, 'grp', split_axis=0, concat_axis=0, tiled=True)  31.4 us
    all_to_all x4, starting transfers between devices, shards(): lax.all_to_all(send, 'grp', split_axis=0, concat_axis=0, tiled=True)  24.1 us
    unnamed x47, local copies, waits for them, and re-layouts  23.9 us
    all_to_all x1, waiting for transfers between devices, shards(): lax.all_to_all(load, 'level', split_axis=0, concat_axis=0, tiled=True)  13.5 us
    pallas_call x1, Pallas kernels, shards(): pl.pallas_call(functools.partial(finish_kernel, steps), grid=(steps + tur...  11.5 us
    pallas_call x6, Pallas kernels, shards(): pl.pallas_call(functools.partial(hop_kernel, level), grid=(1,), in_specs=...  10.5 us
  transfers between devices with their start and end apart: 6, of which 5 were waited for; matrix products, arithmetic and copies ran while one was open for 5% of the time, Pallas kernels for 0%

profile of v1, /device:TPU:25, one launch (start us, length us, event | category | flops | bytes accessed | tf_op | source)
XLA Modules:
  0.0 233.0 jit_solution(5755953642649263889)
XLA Ops:
  7.2 1.0 slice_reduce_fusion
  8.7 0.8 reshape.105
  10.0 0.7 copy.62
  10.7 1.0 copy.79
  11.7 0.9 select_reduce_fusion.8.slot_ref
  12.6 1.3 select_reduce_fusion.1
  14.2 1.6 copy-done.5
  15.8 1.0 copy-done.12
  16.8 4.0 %prepare.1 = (bf16[32,64,128]{2,1,0:T(8,128)(2,1)S(1)}, bf16[8,16,32,128]{3,2,1,0:T(8,128)(2,1)S(1)}) custom-call(bf16[32,128,256]{2,1,0:T(8,128)(2,1)S(1)} %bitcast.60, bf16[32,128,128]{2,1,0:T(8,128)(2,1)S(1)} %bitcast.62, bf16[32,64,128]{2,1,0:T(8,128)(2,1)S(1)} %bitcast.64), custom_call_target="tpu_custom_call" | custom-call | tf_op jit(solution)/shard_map/prepare/pallas_call | solution.py:203
  20.8 1.0 copy-done.18
  21.8 2.0 operators.1
  23.8 5.8 %all-to-all-start = ((bf16[8,16,32,128]{3,2,1,0:T(8,128)(2,1)}), bf16[8,16,32,128]{3,2,1,0:T(8,128)(2,1)S(1)}, u32[]{:S(2)}, u32[]{:S(2)}) async-start(bf16[8,16,32,128]{3,2,1,0:T(8,128)(2,1)} %copy-done.18), calls=%async_computation | async-start | bytes 2097152 | tf_op jit(solution)/shard_map/all_to_all | solution.py:232
  30.1 13.5 %all-to-all-done.load_ref = bf16[8,16,32,128]{3,2,1,0:T(8,128)(2,1)S(1)} async-done(((bf16[8,16,32,128]{3,2,1,0:T(8,128)(2,1)}), bf16[8,16,32,128]{3,2,1,0:T(8,128)(2,1)S(1)}, u32[]{:S(2)}, u32[]{:S(2)}) %all-to-all-start) | async-done | bytes 1048608 | tf_op jit(solution)/shard_map/all_to_all | solution.py:232
  43.7 0.8 first.1
  45.2 11.1 %all-to-all-start.1 = ((bf16[32,32,128]{2,1,0:T(8,128)(2,1)}), bf16[32,32,128]{2,1,0:T(8,128)(2,1)S(1)}, u32[]{:S(2)}, u32[]{:S(2)}) async-start(bf16[32,32,128]{2,1,0:T(8,128)(2,1)} %copy-done.16), calls=%async_computation.1 | async-start | bytes 524288 | tf_op jit(solution)/shard_map/all_to_all | solution.py:270
  56.3 0.8 copy.67.slot_ref
  57.1 9.6 %all-to-all-done.1.got_ref = bf16[32,32,128]{2,1,0:T(8,128)(2,1)S(1)} async-done(((bf16[32,32,128]{2,1,0:T(8,128)(2,1)}), bf16[32,32,128]{2,1,0:T(8,128)(2,1)S(1)}, u32[]{:S(2)}, u32[]{:S(2)}) %all-to-all-start.1) | async-done | bytes 262176 | tf_op jit(solution)/shard_map/all_to_all | solution.py:270
  66.7 2.3 copy-done.1
  68.9 1.6 hop.6
  70.6 15.7 %all_to_all.45.got_ref = bf16[32,32,128]{2,1,0:T(8,128)(2,1)S(1)} all-to-all(bf16[32,32,128]{2,1,0:T(8,128)(2,1)S(1)} %hop.6), channel_id=1, replica_groups=mesh['level'=8,'grp'=32] {'grp'}, dimensions={0} | all-to-all | bytes 524288 | tf_op jit(solution)/shard_map/all_to_all | solution.py:270
  86.3 1.6 hop.7
  88.0 14.9 %all_to_all.46.got_ref = bf16[32,32,128]{2,1,0:T(8,128)(2,1)S(1)} all-to-all(bf16[32,32,128]{2,1,0:T(8,128)(2,1)S(1)} %hop.7), channel_id=1, replica_groups=mesh['level'=8,'grp'=32] {'grp'}, dimensions={0} | all-to-all | bytes 524288 | tf_op jit(solution)/shard_map/all_to_all | solution.py:270
  102.9 1.6 hop.8
  104.6 14.0 %all_to_all.47.got_ref = bf16[32,32,128]{2,1,0:T(8,128)(2,1)S(1)} all-to-all(bf16[32,32,128]{2,1,0:T(8,128)(2,1)S(1)} %hop.8), channel_id=1, replica_groups=mesh['level'=8,'grp'=32] {'grp'}, dimensions={0} | all-to-all | bytes 524288 | tf_op jit(solution)/shard_map/all_to_all | solution.py:270
  118.6 1.6 hop.9
  120.3 0.7 copy-done.17
  121.0 4.6 %all-to-all-start.5 = ((bf16[32,32,128]{2,1,0:T(8,128)(2,1)}), bf16[32,32,128]{2,1,0:T(8,128)(2,1)}, u32[]{:S(2)}, u32[]{:S(2)}) async-start(bf16[32,32,128]{2,1,0:T(8,128)(2,1)} %copy-done.17), calls=%async_computation.5 | async-start | bytes 524288 | tf_op jit(solution)/shard_map/all_to_all | solution.py:270
  125.6 0.7 broadcast_dynamic-update-slice_fusion
  126.3 9.8 %all-to-all-done.5.got_ref = bf16[32,32,128]{2,1,0:T(8,128)(2,1)} async-done(((bf16[32,32,128]{2,1,0:T(8,128)(2,1)}), bf16[32,32,128]{2,1,0:T(8,128)(2,1)}, u32[]{:S(2)}, u32[]{:S(2)}) %all-to-all-start.5) | async-done | bytes 262176 | tf_op jit(solution)/shard_map/all_to_all | solution.py:270
  136.1 2.2 copy-done.3
  138.3 1.9 hop.10
  140.3 0.7 copy-done.15
  141.0 4.6 %all-to-all-start.6 = ((bf16[32,32,128]{2,1,0:T(8,128)(2,1)}), bf16[32,32,128]{2,1,0:T(8,128)(2,1)}, u32[]{:S(2)}, u32[]{:S(2)}) async-start(bf16[32,32,128]{2,1,0:T(8,128)(2,1)} %copy-done.15), calls=%async_computation.6 | async-start | bytes 524288 | tf_op jit(solution)/shard_map/all_to_all | solution.py:270
  145.6 1.7 bitcast_dynamic-update-slice_fusion.6
  147.2 1.7 bitcast_dynamic-update-slice_fusion.5
  148.9 1.7 bitcast_dynamic-update-slice_fusion.4
  150.6 5.5 %all-to-all-done.6.got_ref = bf16[32,32,128]{2,1,0:T(8,128)(2,1)} async-done(((bf16[32,32,128]{2,1,0:T(8,128)(2,1)}), bf16[32,32,128]{2,1,0:T(8,128)(2,1)}, u32[]{:S(2)}, u32[]{:S(2)}) %all-to-all-start.6) | async-done | bytes 262176 | tf_op jit(solution)/shard_map/all_to_all | solution.py:270
  156.1 2.2 copy-done.4
  158.3 1.9 hop.11
  160.3 0.7 copy-done.14
  161.0 3.9 %all-to-all-start.7 = ((bf16[32,32,128]{2,1,0:T(8,128)(2,1)}), bf16[32,32,128]{2,1,0:T(8,128)(2,1)S(1)}, u32[]{:S(2)}, u32[]{:S(2)}) async-start(bf16[32,32,128]{2,1,0:T(8,128)(2,1)} %copy-done.14), calls=%async_computation.7 | async-start | bytes 524288 | tf_op jit(solution)/shard_map/all_to_all | solution.py:270
  164.8 0.7 bitcast_dynamic-update-slice_fusion.3
  165.6 1.7 bitcast_dynamic-update-slice_fusion.2
  167.2 1.7 bitcast_dynamic-update-slice_fusion.1
  168.9 6.5 %all-to-all-done.7 = bf16[32,32,128]{2,1,0:T(8,128)(2,1)S(1)} async-done(((bf16[32,32,128]{2,1,0:T(8,128)(2,1)}), bf16[32,32,128]{2,1,0:T(8,128)(2,1)S(1)}, u32[]{:S(2)}, u32[]{:S(2)}) %all-to-all-start.7) | async-done | bytes 262176 | tf_op jit(solution)/shard_map/all_to_all | solution.py:270
  175.4 0.7 bitcast_dynamic-update-slice_fusion
  176.1 38.5 %all_to_all.48.got_ref = bf16[8,32,32,128]{3,2,1,0:T(8,128)(2,1)S(1)} all-to-all(bf16[8,32,32,128]{3,2,1,0:T(8,128)(2,1)} %bitcast_dynamic-update-slice_fusion), channel_id=1, replica_groups=mesh['level'=8,'grp'=32] {'level'}, dimensions={0} | all-to-all | bytes 4194304 | tf_op jit(solution)/shard_map/all_to_all | solution.py:272
  214.6 11.5 %finish.1 = (bf16[1,32,128,256]{3,2,1,0:T(8,128)(2,1)}, bf16[1,32,64,256]{3,2,1,0:T(8,128)(2,1)}) custom-call(s32[64]{0:T(128)S(1)} %select_reduce_fusion.8.slot_ref, s32[32,128]{1,0:T(8,128)S(1)} %add_bitcast_fusion.rows_ref, bf16[8,32,32,128]{3,2,1,0:T(8,128)(2,1)S(1)} %all_to_all.48.got_ref, bf16[32,128,256]{2,1,0:T(8,128)(2,1)S(1)} %bitcast.61, ...), custom_call_target="tpu_custom_call" | custom-call | tf_op jit(solution)/shard_map/finish/pallas_call | solution.py:278
  (51 shorter events, 2.4 us)
Async XLA Ops:
  7.2 3.5 %copy-start = (s32[8,64,1024]{2,1,0:T(8,128)S(1)}, s32[8,64,1024]{2,1,0:T(8,128)}, u32[]{:S(2)}) copy-start(s32[8,64,1024]{2,1,0:T(8,128)} %param.11) | copy-start | bytes 6291460
  7.2 7.0 %copy-start.7 = (bf16[1,32,128,128]{3,2,1,0:T(8,128)(2,1)S(1)}, bf16[1,32,128,128]{3,2,1,0:T(8,128)(2,1)}, u32[]{:S(2)}) copy-start(bf16[1,32,128,128]{3,2,1,0:T(8,128)(2,1)} %param.7) | copy-start | bytes 3145732
  7.2 59.5 %all-gather.3.cloned.1.call-start = ((), (), s32[]{:S(2)}) async-start(), calls=%async_computation.9 | async-start | bytes 4718592 | tf_op jit(solution)/shard_map/all_gather | solution.py:231
  14.2 1.6 copy-start.5
  15.8 1.0 copy-start.12
  20.8 1.0 copy-start.18
  23.8 19.9 %all-to-all-start = ((bf16[8,16,32,128]{3,2,1,0:T(8,128)(2,1)}), bf16[8,16,32,128]{3,2,1,0:T(8,128)(2,1)S(1)}, u32[]{:S(2)}, u32[]{:S(2)}) async-start(bf16[8,16,32,128]{3,2,1,0:T(8,128)(2,1)} %copy-done.18), calls=%async_computation | async-start | bytes 2097152 | tf_op jit(solution)/shard_map/all_to_all | solution.py:232
  44.5 0.7 copy-start.16
  45.2 21.5 %all-to-all-start.1 = ((bf16[32,32,128]{2,1,0:T(8,128)(2,1)}), bf16[32,32,128]{2,1,0:T(8,128)(2,1)S(1)}, u32[]{:S(2)}, u32[]{:S(2)}) async-start(bf16[32,32,128]{2,1,0:T(8,128)(2,1)} %copy-done.16), calls=%async_computation.1 | async-start | bytes 524288 | tf_op jit(solution)/shard_map/all_to_all | solution.py:270
  66.7 3.9 %copy-start.9 = (bf16[32,32,128]{2,1,0:T(8,128)(2,1)}, bf16[32,32,128]{2,1,0:T(8,128)(2,1)S(1)}, u32[]{:S(2)}) copy-start(bf16[32,32,128]{2,1,0:T(8,128)(2,1)S(1)} %all-to-all-done.1.got_ref) | copy-start | bytes 786436
  66.7 2.3 copy-start.1
  68.9 17.4 %copy-start.2 = (bf16[256,64,128]{2,1,0:T(8,128)(2,1)S(1)}, bf16[256,64,128]{2,1,0:T(8,128)(2,1)}, u32[]{:S(2)}) copy-start(bf16[256,64,128]{2,1,0:T(8,128)(2,1)} %all-gather.3.cloned.1.call-done) | copy-start | bytes 12582916
  86.3 1.6 copy-start.10
  102.9 1.7 copy-start.11
  120.3 0.7 copy-start.17
  121.0 15.1 %all-to-all-start.5 = ((bf16[32,32,128]{2,1,0:T(8,128)(2,1)}), bf16[32,32,128]{2,1,0:T(8,128)(2,1)}, u32[]{:S(2)}, u32[]{:S(2)}) async-start(bf16[32,32,128]{2,1,0:T(8,128)(2,1)} %copy-done.17), calls=%async_computation.5 | async-start | bytes 524288 | tf_op jit(solution)/shard_map/all_to_all | solution.py:270
  136.1 2.2 copy-start.3
  140.2 0.7 copy-start.15
  141.0 15.1 %all-to-all-start.6 = ((bf16[32,32,128]{2,1,0:T(8,128)(2,1)}), bf16[32,32,128]{2,1,0:T(8,128)(2,1)}, u32[]{:S(2)}, u32[]{:S(2)}) async-start(bf16[32,32,128]{2,1,0:T(8,128)(2,1)} %copy-done.15), calls=%async_computation.6 | async-start | bytes 524288 | tf_op jit(solution)/shard_map/all_to_all | solution.py:270
  156.1 2.2 copy-start.4
  160.3 0.7 copy-start.14
  161.0 14.5 %all-to-all-start.7 = ((bf16[32,32,128]{2,1,0:T(8,128)(2,1)}), bf16[32,32,128]{2,1,0:T(8,128)(2,1)S(1)}, u32[]{:S(2)}, u32[]{:S(2)}) async-start(bf16[32,32,128]{2,1,0:T(8,128)(2,1)} %copy-done.14), calls=%async_computation.7 | async-start | bytes 524288 | tf_op jit(solution)/shard_map/all_to_all | solution.py:270
  176.1 38.5 %copy-start.6 = (bf16[1,32,128,256]{3,2,1,0:T(8,128)(2,1)S(1)}, bf16[1,32,128,256]{3,2,1,0:T(8,128)(2,1)}, u32[]{:S(2)}) copy-start(bf16[1,32,128,256]{3,2,1,0:T(8,128)(2,1)} %param.6) | copy-start | bytes 6291460
  176.1 38.5 %copy-start.8 = (bf16[1,32,128,128]{3,2,1,0:T(8,128)(2,1)S(1)}, bf16[1,32,128,128]{3,2,1,0:T(8,128)(2,1)}, u32[]{:S(2)}) copy-start(bf16[1,32,128,128]{3,2,1,0:T(8,128)(2,1)} %param.7) | copy-start | bytes 3145732
  176.1 38.5 %copy-start.13 = (bf16[1,32,64,128]{3,2,1,0:T(8,128)(2,1)S(1)}, bf16[1,32,64,128]{3,2,1,0:T(8,128)(2,1)}, u32[]{:S(2)}) copy-start(bf16[1,32,64,128]{3,2,1,0:T(8,128)(2,1)} %param.8) | copy-start | bytes 1572868
Sparse Core Ops, SparseCore 0:
  23.9 38.0 all-gather.2

commit v2 on v1

v2 whole, which is shorter than its diff:
```python
import functools

import jax
import jax.numpy as jnp
from jax import lax
from jax.experimental import pallas as pl
from jax.experimental.pallas import tpu as pltpu
from jax.sharding import PartitionSpec as P

F32 = jnp.float32
BF16 = jnp.bfloat16


def dot(a, b):
    return jnp.dot(a, b, preferred_element_type=F32)


def dot_nt(a, b):
    return lax.dot_general(a, b, (((1,), (1,)), ((), ())), preferred_element_type=F32)


def low_lanes(shape, half):
    return lax.broadcasted_iota(jnp.int32, shape, len(shape) - 1) < half


def prepare_kernel(rhs_ref, inv_ref, below_ref, gain_ref, load_ref):
    nodes = rhs_ref.shape[0]
    levels, _, span, _ = load_ref.shape
    for pair in range(nodes // 2):
        halves = []
        for node in (2 * pair, 2 * pair + 1):
            inv, below = inv_ref[node], below_ref[node]
            gain_ref[node] = dot(below, inv).astype(BF16)
            solved = dot(inv, rhs_ref[node]).astype(BF16)
            halves.append(dot(below, solved))
        both = jnp.concatenate(halves, axis=0).T.astype(BF16)
        load_ref[:, pair] = both.reshape(levels, span, both.shape[1])


def operator_kernel(slot_ref, rows_ref, gain_ref, op_ref):
    senders, rows, lanes = op_ref.shape
    nodes, _, block = gain_ref.shape
    low = low_lanes((rows, lanes), rows)
    for s in range(senders):
        hot = (
            lax.broadcasted_iota(jnp.int32, (block, lanes), 0) == rows_ref[s : s + 1, :]
        ).astype(BF16)
        first = dot(gain_ref[jnp.minimum(slot_ref[2 * s], nodes - 1)], hot)
        second = dot(gain_ref[jnp.minimum(slot_ref[2 * s + 1], nodes - 1)], hot)
        op_ref[s] = jnp.where(low, first, second).astype(BF16)


def pack(values, take_ref, level, send_ref):
    senders, span, lanes = send_ref.shape
    low = low_lanes((span, lanes), lanes // 2)
    for d in range(senders):
        first = values[take_ref[level, 2 * d]]
        second = values[take_ref[level, 2 * d + 1]]
        send_ref[d] = jnp.where(low, first, second)


def both_halves(pair_value, odd, low, half):
    turned = pltpu.roll(pair_value, half, 1)
    return jnp.where(low, turned, pair_value) if odd else jnp.where(low, pair_value, turned)


def first_kernel(take_ref, load_ref, send_ref, values):
    _, pairs, span, lanes = load_ref.shape
    low = low_lanes((span, lanes), lanes // 2)
    for pair in range(pairs):
        value = load_ref[0, pair].astype(F32)
        for odd in (0, 1):
            values[2 * pair + odd] = both_halves(value, odd, low, lanes // 2).astype(BF16)
    values[2 * pairs] = jnp.zeros((span, lanes), BF16)
    pack(values, take_ref, 0, send_ref)


def hop_kernel(
    level,
    take_ref,
    slot_ref,
    got_ref,
    op_ref,
    load_ref,
    send_ref,
    got,
    ops,
    load,
    total,
    values,
    ready,
):
    senders, span, lanes = got.shape
    pairs = load.shape[0]
    half = lanes // 2
    parts = ready.shape[1]
    share = senders // parts
    copies = []
    for i in range(parts):
        where = pl.ds(i * share, share)
        copies.append(
            (
                pltpu.make_async_copy(got_ref.at[where], got.at[where], ready.at[0, i]),
                pltpu.make_async_copy(op_ref.at[level, where], ops.at[where], ready.at[1, i]),
            )
        )
    loading = pltpu.make_async_copy(load_ref.at[level], load, ready.at[2, 0])
    for pair in copies:
        for copy in pair:
            copy.start()
    loading.start()
    low = low_lanes((span, lanes), half)
    low_op = low_lanes((half, lanes), half)
    total[...] = jnp.zeros_like(total)
    for s in range(senders):
        if s % share == 0:
            for copy in copies[s // share]:
                copy.wait()
        op = ops[s]
        zero = jnp.zeros_like(op)
        split = jnp.concatenate(
            [jnp.where(low_op, op, zero), jnp.where(low_op, zero, op)], axis=0
        )
        part = dot_nt(got[s], split)
        one = slot_ref[level - 1, 2 * s]
        two = slot_ref[level - 1, 2 * s + 1]
        total[one] += jnp.where(low, part, 0.0)
        total[two] += jnp.where(low, 0.0, part)
    loading.wait()
    for pair in range(pairs):
        value = load[pair].astype(F32)
        for odd in (0, 1):
            node = 2 * pair + odd
            come = total[node]
            come = come + pltpu.roll(come, half, 1)
            values[node] = (both_halves(value, odd, low, half) - come).astype(BF16)
    values[2 * pairs] = jnp.zeros((span, lanes), BF16)
    pack(values, take_ref, level, send_ref)


def finish_kernel(
    early_counts,
    level_ref,
    slot_ref,
    rows_ref,
    rhs_ref,
    inv_ref,
    below_ref,
    *rest,
):
    chunks, parts = rest[-1].shape
    groups = len(early_counts)
    early = rest[:groups]
    sol_ref, out_ref, got, rhs, inv, below, inflow, base_ready, ready = rest[-9:]
    late = rest[groups:-9]
    late = [late[i : i + chunks] for i in range(0, len(late), chunks)]
    level = level_ref[0]
    step = pl.program_id(0)
    _, senders, span, lanes = got.shape
    _, nodes, block, _ = sol_ref.shape
    half = lanes // 2
    share = senders // parts
    spots = [pl.ds(p * share, share) for p in range(parts)]
    base = [
        pltpu.make_async_copy(source, target, base_ready.at[i])
        for i, (source, target) in enumerate(((rhs_ref, rhs), (inv_ref, inv), (below_ref, below)))
    ]

    @pl.when(step == 0)
    def _():
        def fetch(source):
            for p, spot in enumerate(spots):
                for c in range(chunks):
                    pltpu.make_async_copy(
                        source(c).at[spot], got.at[c, spot], ready.at[c, p]
                    ).start()

        reach = 1
        for index, (array, count) in enumerate(zip(early, early_counts)):
            inside = level < reach + count
            if index > 0:
                inside = jnp.logical_and(inside, level >= reach)

            @pl.when(inside)
            def _(array=array, reach=reach):
                fetch(lambda c: array.at[c, jnp.maximum(level - reach, 0)])

            reach += count
        for arrays in late:

            @pl.when(level == reach)
            def _(arrays=arrays):
                fetch(lambda c: arrays[c])

            reach += 1
        for copy in base:
            copy.start()

        inflow[...] = jnp.zeros_like(inflow)
        low = low_lanes((block, lanes), half)
        for s in range(senders):
            if s % share == 0:
                p = s // share
                for c in range(chunks):
                    pltpu.make_async_copy(
                        got.at[c, spots[p]], got.at[c, spots[p]], ready.at[c, p]
                    ).wait()
            hot = lax.broadcasted_iota(jnp.int32, (block, lanes), 0) == rows_ref[s : s + 1, :]
            hot = jnp.concatenate(
                [jnp.logical_and(hot, low), jnp.logical_and(hot, jnp.logical_not(low))], axis=0
            )
            part = dot(hot.astype(BF16), got[:, s].reshape(chunks * span, lanes).T)
            inflow[slot_ref[2 * s]] += part[:block]
            inflow[slot_ref[2 * s + 1]] += part[block:]
        for copy in base:
            copy.wait()

    @pl.when(step > 0)
    def _():
        at = (step - 1) * nodes
        reduced = [
            (rhs[at + n].astype(F32) - inflow[at + n]).astype(BF16) for n in range(nodes)
        ]
        solved = [dot(inv[at + n], reduced[n]).astype(BF16) for n in range(nodes)]
        for n in range(nodes):
            sol_ref[0, n] = solved[n]
        for n in range(nodes):
            out_ref[0, n] = dot(below[at + n], solved[n]).astype(BF16)


def params(limit, *semantics):
    return pltpu.CompilerParams(
        vmem_limit_bytes=limit * 1024 * 1024, dimension_semantics=semantics or None
    )


SMEM_SPEC = pl.BlockSpec(memory_space=pltpu.SMEM)
VMEM_SPEC = pl.BlockSpec(memory_space=pltpu.VMEM)
HBM_SPEC = pl.BlockSpec(memory_space=pltpu.HBM)


def shards(right_side, diag_inverse, below_block, parent_device, parent_slot, row_index):
    levels = lax.axis_size("level")
    group = lax.axis_size("grp")
    level_id = lax.axis_index("level")
    member = lax.axis_index("grp")
    _, nodes, block, columns = right_side.shape
    rows = below_block.shape[2]
    span = columns // levels
    lanes = 2 * rows
    pairs = nodes // 2
    hops = levels - 1

    step = 4
    gain, load = pl.pallas_call(
        prepare_kernel,
        grid=(nodes // step,),
        in_specs=[
            pl.BlockSpec((step, block, columns), lambda i: (i, 0, 0)),
            pl.BlockSpec((step, block, block), lambda i: (i, 0, 0)),
            pl.BlockSpec((step, rows, block), lambda i: (i, 0, 0)),
        ],
        out_specs=[
            pl.BlockSpec((step, rows, block), lambda i: (i, 0, 0)),
            pl.BlockSpec((levels, step // 2, span, lanes), lambda i: (0, i, 0, 0)),
        ],
        out_shape=[
            jax.ShapeDtypeStruct((nodes, rows, block), BF16),
            jax.ShapeDtypeStruct((levels, pairs, span, lanes), BF16),
        ],
        compiler_params=params(60, "arbitrary"),
        name="prepare",
    )(right_side[0], diag_inverse[0], below_block[0])

    devices = parent_device[:hops, :, 0].reshape(hops, group, nodes)
    slots = parent_slot[:hops].reshape(hops, group, nodes)
    place = lax.broadcasted_iota(jnp.int32, (hops, group, nodes), 2)

    def ends(named):
        first = jnp.min(jnp.where(named, place, nodes), axis=-1)
        last = jnp.max(jnp.where(named, place, -1), axis=-1)
        return first, jnp.where(last > first, last, nodes)

    first, last = ends(devices == member)
    own = lax.dynamic_index_in_dim(devices, member, 1, keepdims=True)
    take = jnp.stack(ends(own == lax.broadcasted_iota(jnp.int32, (hops, group, nodes), 1)), -1)
    take = take.reshape(hops, 2 * group)

    def slot_of(which):
        hit = place == which[..., None]
        found = jnp.sum(jnp.where(hit, slots, 0), axis=-1)
        return jnp.where(which < nodes, found, nodes)

    slot = jnp.stack([slot_of(first), slot_of(last)], -1).reshape(hops, 2 * group)

    before = jnp.maximum(level_id - 1, 0)
    home_slot = lax.dynamic_index_in_dim(slot, before, 0, keepdims=False)
    home_slot = jnp.where(level_id > 0, home_slot, nodes)
    landing = lax.dynamic_index_in_dim(row_index, before, 0, keepdims=False)
    landing = landing.reshape(rows, group, nodes)

    def rows_of(which):
        which = lax.dynamic_index_in_dim(which, before, 0, keepdims=False)[None, :, None]
        hit = lax.broadcasted_iota(jnp.int32, (rows, group, nodes), 2) == which
        found = jnp.sum(jnp.where(hit, landing, 0), axis=-1)
        return jnp.where(which[..., 0] < nodes, found, -1)

    home_rows = jnp.concatenate([rows_of(first), rows_of(last)], axis=0).T

    operators = pl.pallas_call(
        operator_kernel,
        in_specs=[SMEM_SPEC, VMEM_SPEC, VMEM_SPEC],
        out_specs=VMEM_SPEC,
        out_shape=jax.ShapeDtypeStruct((group, rows, lanes), BF16),
        compiler_params=params(16),
        name="operators",
    )(home_slot, home_rows, gain)
    operators = lax.all_gather(operators, "level", axis=0)
    loads = lax.all_to_all(load, "level", split_axis=0, concat_axis=0, tiled=True)

    message = jax.ShapeDtypeStruct((group, span, lanes), BF16)
    values_shape = pltpu.VMEM((nodes + 1, span, lanes), BF16)
    arrived = [None]
    early_counts = (hops // 2, hops - 2 - hops // 2)
    early = []
    for level in range(hops):
        if level == 0:
            send = pl.pallas_call(
                first_kernel,
                in_specs=[SMEM_SPEC, VMEM_SPEC],
                out_specs=VMEM_SPEC,
                out_shape=message,
                scratch_shapes=[values_shape],
                compiler_params=params(16),
                name="first",
            )(take, loads)
        else:
            send = pl.pallas_call(
                functools.partial(hop_kernel, level),
                in_specs=[SMEM_SPEC, SMEM_SPEC, HBM_SPEC, HBM_SPEC, HBM_SPEC],
                out_specs=VMEM_SPEC,
                out_shape=message,
                scratch_shapes=[
                    pltpu.VMEM((group, span, lanes), BF16),
                    pltpu.VMEM((group, rows, lanes), BF16),
                    pltpu.VMEM((pairs, span, lanes), BF16),
                    pltpu.VMEM((nodes + 1, span, lanes), F32),
                    values_shape,
                    pltpu.SemaphoreType.DMA((3, 4)),
                ],
                compiler_params=params(53),
                name="hop",
            )(take, slot, arrived[-1], operators, loads)
        arrived.append(lax.all_to_all(send, "grp", split_axis=0, concat_axis=0, tiled=True))
        if len(arrived) == 1 + sum(early_counts[: len(early) + 1]) and len(early) < 2:
            ready = jnp.stack(arrived[1 + sum(early_counts[: len(early)]) :])
            early.append(lax.all_gather(ready, "level", axis=0))
        elif len(arrived) == hops:
            arrived[-1], early[0] = lax.optimization_barrier((arrived[-1], early[0]))

    late = []
    for level in range(1 + sum(early_counts), levels):
        late += [
            arrived[level]
            if c == level
            else lax.ppermute(arrived[level], "level", [(c, level)])
            for c in range(levels)
        ]

    step = 8
    parts = 4
    tail = lambda i: jnp.maximum(i - 1, 0)
    return pl.pallas_call(
        functools.partial(finish_kernel, early_counts),
        grid=(1 + nodes // step,),
        in_specs=[SMEM_SPEC, SMEM_SPEC, VMEM_SPEC]
        + [HBM_SPEC] * (3 + len(early) + len(late)),
        out_specs=[
            pl.BlockSpec((1, step, block, columns), lambda i: (0, tail(i), 0, 0)),
            pl.BlockSpec((1, step, rows, columns), lambda i: (0, tail(i), 0, 0)),
        ],
        out_shape=[
            jax.ShapeDtypeStruct((1, nodes, block, columns), BF16),
            jax.ShapeDtypeStruct((1, nodes, rows, columns), BF16),
        ],
        scratch_shapes=[
            pltpu.VMEM((levels, group, span, lanes), BF16),
            pltpu.VMEM((nodes, block, columns), BF16),
            pltpu.VMEM((nodes, block, block), BF16),
            pltpu.VMEM((nodes, rows, block), BF16),
            pltpu.VMEM((nodes + 1, block, columns), F32),
            pltpu.SemaphoreType.DMA((3,)),
            pltpu.SemaphoreType.DMA((levels, parts)),
        ],
        compiler_params=params(50, "arbitrary"),
        name="finish",
    )(
        level_id.reshape(1),
        home_slot,
        home_rows,
        right_side[0],
        diag_inverse[0],
        below_block[0],
        *early,
        *late,
    )


def solution(mesh):
    return jax.shard_map(
        shards,
        mesh=mesh,
        in_specs=(
            P("level", "grp", None, None),
            P("level", "grp", None, None),
            P("level", "grp", None, None),
            P(),
            P(),
            P(),
        ),
        out_specs=(P("level", "grp", None, None), P("level", "grp", None, None)),
        check_vma=False,
    )
```

time: 237 us -> 226 us (0.954); the launches traced: 233 us -> 225 us
  local copies, waits for them, and re-layouts: 28.3 us -> 7.52 us
  starting transfers between devices: 29.9 us -> 45.6 us
  blocking collectives: 83.2 us -> 73 us
  Pallas kernels: 28.8 us -> 37.1 us
    all_to_all x1 -> x0, blocking collectives: 38.5 us -> none  [shards(): lax.all_to_all(jnp.stack(arrived), 'level', split_axis=0, concat_axis=0,...]
    all_to_all x3 -> x5, blocking collectives: 44.7 us -> 73 us  [shards(): lax.all_to_all(send, 'grp', split_axis=0, concat_axis=0, tiled=True)]
    ppermute x0 -> x14, starting transfers between devices: none -> 24 us  [shards(): lax.ppermute(arrived[level], 'level', [(c, level)])]
    all_to_all x4 -> x2, waiting for transfers between devices: 31.4 us -> 10.3 us  [shards(): lax.all_to_all(send, 'grp', split_axis=0, concat_axis=0, tiled=True)]
    ppermute x0 -> x14, waiting for transfers between devices: none -> 20.2 us  [shards(): lax.ppermute(arrived[level], 'level', [(c, level)])]
    unnamed x47 -> x18, local copies, waits for them, and re-layouts: 23.9 us -> 5.25 us
    all_to_all x4 -> x2, starting transfers between devices: 24.1 us -> 15.7 us  [shards(): lax.all_to_all(send, 'grp', split_axis=0, concat_axis=0, tiled=True)]
    pallas_call x8, Pallas kernels: 22.8 us -> 27.6 us  [the longest x6 19.7 us: shards(): pl.pallas_call(functools.partial(hop_kernel, level), in_specs=[SMEM_SPEC,...]
  transfers between devices with their start and end apart: 6 -> 20, of which waited for: 5 -> 7; matrix products, arithmetic and copies ran while one was open for 5% -> 1% of each run, Pallas kernels for 0% -> 6%
where the time goes in v2:
time: 226 us; the launch traced here: 225 us
  blocking collectives  73 us (32%)
  starting transfers between devices  45.6 us (20%)
  waiting for transfers between devices  44.1 us (20%)
  Pallas kernels  37.1 us (16%)
  between operations  14.1 us (6%)
  local copies, waits for them, and re-layouts  7.52 us (3%)
  other arithmetic  3.56 us (2%)
    all_to_all x5, blocking collectives, shards(): lax.all_to_all(send, 'grp', split_axis=0, concat_axis=0, tiled=True)  73 us
    ppermute x14, starting transfers between devices, shards(): lax.ppermute(arrived[level], 'level', [(c, level)])  24 us
    ppermute x14, waiting for transfers between devices, shards(): lax.ppermute(arrived[level], 'level', [(c, level)])  20.2 us
    pallas_call x6, Pallas kernels, shards(): pl.pallas_call(functools.partial(hop_kernel, level), in_specs=[SMEM_SPEC,...  19.7 us
    all_to_all x2, starting transfers between devices, shards(): lax.all_to_all(send, 'grp', split_axis=0, concat_axis=0, tiled=True)  15.7 us
    all_to_all x1, waiting for transfers between devices, shards(): lax.all_to_all(load, 'level', split_axis=0, concat_axis=0, tiled=True)  13.5 us
    all_to_all x2, waiting for transfers between devices, shards(): lax.all_to_all(send, 'grp', split_axis=0, concat_axis=0, tiled=True)  10.3 us
    pallas_call x1, Pallas kernels, shards(): pl.pallas_call(prepare_kernel, grid=(nodes // step,), in_specs=[pl.BlockS...  7.55 us
  transfers between devices with their start and end apart: 20, of which 7 were waited for; matrix products, arithmetic and copies ran while one was open for 1% of the time, Pallas kernels for 6%

profile of v2, /device:TPU:25, one launch (start us, length us, event | category | flops | bytes accessed | tf_op | source)
XLA Modules:
  0.0 225.0 jit_solution(8655850134924580740)
XLA Ops:
  7.2 0.9 slice_reduce_fusion
  8.6 0.8 reshape.109
  11.0 7.5 %prepare.1 = (bf16[32,64,128]{2,1,0:T(8,128)(2,1)}, bf16[8,16,32,128]{3,2,1,0:T(8,128)(2,1)}) custom-call(bf16[32,128,256]{2,1,0:T(8,128)(2,1)} %bitcast.59, bf16[32,128,128]{2,1,0:T(8,128)(2,1)} %bitcast.63, bf16[32,64,128]{2,1,0:T(8,128)(2,1)} %bitcast.65), custom_call_target="tpu_custom_call" | custom-call | tf_op jit(solution)/shard_map/prepare/pallas_call | solution.py:255
  18.5 1.0 copy-done.3
  19.6 2.0 operators.1
  21.6 5.8 %all-to-all-start = ((bf16[8,16,32,128]{3,2,1,0:T(8,128)(2,1)}), bf16[8,16,32,128]{3,2,1,0:T(8,128)(2,1)S(1)}, u32[]{:S(2)}, u32[]{:S(2)}) async-start(bf16[8,16,32,128]{3,2,1,0:T(8,128)(2,1)} %get-tuple-element.6), calls=%async_computation | async-start | bytes 2097152 | tf_op jit(solution)/shard_map/all_to_all | solution.py:319
  27.9 13.5 %all-to-all-done.load_ref = bf16[8,16,32,128]{3,2,1,0:T(8,128)(2,1)S(1)} async-done(((bf16[8,16,32,128]{3,2,1,0:T(8,128)(2,1)}), bf16[8,16,32,128]{3,2,1,0:T(8,128)(2,1)S(1)}, u32[]{:S(2)}, u32[]{:S(2)}) %all-to-all-start) | async-done | bytes 1048608 | tf_op jit(solution)/shard_map/all_to_all | solution.py:319
  41.5 0.8 first.1
  42.3 0.7 copy-done.2
  43.0 11.1 %all-to-all-start.1 = ((bf16[32,32,128]{2,1,0:T(8,128)(2,1)}), bf16[32,32,128]{2,1,0:T(8,128)(2,1)S(1)}, u32[]{:S(2)}, u32[]{:S(2)}) async-start(bf16[32,32,128]{2,1,0:T(8,128)(2,1)} %copy-done.2), calls=%async_computation.1 | async-start | bytes 524288 | tf_op jit(solution)/shard_map/all_to_all | solution.py:354
  54.2 10.3 %all-to-all-done.1.got_ref = bf16[32,32,128]{2,1,0:T(8,128)(2,1)S(1)} async-done(((bf16[32,32,128]{2,1,0:T(8,128)(2,1)}), bf16[32,32,128]{2,1,0:T(8,128)(2,1)S(1)}, u32[]{:S(2)}, u32[]{:S(2)}) %all-to-all-start.1) | async-done | bytes 262176 | tf_op jit(solution)/shard_map/all_to_all | solution.py:354
  64.5 3.2 %hop.6 = bf16[32,32,128]{2,1,0:T(8,128)(2,1)S(1)} custom-call(s32[7,64]{1,0:T(8,128)S(1)} %copy.74.take_ref, s32[7,64]{1,0:T(8,128)S(1)} %copy.75.slot_ref, bf16[32,32,128]{2,1,0:T(8,128)(2,1)S(1)} %all-to-all-done.1.got_ref, bf16[8,32,64,128]{3,2,1,0:T(8,128)(2,1)} %bitcast.53, bf16[8,16,32,128]{3,2,1,0:T(8,128)(2,1)} %copy-done.1), custom_call_target="tpu_custom_call" | custom-call | tf_op jit(solution)/shard_map/hop/pallas_call | solution.py:338
  67.6 15.8 %all_to_all.40.got_ref = bf16[32,32,128]{2,1,0:T(8,128)(2,1)S(1)} all-to-all(bf16[32,32,128]{2,1,0:T(8,128)(2,1)S(1)} %hop.6), channel_id=1, replica_groups=mesh['level'=8,'grp'=32] {'grp'}, dimensions={0} | all-to-all | bytes 524288 | tf_op jit(solution)/shard_map/all_to_all | solution.py:354
  83.4 3.2 %hop.7 = bf16[32,32,128]{2,1,0:T(8,128)(2,1)S(1)} custom-call(s32[7,64]{1,0:T(8,128)S(1)} %copy.74.take_ref, s32[7,64]{1,0:T(8,128)S(1)} %copy.75.slot_ref, bf16[32,32,128]{2,1,0:T(8,128)(2,1)S(1)} %all_to_all.40.got_ref, bf16[8,32,64,128]{3,2,1,0:T(8,128)(2,1)} %bitcast.54, bf16[8,16,32,128]{3,2,1,0:T(8,128)(2,1)} %copy-done.1), custom_call_target="tpu_custom_call" | custom-call | tf_op jit(solution)/shard_map/hop/pallas_call | solution.py:338
  86.6 15.1 %all_to_all.41.got_ref = bf16[32,32,128]{2,1,0:T(8,128)(2,1)S(1)} all-to-all(bf16[32,32,128]{2,1,0:T(8,128)(2,1)S(1)} %hop.7), channel_id=1, replica_groups=mesh['level'=8,'grp'=32] {'grp'}, dimensions={0} | all-to-all | bytes 524288 | tf_op jit(solution)/shard_map/all_to_all | solution.py:354
  101.7 1.0 pad_maximum_fusion
  102.8 3.2 %hop.8 = bf16[32,32,128]{2,1,0:T(8,128)(2,1)S(1)} custom-call(s32[7,64]{1,0:T(8,128)S(1)} %copy.74.take_ref, s32[7,64]{1,0:T(8,128)S(1)} %copy.75.slot_ref, bf16[32,32,128]{2,1,0:T(8,128)(2,1)S(1)} %all_to_all.41.got_ref, bf16[8,32,64,128]{3,2,1,0:T(8,128)(2,1)} %bitcast.55, bf16[8,16,32,128]{3,2,1,0:T(8,128)(2,1)} %copy-done.1), custom_call_target="tpu_custom_call" | custom-call | tf_op jit(solution)/shard_map/hop/pallas_call | solution.py:338
  105.9 14.0 %all_to_all.42.got_ref = bf16[32,32,128]{2,1,0:T(8,128)(2,1)S(1)} all-to-all(bf16[32,32,128]{2,1,0:T(8,128)(2,1)S(1)} %hop.8), channel_id=1, replica_groups=mesh['level'=8,'grp'=32] {'grp'}, dimensions={0} | all-to-all | bytes 524288 | tf_op jit(solution)/shard_map/all_to_all | solution.py:354
  120.0 3.2 %hop.9 = bf16[32,32,128]{2,1,0:T(8,128)(2,1)S(1)} custom-call(s32[7,64]{1,0:T(8,128)S(1)} %copy.74.take_ref, s32[7,64]{1,0:T(8,128)S(1)} %copy.75.slot_ref, bf16[32,32,128]{2,1,0:T(8,128)(2,1)S(1)} %all_to_all.42.got_ref, bf16[8,32,64,128]{3,2,1,0:T(8,128)(2,1)} %bitcast.56, bf16[8,16,32,128]{3,2,1,0:T(8,128)(2,1)} %copy-done.1), custom_call_target="tpu_custom_call" | custom-call | tf_op jit(solution)/shard_map/hop/pallas_call | solution.py:338
  123.1 14.1 %all_to_all.43.got_ref = bf16[32,32,128]{2,1,0:T(8,128)(2,1)S(1)} all-to-all(bf16[32,32,128]{2,1,0:T(8,128)(2,1)S(1)} %hop.9), channel_id=1, replica_groups=mesh['level'=8,'grp'=32] {'grp'}, dimensions={0} | all-to-all | bytes 524288 | tf_op jit(solution)/shard_map/all_to_all | solution.py:354
  137.2 0.8 pad_maximum_fusion.1
  138.1 3.2 %hop.10 = bf16[32,32,128]{2,1,0:T(8,128)(2,1)S(1)} custom-call(s32[7,64]{1,0:T(8,128)S(1)} %copy.74.take_ref, s32[7,64]{1,0:T(8,128)S(1)} %copy.75.slot_ref, bf16[32,32,128]{2,1,0:T(8,128)(2,1)S(1)} %all_to_all.43.got_ref, bf16[8,32,64,128]{3,2,1,0:T(8,128)(2,1)} %bitcast.57, bf16[8,16,32,128]{3,2,1,0:T(8,128)(2,1)} %copy-done.1), custom_call_target="tpu_custom_call" | custom-call | tf_op jit(solution)/shard_map/hop/pallas_call | solution.py:338
  141.3 14.0 %all_to_all.44.got_ref.rest_8_ = bf16[32,32,128]{2,1,0:T(8,128)(2,1)S(1)} all-to-all(bf16[32,32,128]{2,1,0:T(8,128)(2,1)S(1)} %hop.10), channel_id=1, replica_groups=mesh['level'=8,'grp'=32] {'grp'}, dimensions={0} | all-to-all | bytes 524288 | tf_op jit(solution)/shard_map/all_to_all | solution.py:354
  155.2 3.9 %hop.11 = bf16[32,32,128]{2,1,0:T(8,128)(2,1)} custom-call(s32[7,64]{1,0:T(8,128)S(1)} %copy.74.take_ref, s32[7,64]{1,0:T(8,128)S(1)} %copy.75.slot_ref, bf16[32,32,128]{2,1,0:T(8,128)(2,1)S(1)} %all_to_all.44.got_ref.rest_8_, bf16[8,32,64,128]{3,2,1,0:T(8,128)(2,1)} %bitcast.58, bf16[8,16,32,128]{3,2,1,0:T(8,128)(2,1)} %copy-done.1), custom_call_target="tpu_custom_call" | custom-call | tf_op jit(solution)/shard_map/hop/pallas_call | solution.py:338
  159.1 4.6 %all-to-all-start.7 = ((bf16[32,32,128]{2,1,0:T(8,128)(2,1)}), bf16[32,32,128]{2,1,0:T(8,128)(2,1)}, u32[]{:S(2)}, u32[]{:S(2)}) async-start(bf16[32,32,128]{2,1,0:T(8,128)(2,1)} %hop.11), calls=%async_computation.7 | async-start | bytes 524288 | tf_op jit(solution)/shard_map/all_to_all | solution.py:354
  163.7 8.9 %collective-permute-start.6 = (bf16[32,32,128]{2,1,0:T(8,128)(2,1)S(1)}, bf16[32,32,128]{2,1,0:T(8,128)(2,1)S(1)}, u32[]{:S(2)}, u32[]{:S(2)}) collective-permute-start(bf16[32,32,128]{2,1,0:T(8,128)(2,1)S(1)} %all_to_all.44.got_ref.rest_8_), channel_id=1, source_target_pairs={{224,192},{225,193},{226,194},{227,195},{228,196},{229,197},{230,1... | collective-permute-start | bytes 786440 | tf_op jit(solution)/shard_map/ppermute | solution.py:366
  172.6 0.7 collective-permute-start.5
  173.3 0.7 collective-permute-start.4
  174.0 0.7 collective-permute-start.3
  174.7 1.4 collective-permute-start.2
  176.0 1.4 collective-permute-start.1
  177.4 1.4 collective-permute-start
  178.8 1.3 collective-permute-start.13
  180.1 1.3 collective-permute-start.12
  181.4 1.3 collective-permute-start.11
  182.7 1.3 collective-permute-start.10
  184.0 1.3 collective-permute-start.9
  185.3 1.8 collective-permute-done.13.rest_16_
  187.1 0.7 copy-done.4
  187.8 1.3 collective-permute-start.8
  189.1 3.1 %collective-permute-done.12.rest_15_ = bf16[32,32,128]{2,1,0:T(8,128)(2,1)S(1)} collective-permute-done((bf16[32,32,128]{2,1,0:T(8,128)(2,1)}, bf16[32,32,128]{2,1,0:T(8,128)(2,1)S(1)}, u32[]{:S(2)}, u32[]{:S(2)}) %collective-permute-start.12) | collective-permute-done | bytes 262176 | tf_op jit(solution)/shard_map/ppermute | solution.py:366
  192.3 0.7 copy-done.6
  193.0 1.3 collective-permute-start.7
  194.5 5.7 %collective-permute-done.8.rest_11_ = bf16[32,32,128]{2,1,0:T(8,128)(2,1)} collective-permute-done((bf16[32,32,128]{2,1,0:T(8,128)(2,1)}, bf16[32,32,128]{2,1,0:T(8,128)(2,1)}, u32[]{:S(2)}, u32[]{:S(2)}) %collective-permute-start.8) | collective-permute-done | bytes 262176 | tf_op jit(solution)/shard_map/ppermute | solution.py:366
  200.2 9.2 %collective-permute-done.7.rest_10_ = bf16[32,32,128]{2,1,0:T(8,128)(2,1)} collective-permute-done((bf16[32,32,128]{2,1,0:T(8,128)(2,1)}, bf16[32,32,128]{2,1,0:T(8,128)(2,1)}, u32[]{:S(2)}, u32[]{:S(2)}) %collective-permute-start.7) | collective-permute-done | bytes 262176 | tf_op jit(solution)/shard_map/ppermute | solution.py:366
  209.5 0.9 copy-done.5
  210.4 0.9 copy-done.7
  211.4 7.1 %finish.1 = (bf16[1,32,128,256]{3,2,1,0:T(8,128)(2,1)}, bf16[1,32,64,256]{3,2,1,0:T(8,128)(2,1)}) custom-call(s32[1]{0:T(128)} %bitcast.level_ref, s32[64]{0:T(128)S(1)} %select_reduce_fusion.8.slot_ref, s32[32,128]{1,0:T(8,128)S(1)} %add_bitcast_fusion.rows_ref, bf16[32,128,256]{2,1,0:T(8,128)(2,1)} %bitcast.60, bf16[32,128,128]{2,1,0:T(8,128)(2,1)} %bitcast.64, ...), custom_call_target="tpu_custom_call" | custom-call | tf_op jit(solution)/shard_map/finish/pallas_call | solution.py:373
  (54 shorter events, 2.9 us)
Async XLA Ops:
  7.2 2.9 %copy-start = (s32[8,64,1024]{2,1,0:T(8,128)S(1)}, s32[8,64,1024]{2,1,0:T(8,128)}, u32[]{:S(2)}) copy-start(s32[8,64,1024]{2,1,0:T(8,128)} %param.11) | copy-start | bytes 6291460
  7.2 57.3 %all-gather.7.cloned.1.call-start = ((), (), s32[]{:S(2)}) async-start(), calls=%async_computation.8 | async-start | bytes 4718592 | tf_op jit(solution)/shard_map/all_gather | solution.py:318
  18.5 1.0 copy-start.3
  21.6 19.9 %all-to-all-start = ((bf16[8,16,32,128]{3,2,1,0:T(8,128)(2,1)}), bf16[8,16,32,128]{3,2,1,0:T(8,128)(2,1)S(1)}, u32[]{:S(2)}, u32[]{:S(2)}) async-start(bf16[8,16,32,128]{3,2,1,0:T(8,128)(2,1)} %get-tuple-element.6), calls=%async_computation | async-start | bytes 2097152 | tf_op jit(solution)/shard_map/all_to_all | solution.py:319
  41.5 23.0 %copy-start.1 = (bf16[8,16,32,128]{3,2,1,0:T(8,128)(2,1)}, bf16[8,16,32,128]{3,2,1,0:T(8,128)(2,1)S(1)}, u32[]{:S(2)}) copy-start(bf16[8,16,32,128]{3,2,1,0:T(8,128)(2,1)S(1)} %all-to-all-done.load_ref) | copy-start | bytes 3145732
  42.3 0.7 copy-start.2
  43.0 21.5 %all-to-all-start.1 = ((bf16[32,32,128]{2,1,0:T(8,128)(2,1)}), bf16[32,32,128]{2,1,0:T(8,128)(2,1)S(1)}, u32[]{:S(2)}, u32[]{:S(2)}) async-start(bf16[32,32,128]{2,1,0:T(8,128)(2,1)} %copy-done.2), calls=%async_computation.1 | async-start | bytes 524288 | tf_op jit(solution)/shard_map/all_to_all | solution.py:354
  54.0 101.2 %all-gather.9.cloned.1.call-start = ((), (), s32[]{:S(2)}) async-start(), calls=%async_computation.9 | async-start | bytes 7077888 | tf_op jit(solution)/shard_map/all_gather | solution.py:357
  102.7 91.6 %all-gather.11.cloned.1.call-start = ((), (), s32[]{:S(2)}) async-start(), calls=%async_computation.10 | async-start | bytes 4718592 | tf_op jit(solution)/shard_map/all_gather | solution.py:357
  159.1 19.7 %all-to-all-start.7 = ((bf16[32,32,128]{2,1,0:T(8,128)(2,1)}), bf16[32,32,128]{2,1,0:T(8,128)(2,1)}, u32[]{:S(2)}, u32[]{:S(2)}) async-start(bf16[32,32,128]{2,1,0:T(8,128)(2,1)} %hop.11), calls=%async_computation.7 | async-start | bytes 524288 | tf_op jit(solution)/shard_map/all_to_all | solution.py:354
  163.7 12.3 %collective-permute-start.6 = (bf16[32,32,128]{2,1,0:T(8,128)(2,1)S(1)}, bf16[32,32,128]{2,1,0:T(8,128)(2,1)S(1)}, u32[]{:S(2)}, u32[]{:S(2)}) collective-permute-start(bf16[32,32,128]{2,1,0:T(8,128)(2,1)S(1)} %all_to_all.44.got_ref.rest_8_), channel_id=1, source_target_pairs={{224,192},{225,193},{226,194},{227,195},{228,196},{229,197},{230,1... | collective-permute-start | bytes 786440 | tf_op jit(solution)/shard_map/ppermute | solution.py:366
  172.6 4.8 %collective-permute-start.5 = (bf16[32,32,128]{2,1,0:T(8,128)(2,1)S(1)}, bf16[32,32,128]{2,1,0:T(8,128)(2,1)S(1)}, u32[]{:S(2)}, u32[]{:S(2)}) collective-permute-start(bf16[32,32,128]{2,1,0:T(8,128)(2,1)S(1)} %all_to_all.44.got_ref.rest_8_), channel_id=1, source_target_pairs={{160,192},{161,193},{162,194},{163,195},{164,196},{165,197},{166,1... | collective-permute-start | bytes 786440 | tf_op jit(solution)/shard_map/ppermute | solution.py:366
  173.3 5.5 %collective-permute-start.4 = (bf16[32,32,128]{2,1,0:T(8,128)(2,1)S(1)}, bf16[32,32,128]{2,1,0:T(8,128)(2,1)S(1)}, u32[]{:S(2)}, u32[]{:S(2)}) collective-permute-start(bf16[32,32,128]{2,1,0:T(8,128)(2,1)S(1)} %all_to_all.44.got_ref.rest_8_), channel_id=1, source_target_pairs={{128,192},{129,193},{130,194},{131,195},{132,196},{133,197},{134,1... | collective-permute-start | bytes 786440 | tf_op jit(solution)/shard_map/ppermute | solution.py:366
  174.0 6.1 %collective-permute-start.3 = (bf16[32,32,128]{2,1,0:T(8,128)(2,1)S(1)}, bf16[32,32,128]{2,1,0:T(8,128)(2,1)S(1)}, u32[]{:S(2)}, u32[]{:S(2)}) collective-permute-start(bf16[32,32,128]{2,1,0:T(8,128)(2,1)S(1)} %all_to_all.44.got_ref.rest_8_), channel_id=1, source_target_pairs={{96,192},{97,193},{98,194},{99,195},{100,196},{101,197},{102,198},... | collective-permute-start | bytes 786440 | tf_op jit(solution)/shard_map/ppermute | solution.py:366
  174.7 6.7 %collective-permute-start.2 = (bf16[32,32,128]{2,1,0:T(8,128)(2,1)S(1)}, bf16[32,32,128]{2,1,0:T(8,128)(2,1)}, u32[]{:S(2)}, u32[]{:S(2)}) collective-permute-start(bf16[32,32,128]{2,1,0:T(8,128)(2,1)S(1)} %all_to_all.44.got_ref.rest_8_), channel_id=1, source_target_pairs={{64,192},{65,193},{66,194},{67,195},{68,196},{69,197},{70,198},{71... | collective-permute-start | bytes 786440 | tf_op jit(solution)/shard_map/ppermute | solution.py:366
  176.0 6.6 %collective-permute-start.1 = (bf16[32,32,128]{2,1,0:T(8,128)(2,1)S(1)}, bf16[32,32,128]{2,1,0:T(8,128)(2,1)}, u32[]{:S(2)}, u32[]{:S(2)}) collective-permute-start(bf16[32,32,128]{2,1,0:T(8,128)(2,1)S(1)} %all_to_all.44.got_ref.rest_8_), channel_id=1, source_target_pairs={{32,192},{33,193},{34,194},{35,195},{36,196},{37,197},{38,198},{39... | collective-permute-start | bytes 786440 | tf_op jit(solution)/shard_map/ppermute | solution.py:366
  177.4 6.6 %collective-permute-start = (bf16[32,32,128]{2,1,0:T(8,128)(2,1)S(1)}, bf16[32,32,128]{2,1,0:T(8,128)(2,1)}, u32[]{:S(2)}, u32[]{:S(2)}) collective-permute-start(bf16[32,32,128]{2,1,0:T(8,128)(2,1)S(1)} %all_to_all.44.got_ref.rest_8_), channel_id=1, source_target_pairs={{0,192},{1,193},{2,194},{3,195},{4,196},{5,197},{6,198},{7,199},{8... | collective-permute-start | bytes 786440 | tf_op jit(solution)/shard_map/ppermute | solution.py:366
  178.8 8.4 %collective-permute-start.13 = (bf16[32,32,128]{2,1,0:T(8,128)(2,1)}, bf16[32,32,128]{2,1,0:T(8,128)(2,1)S(1)}, u32[]{:S(2)}, u32[]{:S(2)}) collective-permute-start(bf16[32,32,128]{2,1,0:T(8,128)(2,1)} %all-to-all-done.7.rest_17_), channel_id=1, source_target_pairs={{192,224},{193,225},{194,226},{195,227},{196,228},{197,229},{198,2... | collective-permute-start | bytes 786440 | tf_op jit(solution)/shard_map/ppermute | solution.py:366
  180.1 12.2 %collective-permute-start.12 = (bf16[32,32,128]{2,1,0:T(8,128)(2,1)}, bf16[32,32,128]{2,1,0:T(8,128)(2,1)S(1)}, u32[]{:S(2)}, u32[]{:S(2)}) collective-permute-start(bf16[32,32,128]{2,1,0:T(8,128)(2,1)} %all-to-all-done.7.rest_17_), channel_id=1, source_target_pairs={{160,224},{161,225},{162,226},{163,227},{164,228},{165,229},{166,2... | collective-permute-start | bytes 786440 | tf_op jit(solution)/shard_map/ppermute | solution.py:366
  181.4 12.9 %collective-permute-start.11 = (bf16[32,32,128]{2,1,0:T(8,128)(2,1)}, bf16[32,32,128]{2,1,0:T(8,128)(2,1)}, u32[]{:S(2)}, u32[]{:S(2)}) collective-permute-start(bf16[32,32,128]{2,1,0:T(8,128)(2,1)} %all-to-all-done.7.rest_17_), channel_id=1, source_target_pairs={{128,224},{129,225},{130,226},{131,227},{132,228},{133,229},{134,2... | collective-permute-start | bytes 786440 | tf_op jit(solution)/shard_map/ppermute | solution.py:366
  182.7 11.6 %collective-permute-start.10 = (bf16[32,32,128]{2,1,0:T(8,128)(2,1)}, bf16[32,32,128]{2,1,0:T(8,128)(2,1)}, u32[]{:S(2)}, u32[]{:S(2)}) collective-permute-start(bf16[32,32,128]{2,1,0:T(8,128)(2,1)} %all-to-all-done.7.rest_17_), channel_id=1, source_target_pairs={{96,224},{97,225},{98,226},{99,227},{100,228},{101,229},{102,230},... | collective-permute-start | bytes 786440 | tf_op jit(solution)/shard_map/ppermute | solution.py:366
  184.0 10.5 %collective-permute-start.9 = (bf16[32,32,128]{2,1,0:T(8,128)(2,1)}, bf16[32,32,128]{2,1,0:T(8,128)(2,1)}, u32[]{:S(2)}, u32[]{:S(2)}) collective-permute-start(bf16[32,32,128]{2,1,0:T(8,128)(2,1)} %all-to-all-done.7.rest_17_), channel_id=1, source_target_pairs={{64,224},{65,225},{66,226},{67,227},{68,228},{69,229},{70,230},{71... | collective-permute-start | bytes 786440 | tf_op jit(solution)/shard_map/ppermute | solution.py:366
  187.1 0.7 copy-start.4
  187.8 12.4 %collective-permute-start.8 = (bf16[32,32,128]{2,1,0:T(8,128)(2,1)}, bf16[32,32,128]{2,1,0:T(8,128)(2,1)}, u32[]{:S(2)}, u32[]{:S(2)}) collective-permute-start(bf16[32,32,128]{2,1,0:T(8,128)(2,1)} %all-to-all-done.7.rest_17_), channel_id=1, source_target_pairs={{32,224},{33,225},{34,226},{35,227},{36,228},{37,229},{38,230},{39... | collective-permute-start | bytes 786440 | tf_op jit(solution)/shard_map/ppermute | solution.py:366
  192.3 0.7 copy-start.6
  193.0 16.5 %collective-permute-start.7 = (bf16[32,32,128]{2,1,0:T(8,128)(2,1)}, bf16[32,32,128]{2,1,0:T(8,128)(2,1)}, u32[]{:S(2)}, u32[]{:S(2)}) collective-permute-start(bf16[32,32,128]{2,1,0:T(8,128)(2,1)} %all-to-all-done.7.rest_17_), channel_id=1, source_target_pairs={{0,224},{1,225},{2,226},{3,227},{4,228},{5,229},{6,230},{7,231},{8... | collective-permute-start | bytes 786440 | tf_op jit(solution)/shard_map/ppermute | solution.py:366
  209.5 1.0 copy-start.5
  210.4 0.9 copy-start.7
Sparse Core Ops, SparseCore 0:
  21.7 38.0 all-gather.6
  102.8 40.1 all-gather.8
  144.9 35.8 all-gather.10

commit v3 on v2

--- a/solution.py
+++ b/solution.py
@@ -65,10 +65,10 @@
 
 
 def first_kernel(take_ref, load_ref, send_ref, values):
-    _, pairs, span, lanes = load_ref.shape
+    pairs, span, lanes = load_ref.shape
     low = low_lanes((span, lanes), lanes // 2)
     for pair in range(pairs):
-        value = load_ref[0, pair].astype(F32)
+        value = load_ref[pair].astype(F32)
         for odd in (0, 1):
             values[2 * pair + odd] = both_halves(value, odd, low, lanes // 2).astype(BF16)
     values[2 * pairs] = jnp.zeros((span, lanes), BF16)
@@ -76,59 +76,37 @@
 
 
 def hop_kernel(
-    level,
-    take_ref,
-    slot_ref,
-    got_ref,
-    op_ref,
-    load_ref,
-    send_ref,
-    got,
-    ops,
-    load,
-    total,
-    values,
-    ready,
+    level, take_ref, slot_ref, got_ref, op_ref, load_ref, send_ref, ops, total, values, ready
 ):
-    senders, span, lanes = got.shape
-    pairs = load.shape[0]
+    senders, span, lanes = got_ref.shape
+    pairs = load_ref.shape[0]
     half = lanes // 2
-    parts = ready.shape[1]
-    share = senders // parts
+    share = senders // ready.shape[0]
     copies = []
-    for i in range(parts):
+    for i in range(ready.shape[0]):
         where = pl.ds(i * share, share)
         copies.append(
-            (
-                pltpu.make_async_copy(got_ref.at[where], got.at[where], ready.at[0, i]),
-                pltpu.make_async_copy(op_ref.at[level, where], ops.at[where], ready.at[1, i]),
-            )
+            pltpu.make_async_copy(op_ref.at[level, where], ops.at[where], ready.at[i])
         )
-    loading = pltpu.make_async_copy(load_ref.at[level], load, ready.at[2, 0])
-    for pair in copies:
-        for copy in pair:
-            copy.start()
-    loading.start()
+        copies[-1].start()
     low = low_lanes((span, lanes), half)
     low_op = low_lanes((half, lanes), half)
     total[...] = jnp.zeros_like(total)
     for s in range(senders):
         if s % share == 0:
-            for copy in copies[s // share]:
-                copy.wait()
+            copies[s // share].wait()
         op = ops[s]
         zero = jnp.zeros_like(op)
         split = jnp.concatenate(
             [jnp.where(low_op, op, zero), jnp.where(low_op, zero, op)], axis=0
         )
-        part = dot_nt(got[s], split)
+        part = dot_nt(got_ref[s], split)
         one = slot_ref[level - 1, 2 * s]
         two = slot_ref[level - 1, 2 * s + 1]
         total[one] += jnp.where(low, part, 0.0)
         total[two] += jnp.where(low, 0.0, part)
-    loading.wait()
     for pair in range(pairs):
-        value = load[pair].astype(F32)
+        value = load_ref[pair].astype(F32)
         for odd in (0, 1):
             node = 2 * pair + odd
             come = total[node]
@@ -321,7 +299,7 @@
     message = jax.ShapeDtypeStruct((group, span, lanes), BF16)
     values_shape = pltpu.VMEM((nodes + 1, span, lanes), BF16)
     arrived = [None]
-    early_counts = (hops // 2, hops - 2 - hops // 2)
+    early_counts = (hops // 2, hops - 1 - hops // 2)
     early = []
     for level in range(hops):
         if level == 0:
@@ -333,24 +311,22 @@
                 scratch_shapes=[values_shape],
                 compiler_params=params(16),
                 name="first",
-            )(take, loads)
+            )(take, loads[0])
         else:
             send = pl.pallas_call(
                 functools.partial(hop_kernel, level),
-                in_specs=[SMEM_SPEC, SMEM_SPEC, HBM_SPEC, HBM_SPEC, HBM_SPEC],
+                in_specs=[SMEM_SPEC, SMEM_SPEC, VMEM_SPEC, HBM_SPEC, VMEM_SPEC],
                 out_specs=VMEM_SPEC,
                 out_shape=message,
                 scratch_shapes=[
-                    pltpu.VMEM((group, span, lanes), BF16),
                     pltpu.VMEM((group, rows, lanes), BF16),
-                    pltpu.VMEM((pairs, span, lanes), BF16),
                     pltpu.VMEM((nodes + 1, span, lanes), F32),
                     values_shape,
-                    pltpu.SemaphoreType.DMA((3, 4)),
+                    pltpu.SemaphoreType.DMA((8,)),
                 ],
                 compiler_params=params(53),
                 name="hop",
-            )(take, slot, arrived[-1], operators, loads)
+            )(take, slot, arrived[-1], operators, loads[level])
         arrived.append(lax.all_to_all(send, "grp", split_axis=0, concat_axis=0, tiled=True))
         if len(arrived) == 1 + sum(early_counts[: len(early) + 1]) and len(early) < 2:
             ready = jnp.stack(arrived[1 + sum(early_counts[: len(early)]) :])
@@ -392,7 +368,7 @@
             pltpu.SemaphoreType.DMA((3,)),
             pltpu.SemaphoreType.DMA((levels, parts)),
         ],
-        compiler_params=params(50, "arbitrary"),
+        compiler_params=params(58, "arbitrary"),
         name="finish",
     )(
         level_id.reshape(1),

time: 226 us -> 228 us (level)
  starting transfers between devices: 45.6 us -> 25.3 us
  blocking collectives: 73 us -> 84 us
  waiting for transfers between devices: 44.1 us -> 54.5 us
    ppermute x14 -> x7, starting transfers between devices: 24 us -> 9.01 us  [shards(): lax.ppermute(arrived[level], 'level', [(c, level)])]
    all_to_all x5 -> x6, blocking collectives: 73 us -> 84 us  [shards(): lax.all_to_all(send, 'grp', split_axis=0, concat_axis=0, tiled=True)]
    all_gather x2, waiting for transfers between devices: 0.02 us -> 6.14 us  [shards(): early.append(lax.all_gather(ready, 'level', axis=0))]
    all_to_all x2 -> x1, starting transfers between devices: 15.7 us -> 9.76 us  [shards(): lax.all_to_all(send, 'grp', split_axis=0, concat_axis=0, tiled=True)]
    ppermute x14 -> x7, waiting for transfers between devices: 20.2 us -> 23.8 us  [shards(): lax.ppermute(arrived[level], 'level', [(c, level)])]
    unnamed x18 -> x24, local copies, waits for them, and re-layouts: 5.25 us -> 1.98 us
    all_to_all x2 -> x1, waiting for transfers between devices: 10.3 us -> 10.3 us  [shards(): lax.all_to_all(send, 'grp', split_axis=0, concat_axis=0, tiled=True)]
  transfers between devices with their start and end apart: 20 -> 12, of which waited for: 7 -> 9; matrix products, arithmetic and copies ran while one was open for 1% -> 1% of each run, Pallas kernels for 6% -> 7%
where the time goes in v3:
time: 228 us; the launch traced here: 226 us
  blocking collectives  84 us (37%)
  waiting for transfers between devices  54.5 us (24%)
  Pallas kernels  39.1 us (17%)
  starting transfers between devices  25.3 us (11%)
  between operations  14 us (6%)
  local copies, waits for them, and re-layouts  5.61 us (2%)
  other arithmetic  3.67 us (2%)
    all_to_all x6, blocking collectives, shards(): lax.all_to_all(send, 'grp', split_axis=0, concat_axis=0, tiled=True)  84 us
    ppermute x7, waiting for transfers between devices, shards(): lax.ppermute(arrived[level], 'level', [(c, level)])  23.8 us
    pallas_call x6, Pallas kernels, shards(): pl.pallas_call(functools.partial(hop_kernel, level), in_specs=[SMEM_SPEC,...  20.7 us
    all_to_all x1, waiting for transfers between devices, shards(): lax.all_to_all(load, 'level', split_axis=0, concat_axis=0, tiled=True)  14.3 us
    all_to_all x1, waiting for transfers between devices, shards(): lax.all_to_all(send, 'grp', split_axis=0, concat_axis=0, tiled=True)  10.3 us
    all_to_all x1, starting transfers between devices, shards(): lax.all_to_all(send, 'grp', split_axis=0, concat_axis=0, tiled=True)  9.76 us
    ppermute x7, starting transfers between devices, shards(): lax.ppermute(arrived[level], 'level', [(c, level)])  9.01 us
    pallas_call x1, Pallas kernels, shards(): pl.pallas_call(prepare_kernel, grid=(nodes // step,), in_specs=[pl.BlockS...  7.55 us
  transfers between devices with their start and end apart: 12, of which 9 were waited for; matrix products, arithmetic and copies ran while one was open for 1% of the time, Pallas kernels for 7%

profile of v3, /device:TPU:25, one launch (start us, length us, event | category | flops | bytes accessed | tf_op | source)
XLA Modules:
  0.0 226.3 jit_solution(7640864653056534339)
XLA Ops:
  7.2 0.9 slice_reduce_fusion
  8.3 0.3 select_reduce_fusion.7
  8.6 0.8 reshape.109
  9.5 0.4 select_reduce_fusion.6
  9.9 0.1 copy.62
  10.1 0.2 copy.79
  10.3 0.2 select_reduce_fusion.8.slot_ref
  10.5 0.3 select_reduce_fusion.1
  11.0 7.6 %prepare.1 = (bf16[32,64,128]{2,1,0:T(8,128)(2,1)}, bf16[8,16,32,128]{3,2,1,0:T(8,128)(2,1)}) custom-call(bf16[32,128,256]{2,1,0:T(8,128)(2,1)} %bitcast.75, bf16[32,128,128]{2,1,0:T(8,128)(2,1)} %bitcast.79, bf16[32,64,128]{2,1,0:T(8,128)(2,1)} %bitcast.81), custom_call_target="tpu_custom_call" | custom-call | tf_op jit(solution)/shard_map/prepare/pallas_call | solution.py:233
  18.5 1.0 copy-done.1
  19.6 2.0 operators.1
  21.6 6.4 %all-to-all-start = ((bf16[8,16,32,128]{3,2,1,0:T(8,128)(2,1)}), bf16[8,16,32,128]{3,2,1,0:T(8,128)(2,1)}, u32[]{:S(2)}, u32[]{:S(2)}) async-start(bf16[8,16,32,128]{3,2,1,0:T(8,128)(2,1)} %get-tuple-element.4), calls=%async_computation | async-start | bytes 2097152 | tf_op jit(solution)/shard_map/all_to_all | solution.py:297
  28.1 0.3 select_reduce_fusion.3
  28.6 14.3 %all-to-all-done = bf16[8,16,32,128]{3,2,1,0:T(8,128)(2,1)} async-done(((bf16[8,16,32,128]{3,2,1,0:T(8,128)(2,1)}), bf16[8,16,32,128]{3,2,1,0:T(8,128)(2,1)}, u32[]{:S(2)}, u32[]{:S(2)}) %all-to-all-start) | async-done | bytes 1048608 | tf_op jit(solution)/shard_map/all_to_all | solution.py:297
  42.9 1.3 slice_bitcast_fusion
  44.2 1.5 first.1
  45.8 9.8 %all-to-all-start.1 = ((bf16[32,32,128]{2,1,0:T(8,128)(2,1)}), bf16[32,32,128]{2,1,0:T(8,128)(2,1)S(1)}, u32[]{:S(2)}, u32[]{:S(2)}) async-start(bf16[32,32,128]{2,1,0:T(8,128)(2,1)} %first.1), calls=%async_computation.1 | async-start | bytes 524288 | tf_op jit(solution)/shard_map/all_to_all | solution.py:330
  55.6 10.3 %all-to-all-done.1.got_ref = bf16[32,32,128]{2,1,0:T(8,128)(2,1)S(1)} async-done(((bf16[32,32,128]{2,1,0:T(8,128)(2,1)}), bf16[32,32,128]{2,1,0:T(8,128)(2,1)S(1)}, u32[]{:S(2)}, u32[]{:S(2)}) %all-to-all-start.1) | async-done | bytes 262176 | tf_op jit(solution)/shard_map/all_to_all | solution.py:330
  65.9 3.5 %hop.6 = bf16[32,32,128]{2,1,0:T(8,128)(2,1)S(1)} custom-call(s32[7,64]{1,0:T(8,128)S(1)} %copy.65.take_ref, s32[7,64]{1,0:T(8,128)S(1)} %copy.67.slot_ref, bf16[32,32,128]{2,1,0:T(8,128)(2,1)S(1)} %all-to-all-done.1.got_ref, bf16[8,32,64,128]{3,2,1,0:T(8,128)(2,1)} %bitcast.69, bf16[16,32,128]{2,1,0:T(8,128)(2,1)S(1)} %get-tuple-element.19.load_ref), custom_call_target="tpu_custom_call" | custom-call | tf_op jit(solution)/shard_map/hop/pallas_call | solution.py:316
  69.4 14.4 %all_to_all.40.got_ref = bf16[32,32,128]{2,1,0:T(8,128)(2,1)S(1)} all-to-all(bf16[32,32,128]{2,1,0:T(8,128)(2,1)S(1)} %hop.6), channel_id=1, replica_groups=mesh['level'=8,'grp'=32] {'grp'}, dimensions={0} | all-to-all | bytes 524288 | tf_op jit(solution)/shard_map/all_to_all | solution.py:330
  83.8 3.4 %hop.7 = bf16[32,32,128]{2,1,0:T(8,128)(2,1)S(1)} custom-call(s32[7,64]{1,0:T(8,128)S(1)} %copy.65.take_ref, s32[7,64]{1,0:T(8,128)S(1)} %copy.67.slot_ref, bf16[32,32,128]{2,1,0:T(8,128)(2,1)S(1)} %all_to_all.40.got_ref, bf16[8,32,64,128]{3,2,1,0:T(8,128)(2,1)} %bitcast.70, bf16[16,32,128]{2,1,0:T(8,128)(2,1)S(1)} %get-tuple-element.18.load_ref), custom_call_target="tpu_custom_call" | custom-call | tf_op jit(solution)/shard_map/hop/pallas_call | solution.py:316
  87.2 14.1 %all_to_all.41.got_ref = bf16[32,32,128]{2,1,0:T(8,128)(2,1)S(1)} all-to-all(bf16[32,32,128]{2,1,0:T(8,128)(2,1)S(1)} %hop.7), channel_id=1, replica_groups=mesh['level'=8,'grp'=32] {'grp'}, dimensions={0} | all-to-all | bytes 524288 | tf_op jit(solution)/shard_map/all_to_all | solution.py:330
  101.3 1.0 pad_maximum_fusion
  102.3 3.5 %hop.8 = bf16[32,32,128]{2,1,0:T(8,128)(2,1)S(1)} custom-call(s32[7,64]{1,0:T(8,128)S(1)} %copy.65.take_ref, s32[7,64]{1,0:T(8,128)S(1)} %copy.67.slot_ref, bf16[32,32,128]{2,1,0:T(8,128)(2,1)S(1)} %all_to_all.41.got_ref, bf16[8,32,64,128]{3,2,1,0:T(8,128)(2,1)} %bitcast.71, bf16[16,32,128]{2,1,0:T(8,128)(2,1)S(1)} %get-tuple-element.17.load_ref), custom_call_target="tpu_custom_call" | custom-call | tf_op jit(solution)/shard_map/hop/pallas_call | solution.py:316
  105.8 13.8 %all_to_all.42.got_ref = bf16[32,32,128]{2,1,0:T(8,128)(2,1)S(1)} all-to-all(bf16[32,32,128]{2,1,0:T(8,128)(2,1)S(1)} %hop.8), channel_id=1, replica_groups=mesh['level'=8,'grp'=32] {'grp'}, dimensions={0} | all-to-all | bytes 524288 | tf_op jit(solution)/shard_map/all_to_all | solution.py:330
  119.6 3.5 %hop.9 = bf16[32,32,128]{2,1,0:T(8,128)(2,1)S(1)} custom-call(s32[7,64]{1,0:T(8,128)S(1)} %copy.65.take_ref, s32[7,64]{1,0:T(8,128)S(1)} %copy.67.slot_ref, bf16[32,32,128]{2,1,0:T(8,128)(2,1)S(1)} %all_to_all.42.got_ref, bf16[8,32,64,128]{3,2,1,0:T(8,128)(2,1)} %bitcast.72, bf16[16,32,128]{2,1,0:T(8,128)(2,1)S(1)} %get-tuple-element.16.load_ref), custom_call_target="tpu_custom_call" | custom-call | tf_op jit(solution)/shard_map/hop/pallas_call | solution.py:316
  123.1 13.8 %all_to_all.43.got_ref = bf16[32,32,128]{2,1,0:T(8,128)(2,1)S(1)} all-to-all(bf16[32,32,128]{2,1,0:T(8,128)(2,1)S(1)} %hop.9), channel_id=1, replica_groups=mesh['level'=8,'grp'=32] {'grp'}, dimensions={0} | all-to-all | bytes 524288 | tf_op jit(solution)/shard_map/all_to_all | solution.py:330
  136.9 3.4 %hop.10 = bf16[32,32,128]{2,1,0:T(8,128)(2,1)S(1)} custom-call(s32[7,64]{1,0:T(8,128)S(1)} %copy.65.take_ref, s32[7,64]{1,0:T(8,128)S(1)} %copy.67.slot_ref, bf16[32,32,128]{2,1,0:T(8,128)(2,1)S(1)} %all_to_all.43.got_ref, bf16[8,32,64,128]{3,2,1,0:T(8,128)(2,1)} %bitcast.73, bf16[16,32,128]{2,1,0:T(8,128)(2,1)S(1)} %get-tuple-element.15.load_ref), custom_call_target="tpu_custom_call" | custom-call | tf_op jit(solution)/shard_map/hop/pallas_call | solution.py:316
  140.4 14.0 %all_to_all.44.got_ref = bf16[32,32,128]{2,1,0:T(8,128)(2,1)S(1)} all-to-all(bf16[32,32,128]{2,1,0:T(8,128)(2,1)S(1)} %hop.10), channel_id=1, replica_groups=mesh['level'=8,'grp'=32] {'grp'}, dimensions={0} | all-to-all | bytes 524288 | tf_op jit(solution)/shard_map/all_to_all | solution.py:330
  154.4 1.0 pad_maximum_fusion.1
  155.4 3.5 %hop.11 = bf16[32,32,128]{2,1,0:T(8,128)(2,1)S(1)} custom-call(s32[7,64]{1,0:T(8,128)S(1)} %copy.65.take_ref, s32[7,64]{1,0:T(8,128)S(1)} %copy.67.slot_ref, bf16[32,32,128]{2,1,0:T(8,128)(2,1)S(1)} %all_to_all.44.got_ref, bf16[8,32,64,128]{3,2,1,0:T(8,128)(2,1)} %bitcast.74, bf16[16,32,128]{2,1,0:T(8,128)(2,1)S(1)} %get-tuple-element.14.load_ref), custom_call_target="tpu_custom_call" | custom-call | tf_op jit(solution)/shard_map/hop/pallas_call | solution.py:316
  158.8 13.9 %all_to_all.45.rest_9_ = bf16[32,32,128]{2,1,0:T(8,128)(2,1)S(1)} all-to-all(bf16[32,32,128]{2,1,0:T(8,128)(2,1)S(1)} %hop.11), channel_id=1, replica_groups=mesh['level'=8,'grp'=32] {'grp'}, dimensions={0} | all-to-all | bytes 524288 | tf_op jit(solution)/shard_map/all_to_all | solution.py:330
  172.8 1.3 collective-permute-start.6
  174.1 1.3 collective-permute-start.5
  175.4 1.3 collective-permute-start.4
  176.7 1.3 collective-permute-start.3
  178.0 1.3 collective-permute-start.2
  179.3 6.5 %collective-permute-done.6.rest_8_ = bf16[32,32,128]{2,1,0:T(8,128)(2,1)S(1)} collective-permute-done((bf16[32,32,128]{2,1,0:T(8,128)(2,1)S(1)}, bf16[32,32,128]{2,1,0:T(8,128)(2,1)S(1)}, u32[]{:S(2)}, u32[]{:S(2)}) %collective-permute-start.6) | collective-permute-done | bytes 262176 | tf_op jit(solution)/shard_map/ppermute | solution.py:342
  185.8 1.3 collective-permute-start.1
  187.1 0.1 collective-permute-done.5.rest_7_
  187.2 1.3 collective-permute-start
  188.5 8.2 %collective-permute-done.4.rest_6_ = bf16[32,32,128]{2,1,0:T(8,128)(2,1)S(1)} collective-permute-done((bf16[32,32,128]{2,1,0:T(8,128)(2,1)S(1)}, bf16[32,32,128]{2,1,0:T(8,128)(2,1)S(1)}, u32[]{:S(2)}, u32[]{:S(2)}) %collective-permute-start.4) | collective-permute-done | bytes 262176 | tf_op jit(solution)/shard_map/ppermute | solution.py:342
  196.7 2.4 %collective-permute-done.2.rest_4_ = bf16[32,32,128]{2,1,0:T(8,128)(2,1)S(1)} collective-permute-done((bf16[32,32,128]{2,1,0:T(8,128)(2,1)S(1)}, bf16[32,32,128]{2,1,0:T(8,128)(2,1)S(1)}, u32[]{:S(2)}, u32[]{:S(2)}) %collective-permute-start.2) | collective-permute-done | bytes 262176 | tf_op jit(solution)/shard_map/ppermute | solution.py:342
  199.0 6.0 %collective-permute-done.1.rest_3_ = bf16[32,32,128]{2,1,0:T(8,128)(2,1)S(1)} collective-permute-done((bf16[32,32,128]{2,1,0:T(8,128)(2,1)S(1)}, bf16[32,32,128]{2,1,0:T(8,128)(2,1)S(1)}, u32[]{:S(2)}, u32[]{:S(2)}) %collective-permute-start.1) | collective-permute-done | bytes 262176 | tf_op jit(solution)/shard_map/ppermute | solution.py:342
  205.0 0.7 copy-done.10
  205.7 0.6 collective-permute-done.rest_2_
  206.3 6.1 %all-gather.11.cloned.1.call-done = bf16[24,32,32,128]{3,2,1,0:T(8,128)(2,1)} async-done(((bf16[3,32,32,128]{3,2,1,0:T(8,128)(2,1)}), bf16[24,32,32,128]{3,2,1,0:T(8,128)(2,1)}) %all-gather.11.cloned.1.call-update) | async-done | bytes 6291472 | tf_op jit(solution)/shard_map/all_gather | solution.py:333
  212.5 7.3 %finish.1 = (bf16[1,32,128,256]{3,2,1,0:T(8,128)(2,1)}, bf16[1,32,64,256]{3,2,1,0:T(8,128)(2,1)}) custom-call(s32[1]{0:T(128)} %bitcast.level_ref, s32[64]{0:T(128)} %copy-done.3, s32[32,128]{1,0:T(8,128)} %copy-done.2, bf16[32,128,256]{2,1,0:T(8,128)(2,1)} %bitcast.76, bf16[32,128,128]{2,1,0:T(8,128)(2,1)} %bitcast.80, bf16[32,64,128]{2,1,0:T(8,128)(2,1)} %bitcast.82, ...), custom_call_target="tpu_custom_call" | custom-call | tf_op jit(solution)/shard_map/finish/pallas_call | solution.py:349
  (46 shorter events, 0.9 us)
Async XLA Ops:
  7.2 2.9 %copy-start = (s32[8,64,1024]{2,1,0:T(8,128)S(1)}, s32[8,64,1024]{2,1,0:T(8,128)}, u32[]{:S(2)}) copy-start(s32[8,64,1024]{2,1,0:T(8,128)} %param.11) | copy-start | bytes 6291460
  7.2 58.7 %all-gather.7.cloned.1.call-start = ((), (), s32[]{:S(2)}) async-start(), calls=%async_computation.8 | async-start | bytes 4718592 | tf_op jit(solution)/shard_map/all_gather | solution.py:296
  10.5 8.1 %copy-start.3 = (s32[64]{0:T(128)}, s32[64]{0:T(128)S(1)}, u32[]{:S(2)}) copy-start(s32[64]{0:T(128)S(1)} %select_reduce_fusion.8.slot_ref) | copy-start | bytes 772
  11.0 10.6 %copy-start.2 = (s32[32,128]{1,0:T(8,128)}, s32[32,128]{1,0:T(8,128)S(1)}, u32[]{:S(2)}) copy-start(s32[32,128]{1,0:T(8,128)S(1)} %add_bitcast_fusion.rows_ref) | copy-start | bytes 49156
  18.5 1.0 copy-start.1
  21.6 21.3 %all-to-all-start = ((bf16[8,16,32,128]{3,2,1,0:T(8,128)(2,1)}), bf16[8,16,32,128]{3,2,1,0:T(8,128)(2,1)}, u32[]{:S(2)}, u32[]{:S(2)}) async-start(bf16[8,16,32,128]{3,2,1,0:T(8,128)(2,1)} %get-tuple-element.4), calls=%async_computation | async-start | bytes 2097152 | tf_op jit(solution)/shard_map/all_to_all | solution.py:297
  45.8 20.2 %all-to-all-start.1 = ((bf16[32,32,128]{2,1,0:T(8,128)(2,1)}), bf16[32,32,128]{2,1,0:T(8,128)(2,1)S(1)}, u32[]{:S(2)}, u32[]{:S(2)}) async-start(bf16[32,32,128]{2,1,0:T(8,128)(2,1)} %first.1), calls=%async_computation.1 | async-start | bytes 524288 | tf_op jit(solution)/shard_map/all_to_all | solution.py:330
  55.5 150.8 %all-gather.9.cloned.1.call-start = ((), (), s32[]{:S(2)}) async-start(), calls=%async_computation.9 | async-start | bytes 7077888 | tf_op jit(solution)/shard_map/all_gather | solution.py:333
  102.3 110.2 %all-gather.11.cloned.1.call-start = ((), (), s32[]{:S(2)}) async-start(), calls=%async_computation.10 | async-start | bytes 7077888 | tf_op jit(solution)/shard_map/all_gather | solution.py:333
  172.8 39.7 %copy-start.4 = (bf16[32,32,128]{2,1,0:T(8,128)(2,1)}, bf16[32,32,128]{2,1,0:T(8,128)(2,1)S(1)}, u32[]{:S(2)}) copy-start(bf16[32,32,128]{2,1,0:T(8,128)(2,1)S(1)} %all_to_all.45.rest_9_) | copy-start | bytes 786436
  172.8 13.0 %collective-permute-start.6 = (bf16[32,32,128]{2,1,0:T(8,128)(2,1)S(1)}, bf16[32,32,128]{2,1,0:T(8,128)(2,1)S(1)}, u32[]{:S(2)}, u32[]{:S(2)}) collective-permute-start(bf16[32,32,128]{2,1,0:T(8,128)(2,1)S(1)} %all_to_all.45.rest_9_), channel_id=1, source_target_pairs={{192,224},{193,225},{194,226},{195,227},{196,228},{197,229},{198,2... | collective-permute-start | bytes 786440 | tf_op jit(solution)/shard_map/ppermute | solution.py:342
  174.1 13.1 %collective-permute-start.5 = (bf16[32,32,128]{2,1,0:T(8,128)(2,1)S(1)}, bf16[32,32,128]{2,1,0:T(8,128)(2,1)S(1)}, u32[]{:S(2)}, u32[]{:S(2)}) collective-permute-start(bf16[32,32,128]{2,1,0:T(8,128)(2,1)S(1)} %all_to_all.45.rest_9_), channel_id=1, source_target_pairs={{160,224},{161,225},{162,226},{163,227},{164,228},{165,229},{166,2... | collective-permute-start | bytes 786440 | tf_op jit(solution)/shard_map/ppermute | solution.py:342
  175.4 21.3 %collective-permute-start.4 = (bf16[32,32,128]{2,1,0:T(8,128)(2,1)S(1)}, bf16[32,32,128]{2,1,0:T(8,128)(2,1)S(1)}, u32[]{:S(2)}, u32[]{:S(2)}) collective-permute-start(bf16[32,32,128]{2,1,0:T(8,128)(2,1)S(1)} %all_to_all.45.rest_9_), channel_id=1, source_target_pairs={{128,224},{129,225},{130,226},{131,227},{132,228},{133,229},{134,2... | collective-permute-start | bytes 786440 | tf_op jit(solution)/shard_map/ppermute | solution.py:342
  176.7 20.0 %collective-permute-start.3 = (bf16[32,32,128]{2,1,0:T(8,128)(2,1)S(1)}, bf16[32,32,128]{2,1,0:T(8,128)(2,1)S(1)}, u32[]{:S(2)}, u32[]{:S(2)}) collective-permute-start(bf16[32,32,128]{2,1,0:T(8,128)(2,1)S(1)} %all_to_all.45.rest_9_), channel_id=1, source_target_pairs={{96,224},{97,225},{98,226},{99,227},{100,228},{101,229},{102,230},... | collective-permute-start | bytes 786440 | tf_op jit(solution)/shard_map/ppermute | solution.py:342
  178.0 21.1 %collective-permute-start.2 = (bf16[32,32,128]{2,1,0:T(8,128)(2,1)S(1)}, bf16[32,32,128]{2,1,0:T(8,128)(2,1)S(1)}, u32[]{:S(2)}, u32[]{:S(2)}) collective-permute-start(bf16[32,32,128]{2,1,0:T(8,128)(2,1)S(1)} %all_to_all.45.rest_9_), channel_id=1, source_target_pairs={{64,224},{65,225},{66,226},{67,227},{68,228},{69,229},{70,230},{71... | collective-permute-start | bytes 786440 | tf_op jit(solution)/shard_map/ppermute | solution.py:342
  185.8 26.7 %copy-start.5 = (bf16[32,32,128]{2,1,0:T(8,128)(2,1)}, bf16[32,32,128]{2,1,0:T(8,128)(2,1)S(1)}, u32[]{:S(2)}) copy-start(bf16[32,32,128]{2,1,0:T(8,128)(2,1)S(1)} %collective-permute-done.6.rest_8_) | copy-start | bytes 786436
  185.8 19.2 %collective-permute-start.1 = (bf16[32,32,128]{2,1,0:T(8,128)(2,1)S(1)}, bf16[32,32,128]{2,1,0:T(8,128)(2,1)S(1)}, u32[]{:S(2)}, u32[]{:S(2)}) collective-permute-start(bf16[32,32,128]{2,1,0:T(8,128)(2,1)S(1)} %all_to_all.45.rest_9_), channel_id=1, source_target_pairs={{32,224},{33,225},{34,226},{35,227},{36,228},{37,229},{38,230},{39... | collective-permute-start | bytes 786440 | tf_op jit(solution)/shard_map/ppermute | solution.py:342
  187.2 25.3 %copy-start.6 = (bf16[32,32,128]{2,1,0:T(8,128)(2,1)}, bf16[32,32,128]{2,1,0:T(8,128)(2,1)S(1)}, u32[]{:S(2)}) copy-start(bf16[32,32,128]{2,1,0:T(8,128)(2,1)S(1)} %collective-permute-done.5.rest_7_) | copy-start | bytes 786436
  187.2 19.2 %collective-permute-start = (bf16[32,32,128]{2,1,0:T(8,128)(2,1)S(1)}, bf16[32,32,128]{2,1,0:T(8,128)(2,1)}, u32[]{:S(2)}, u32[]{:S(2)}) collective-permute-start(bf16[32,32,128]{2,1,0:T(8,128)(2,1)S(1)} %all_to_all.45.rest_9_), channel_id=1, source_target_pairs={{0,224},{1,225},{2,226},{3,227},{4,228},{5,229},{6,230},{7,231},{8... | collective-permute-start | bytes 786440 | tf_op jit(solution)/shard_map/ppermute | solution.py:342
  196.6 15.8 %copy-start.7 = (bf16[32,32,128]{2,1,0:T(8,128)(2,1)}, bf16[32,32,128]{2,1,0:T(8,128)(2,1)S(1)}, u32[]{:S(2)}) copy-start(bf16[32,32,128]{2,1,0:T(8,128)(2,1)S(1)} %collective-permute-done.4.rest_6_) | copy-start | bytes 786436
  196.7 15.8 %copy-start.8 = (bf16[32,32,128]{2,1,0:T(8,128)(2,1)}, bf16[32,32,128]{2,1,0:T(8,128)(2,1)S(1)}, u32[]{:S(2)}) copy-start(bf16[32,32,128]{2,1,0:T(8,128)(2,1)S(1)} %collective-permute-done.3.rest_5_) | copy-start | bytes 786436
  199.0 6.0 %copy-start.9 = (bf16[32,32,128]{2,1,0:T(8,128)(2,1)}, bf16[32,32,128]{2,1,0:T(8,128)(2,1)S(1)}, u32[]{:S(2)}) copy-start(bf16[32,32,128]{2,1,0:T(8,128)(2,1)S(1)} %collective-permute-done.2.rest_4_) | copy-start | bytes 786436
  205.0 0.7 copy-start.10
Sparse Core Ops, SparseCore 0:
  21.7 38.6 all-gather.6
  102.4 42.0 all-gather.8
  155.5 56.9 all-gather.10

commit v4 on v2

--- a/solution.py
+++ b/solution.py
@@ -23,31 +23,73 @@
     return lax.broadcasted_iota(jnp.int32, shape, len(shape) - 1) < half
 
 
-def prepare_kernel(rhs_ref, inv_ref, below_ref, gain_ref, load_ref):
-    nodes = rhs_ref.shape[0]
-    levels, _, span, _ = load_ref.shape
-    for pair in range(nodes // 2):
-        halves = []
-        for node in (2 * pair, 2 * pair + 1):
-            inv, below = inv_ref[node], below_ref[node]
-            gain_ref[node] = dot(below, inv).astype(BF16)
-            solved = dot(inv, rhs_ref[node]).astype(BF16)
-            halves.append(dot(below, solved))
-        both = jnp.concatenate(halves, axis=0).T.astype(BF16)
-        load_ref[:, pair] = both.reshape(levels, span, both.shape[1])
-
-
-def operator_kernel(slot_ref, rows_ref, gain_ref, op_ref):
-    senders, rows, lanes = op_ref.shape
-    nodes, _, block = gain_ref.shape
+def prepare_kernel(
+    slot_ref,
+    rows_ref,
+    rhs_ref,
+    inv_ref,
+    below_ref,
+    op_ref,
+    load_ref,
+    rhs,
+    inv,
+    below,
+    gain,
+    op,
+    load,
+    ready,
+    done,
+):
+    nodes, rows, block = below.shape
+    levels, pairs, span, lanes = load.shape
+    senders = op.shape[0]
+    parts = ready.shape[1]
+    share = nodes // parts
+    spots = [pl.ds(p * share, share) for p in range(parts)]
+    coming = [
+        [
+            pltpu.make_async_copy(source.at[spot], target.at[spot], ready.at[i, p])
+            for p, spot in enumerate(spots)
+        ]
+        for i, (source, target) in enumerate(((inv_ref, inv), (below_ref, below), (rhs_ref, rhs)))
+    ]
+    for first, second in zip(coming[0], coming[1]):
+        first.start()
+        second.start()
+    for copy in coming[2]:
+        copy.start()
+    going = [pltpu.make_async_copy(op, op_ref, done.at[0])]
+    for p in range(parts):
+        spot = pl.ds(p * share // 2, share // 2)
+        going.append(
+            pltpu.make_async_copy(load.at[:, spot], load_ref.at[:, spot], done.at[1 + p])
+        )
+
+    for p in range(parts):
+        coming[0][p].wait()
+        coming[1][p].wait()
+        for node in range(p * share, (p + 1) * share):
+            gain[node] = dot(below[node], inv[node]).astype(BF16)
     low = low_lanes((rows, lanes), rows)
     for s in range(senders):
         hot = (
             lax.broadcasted_iota(jnp.int32, (block, lanes), 0) == rows_ref[s : s + 1, :]
         ).astype(BF16)
-        first = dot(gain_ref[jnp.minimum(slot_ref[2 * s], nodes - 1)], hot)
-        second = dot(gain_ref[jnp.minimum(slot_ref[2 * s + 1], nodes - 1)], hot)
-        op_ref[s] = jnp.where(low, first, second).astype(BF16)
+        one = dot(gain[jnp.minimum(slot_ref[2 * s], nodes - 1)], hot)
+        two = dot(gain[jnp.minimum(slot_ref[2 * s + 1], nodes - 1)], hot)
+        op[s] = jnp.where(low, one, two).astype(BF16)
+    going[0].start()
+    for p in range(parts):
+        coming[2][p].wait()
+        mine = range(p * share, (p + 1) * share)
+        solved = [dot(inv[node], rhs[node]).astype(BF16) for node in mine]
+        updates = [dot(below[node], value) for node, value in zip(mine, solved)]
+        for i in range(0, share, 2):
+            both = jnp.concatenate(updates[i : i + 2], axis=0).T.astype(BF16)
+            load[:, (p * share + i) // 2] = both.reshape(levels, span, lanes)
+        going[1 + p].start()
+    for copy in going:
+        copy.wait()
 
 
 def pack(values, take_ref, level, send_ref):
@@ -80,48 +122,49 @@
     take_ref,
     slot_ref,
     got_ref,
-    op_ref,
-    load_ref,
+    all_op_ref,
+    all_load_ref,
     send_ref,
-    got,
     ops,
     load,
     total,
     values,
     ready,
+    loaded,
 ):
-    senders, span, lanes = got.shape
+    senders, span, lanes = got_ref.shape
     pairs = load.shape[0]
     half = lanes // 2
-    parts = ready.shape[1]
+    parts = ready.shape[0]
     share = senders // parts
-    copies = []
-    for i in range(parts):
-        where = pl.ds(i * share, share)
-        copies.append(
-            (
-                pltpu.make_async_copy(got_ref.at[where], got.at[where], ready.at[0, i]),
-                pltpu.make_async_copy(op_ref.at[level, where], ops.at[where], ready.at[1, i]),
-            )
+    copies = [
+        pltpu.make_async_copy(
+            all_op_ref.at[level, pl.ds(i * share, share)],
+            ops.at[pl.ds(i * share, share)],
+            ready.at[i],
         )
-    loading = pltpu.make_async_copy(load_ref.at[level], load, ready.at[2, 0])
-    for pair in copies:
-        for copy in pair:
-            copy.start()
+        for i in range(parts)
+    ]
+    for copy in copies:
+        copy.start()
+    loading = pltpu.make_async_copy(all_load_ref.at[level], load, loaded.at[0])
     loading.start()
     low = low_lanes((span, lanes), half)
     low_op = low_lanes((half, lanes), half)
     total[...] = jnp.zeros_like(total)
     for s in range(senders):
-        if s % share == 0:
-            for copy in copies[s // share]:
+        if s == 0:
+            for copy in copies[: parts // 2]:
+                copy.wait()
+        elif s == senders // 2:
+            for copy in copies[parts // 2 :]:
                 copy.wait()
         op = ops[s]
         zero = jnp.zeros_like(op)
         split = jnp.concatenate(
             [jnp.where(low_op, op, zero), jnp.where(low_op, zero, op)], axis=0
         )
-        part = dot_nt(got[s], split)
+        part = dot_nt(got_ref[s], split)
         one = slot_ref[level - 1, 2 * s]
         two = slot_ref[level - 1, 2 * s + 1]
         total[one] += jnp.where(low, part, 0.0)
@@ -251,27 +294,6 @@
     pairs = nodes // 2
     hops = levels - 1
 
-    step = 4
-    gain, load = pl.pallas_call(
-        prepare_kernel,
-        grid=(nodes // step,),
-        in_specs=[
-            pl.BlockSpec((step, block, columns), lambda i: (i, 0, 0)),
-            pl.BlockSpec((step, block, block), lambda i: (i, 0, 0)),
-            pl.BlockSpec((step, rows, block), lambda i: (i, 0, 0)),
-        ],
-        out_specs=[
-            pl.BlockSpec((step, rows, block), lambda i: (i, 0, 0)),
-            pl.BlockSpec((levels, step // 2, span, lanes), lambda i: (0, i, 0, 0)),
-        ],
-        out_shape=[
-            jax.ShapeDtypeStruct((nodes, rows, block), BF16),
-            jax.ShapeDtypeStruct((levels, pairs, span, lanes), BF16),
-        ],
-        compiler_params=params(60, "arbitrary"),
-        name="prepare",
-    )(right_side[0], diag_inverse[0], below_block[0])
-
     devices = parent_device[:hops, :, 0].reshape(hops, group, nodes)
     slots = parent_slot[:hops].reshape(hops, group, nodes)
     place = lax.broadcasted_iota(jnp.int32, (hops, group, nodes), 2)
@@ -307,21 +329,35 @@
 
     home_rows = jnp.concatenate([rows_of(first), rows_of(last)], axis=0).T
 
-    operators = pl.pallas_call(
-        operator_kernel,
-        in_specs=[SMEM_SPEC, VMEM_SPEC, VMEM_SPEC],
-        out_specs=VMEM_SPEC,
-        out_shape=jax.ShapeDtypeStruct((group, rows, lanes), BF16),
-        compiler_params=params(16),
-        name="operators",
-    )(home_slot, home_rows, gain)
+    parts = 4
+    operators, load = pl.pallas_call(
+        prepare_kernel,
+        in_specs=[SMEM_SPEC, VMEM_SPEC, HBM_SPEC, HBM_SPEC, HBM_SPEC],
+        out_specs=[HBM_SPEC, HBM_SPEC],
+        out_shape=[
+            jax.ShapeDtypeStruct((group, rows, lanes), BF16),
+            jax.ShapeDtypeStruct((levels, pairs, span, lanes), BF16),
+        ],
+        scratch_shapes=[
+            pltpu.VMEM((nodes, block, columns), BF16),
+            pltpu.VMEM((nodes, block, block), BF16),
+            pltpu.VMEM((nodes, rows, block), BF16),
+            pltpu.VMEM((nodes, rows, block), BF16),
+            pltpu.VMEM((group, rows, lanes), BF16),
+            pltpu.VMEM((levels, pairs, span, lanes), BF16),
+            pltpu.SemaphoreType.DMA((3, parts)),
+            pltpu.SemaphoreType.DMA((1 + parts,)),
+        ],
+        compiler_params=params(58),
+        name="prepare",
+    )(home_slot, home_rows, right_side[0], diag_inverse[0], below_block[0])
     operators = lax.all_gather(operators, "level", axis=0)
     loads = lax.all_to_all(load, "level", split_axis=0, concat_axis=0, tiled=True)
 
     message = jax.ShapeDtypeStruct((group, span, lanes), BF16)
     values_shape = pltpu.VMEM((nodes + 1, span, lanes), BF16)
     arrived = [None]
-    early_counts = (hops // 2, hops - 2 - hops // 2)
+    early_counts = (hops // 2, hops - 1 - hops // 2)
     early = []
     for level in range(hops):
         if level == 0:
@@ -337,16 +373,16 @@
         else:
             send = pl.pallas_call(
                 functools.partial(hop_kernel, level),
-                in_specs=[SMEM_SPEC, SMEM_SPEC, HBM_SPEC, HBM_SPEC, HBM_SPEC],
+                in_specs=[SMEM_SPEC, SMEM_SPEC, VMEM_SPEC, HBM_SPEC, HBM_SPEC],
                 out_specs=VMEM_SPEC,
                 out_shape=message,
                 scratch_shapes=[
-                    pltpu.VMEM((group, span, lanes), BF16),
                     pltpu.VMEM((group, rows, lanes), BF16),
                     pltpu.VMEM((pairs, span, lanes), BF16),
                     pltpu.VMEM((nodes + 1, span, lanes), F32),
                     values_shape,
-                    pltpu.SemaphoreType.DMA((3, 4)),
+                    pltpu.SemaphoreType.DMA((8,)),
+                    pltpu.SemaphoreType.DMA((1,)),
                 ],
                 compiler_params=params(53),
                 name="hop",
@@ -368,7 +404,6 @@
         ]
 
     step = 8
-    parts = 4
     tail = lambda i: jnp.maximum(i - 1, 0)
     return pl.pallas_call(
         functools.partial(finish_kernel, early_counts),
@@ -392,7 +427,7 @@
             pltpu.SemaphoreType.DMA((3,)),
             pltpu.SemaphoreType.DMA((levels, parts)),
         ],
-        compiler_params=params(50, "arbitrary"),
+        compiler_params=params(58, "arbitrary"),
         name="finish",
     )(
         level_id.reshape(1),

time: 226 us -> 220 us (0.973)
  starting transfers between devices: 45.6 us -> 26 us
  blocking collectives: 73 us -> 86.9 us
  waiting for transfers between devices: 44.1 us -> 52 us
  Pallas kernels: 37.1 us -> 31.4 us
  local copies, waits for them, and re-layouts: 7.52 us -> 3.91 us
    ppermute x14 -> x7, starting transfers between devices: 24 us -> 9.01 us  [shards(): lax.ppermute(arrived[level], 'level', [(c, level)])]
    all_to_all x5 -> x6, blocking collectives: 73 us -> 86.9 us  [shards(): lax.all_to_all(send, 'grp', split_axis=0, concat_axis=0, tiled=True)]
    all_gather x2, waiting for transfers between devices: 0.02 us -> 5.07 us  [shards(): early.append(lax.all_gather(ready, 'level', axis=0))]
    all_to_all x2 -> x1, starting transfers between devices: 15.7 us -> 11.1 us  [shards(): lax.all_to_all(send, 'grp', split_axis=0, concat_axis=0, tiled=True)]
    unnamed x18 -> x22, local copies, waits for them, and re-layouts: 5.25 us -> 1.64 us
    pallas_call x2 -> x1, Pallas kernels: 9.57 us -> 6.25 us  [shards(): pl.pallas_call(prepare_kernel, in_specs=[SMEM_SPEC, VMEM_SPEC, HBM_SPEC,...]
    ppermute x14 -> x7, waiting for transfers between devices: 20.2 us -> 23.1 us  [shards(): lax.ppermute(arrived[level], 'level', [(c, level)])]
    pallas_call x6, Pallas kernels: 19.7 us -> 17 us  [shards(): pl.pallas_call(functools.partial(hop_kernel, level), in_specs=[SMEM_SPEC,...]
  transfers between devices with their start and end apart: 20 -> 12, of which waited for: 7 -> 9; matrix products, arithmetic and copies ran while one was open for 1% -> 1% of each run, Pallas kernels for 6% -> 6%
where the time goes in v4:
time: 220 us; the launch traced here: 219 us
  blocking collectives  86.9 us (40%)
  waiting for transfers between devices  52 us (24%)
  Pallas kernels  31.4 us (14%)
  starting transfers between devices  26 us (12%)
  between operations  14 us (6%)
  other arithmetic  4.87 us (2%)
  local copies, waits for them, and re-layouts  3.91 us (2%)
    all_to_all x6, blocking collectives, shards(): lax.all_to_all(send, 'grp', split_axis=0, concat_axis=0, tiled=True)  86.9 us
    ppermute x7, waiting for transfers between devices, shards(): lax.ppermute(arrived[level], 'level', [(c, level)])  23.1 us
    pallas_call x6, Pallas kernels, shards(): pl.pallas_call(functools.partial(hop_kernel, level), in_specs=[SMEM_SPEC,...  17 us
    all_to_all x1, waiting for transfers between devices, shards(): lax.all_to_all(load, 'level', split_axis=0, concat_axis=0, tiled=True)  13.6 us
    all_to_all x1, starting transfers between devices, shards(): lax.all_to_all(send, 'grp', split_axis=0, concat_axis=0, tiled=True)  11.1 us
    all_to_all x1, waiting for transfers between devices, shards(): lax.all_to_all(send, 'grp', split_axis=0, concat_axis=0, tiled=True)  10.3 us
    ppermute x7, starting transfers between devices, shards(): lax.ppermute(arrived[level], 'level', [(c, level)])  9.01 us
    pallas_call x1, Pallas kernels, shards(): pl.pallas_call(functools.partial(finish_kernel, early_counts), grid=(1 +...  7.29 us
  transfers between devices with their start and end apart: 12, of which 9 were waited for; matrix products, arithmetic and copies ran while one was open for 1% of the time, Pallas kernels for 6%

profile of v4, /device:TPU:25, one launch (start us, length us, event | category | flops | bytes accessed | tf_op | source)
XLA Modules:
  0.0 219.1 jit_solution(4623662410496167549)
XLA Ops:
  7.2 0.9 slice_reduce_fusion
  8.3 0.3 select_reduce_fusion.7
  8.6 0.8 reshape.109
  9.5 0.4 select_reduce_fusion.6
  9.9 0.1 copy.62
  10.1 0.2 copy.79
  10.3 0.8 select_reduce_fusion.8.slot_ref
  11.0 0.3 select_reduce_fusion.1
  11.5 0.7 add_bitcast_fusion.rows_ref
  12.1 6.2 %prepare.1 = (bf16[32,64,128]{2,1,0:T(8,128)(2,1)}, bf16[8,16,32,128]{3,2,1,0:T(8,128)(2,1)}) custom-call(s32[64]{0:T(128)} %select_reduce_fusion.8.slot_ref, s32[32,128]{1,0:T(8,128)} %add_bitcast_fusion.rows_ref, bf16[32,128,256]{2,1,0:T(8,128)(2,1)} %bitcast.61, bf16[32,128,128]{2,1,0:T(8,128)(2,1)} %bitcast.65, bf16[32,64,128]{2,1,0:T(8,128)(2,1)} %bitcast.67), custom_call_target="tpu_custom_call" | custom-call | tf_op jit(solution)/shard_map/prepare/pallas_call | solution.py:333
  18.4 5.8 %all-to-all-start = ((bf16[8,16,32,128]{3,2,1,0:T(8,128)(2,1)}), bf16[8,16,32,128]{3,2,1,0:T(8,128)(2,1)S(1)}, u32[]{:S(2)}, u32[]{:S(2)}) async-start(bf16[8,16,32,128]{3,2,1,0:T(8,128)(2,1)} %get-tuple-element.4), calls=%async_computation | async-start | bytes 2097152 | tf_op jit(solution)/shard_map/all_to_all | solution.py:355
  24.2 0.3 select_reduce_fusion.3
  24.6 0.1 copy.64
  24.7 13.6 %all-to-all-done.load_ref.all_load_ref = bf16[8,16,32,128]{3,2,1,0:T(8,128)(2,1)S(1)} async-done(((bf16[8,16,32,128]{3,2,1,0:T(8,128)(2,1)}), bf16[8,16,32,128]{3,2,1,0:T(8,128)(2,1)S(1)}, u32[]{:S(2)}, u32[]{:S(2)}) %all-to-all-start) | async-done | bytes 1048608 | tf_op jit(solution)/shard_map/all_to_all | solution.py:355
  38.3 0.8 first.1
  39.1 0.7 copy-done.2
  39.8 11.1 %all-to-all-start.1 = ((bf16[32,32,128]{2,1,0:T(8,128)(2,1)}), bf16[32,32,128]{2,1,0:T(8,128)(2,1)S(1)}, u32[]{:S(2)}, u32[]{:S(2)}) async-start(bf16[32,32,128]{2,1,0:T(8,128)(2,1)} %copy-done.2), calls=%async_computation.1 | async-start | bytes 524288 | tf_op jit(solution)/shard_map/all_to_all | solution.py:390
  51.0 10.3 %all-to-all-done.1.got_ref = bf16[32,32,128]{2,1,0:T(8,128)(2,1)S(1)} async-done(((bf16[32,32,128]{2,1,0:T(8,128)(2,1)}), bf16[32,32,128]{2,1,0:T(8,128)(2,1)S(1)}, u32[]{:S(2)}, u32[]{:S(2)}) %all-to-all-start.1) | async-done | bytes 262176 | tf_op jit(solution)/shard_map/all_to_all | solution.py:390
  61.3 2.8 %hop.6 = bf16[32,32,128]{2,1,0:T(8,128)(2,1)S(1)} custom-call(s32[7,64]{1,0:T(8,128)S(1)} %copy.65.take_ref, s32[7,64]{1,0:T(8,128)S(1)} %copy.67.slot_ref, bf16[32,32,128]{2,1,0:T(8,128)(2,1)S(1)} %all-to-all-done.1.got_ref, bf16[8,32,64,128]{3,2,1,0:T(8,128)(2,1)} %bitcast.55, bf16[8,16,32,128]{3,2,1,0:T(8,128)(2,1)} %copy-done.1), custom_call_target="tpu_custom_call" | custom-call | tf_op jit(solution)/shard_map/hop/pallas_call | solution.py:374
  64.1 15.8 %all_to_all.40.got_ref = bf16[32,32,128]{2,1,0:T(8,128)(2,1)S(1)} all-to-all(bf16[32,32,128]{2,1,0:T(8,128)(2,1)S(1)} %hop.6), channel_id=1, replica_groups=mesh['level'=8,'grp'=32] {'grp'}, dimensions={0} | all-to-all | bytes 524288 | tf_op jit(solution)/shard_map/all_to_all | solution.py:390
  79.9 2.8 %hop.7 = bf16[32,32,128]{2,1,0:T(8,128)(2,1)S(1)} custom-call(s32[7,64]{1,0:T(8,128)S(1)} %copy.65.take_ref, s32[7,64]{1,0:T(8,128)S(1)} %copy.67.slot_ref, bf16[32,32,128]{2,1,0:T(8,128)(2,1)S(1)} %all_to_all.40.got_ref, bf16[8,32,64,128]{3,2,1,0:T(8,128)(2,1)} %bitcast.56, bf16[8,16,32,128]{3,2,1,0:T(8,128)(2,1)} %copy-done.1), custom_call_target="tpu_custom_call" | custom-call | tf_op jit(solution)/shard_map/hop/pallas_call | solution.py:374
  82.8 15.1 %all_to_all.41.got_ref = bf16[32,32,128]{2,1,0:T(8,128)(2,1)S(1)} all-to-all(bf16[32,32,128]{2,1,0:T(8,128)(2,1)S(1)} %hop.7), channel_id=1, replica_groups=mesh['level'=8,'grp'=32] {'grp'}, dimensions={0} | all-to-all | bytes 524288 | tf_op jit(solution)/shard_map/all_to_all | solution.py:390
  97.9 1.0 pad_maximum_fusion
  98.9 2.8 %hop.8 = bf16[32,32,128]{2,1,0:T(8,128)(2,1)S(1)} custom-call(s32[7,64]{1,0:T(8,128)S(1)} %copy.65.take_ref, s32[7,64]{1,0:T(8,128)S(1)} %copy.67.slot_ref, bf16[32,32,128]{2,1,0:T(8,128)(2,1)S(1)} %all_to_all.41.got_ref, bf16[8,32,64,128]{3,2,1,0:T(8,128)(2,1)} %bitcast.57, bf16[8,16,32,128]{3,2,1,0:T(8,128)(2,1)} %copy-done.1), custom_call_target="tpu_custom_call" | custom-call | tf_op jit(solution)/shard_map/hop/pallas_call | solution.py:374
  101.8 14.0 %all_to_all.42.got_ref = bf16[32,32,128]{2,1,0:T(8,128)(2,1)S(1)} all-to-all(bf16[32,32,128]{2,1,0:T(8,128)(2,1)S(1)} %hop.8), channel_id=1, replica_groups=mesh['level'=8,'grp'=32] {'grp'}, dimensions={0} | all-to-all | bytes 524288 | tf_op jit(solution)/shard_map/all_to_all | solution.py:390
  115.8 2.9 %hop.9 = bf16[32,32,128]{2,1,0:T(8,128)(2,1)S(1)} custom-call(s32[7,64]{1,0:T(8,128)S(1)} %copy.65.take_ref, s32[7,64]{1,0:T(8,128)S(1)} %copy.67.slot_ref, bf16[32,32,128]{2,1,0:T(8,128)(2,1)S(1)} %all_to_all.42.got_ref, bf16[8,32,64,128]{3,2,1,0:T(8,128)(2,1)} %bitcast.58, bf16[8,16,32,128]{3,2,1,0:T(8,128)(2,1)} %copy-done.1), custom_call_target="tpu_custom_call" | custom-call | tf_op jit(solution)/shard_map/hop/pallas_call | solution.py:374
  118.7 14.1 %all_to_all.43.got_ref = bf16[32,32,128]{2,1,0:T(8,128)(2,1)S(1)} all-to-all(bf16[32,32,128]{2,1,0:T(8,128)(2,1)S(1)} %hop.9), channel_id=1, replica_groups=mesh['level'=8,'grp'=32] {'grp'}, dimensions={0} | all-to-all | bytes 524288 | tf_op jit(solution)/shard_map/all_to_all | solution.py:390
  132.8 2.8 %hop.10 = bf16[32,32,128]{2,1,0:T(8,128)(2,1)S(1)} custom-call(s32[7,64]{1,0:T(8,128)S(1)} %copy.65.take_ref, s32[7,64]{1,0:T(8,128)S(1)} %copy.67.slot_ref, bf16[32,32,128]{2,1,0:T(8,128)(2,1)S(1)} %all_to_all.43.got_ref, bf16[8,32,64,128]{3,2,1,0:T(8,128)(2,1)} %bitcast.59, bf16[8,16,32,128]{3,2,1,0:T(8,128)(2,1)} %copy-done.1), custom_call_target="tpu_custom_call" | custom-call | tf_op jit(solution)/shard_map/hop/pallas_call | solution.py:374
  135.6 14.0 %all_to_all.44.got_ref = bf16[32,32,128]{2,1,0:T(8,128)(2,1)S(1)} all-to-all(bf16[32,32,128]{2,1,0:T(8,128)(2,1)S(1)} %hop.10), channel_id=1, replica_groups=mesh['level'=8,'grp'=32] {'grp'}, dimensions={0} | all-to-all | bytes 524288 | tf_op jit(solution)/shard_map/all_to_all | solution.py:390
  149.6 1.0 pad_maximum_fusion.1
  150.6 2.8 %hop.11 = bf16[32,32,128]{2,1,0:T(8,128)(2,1)S(1)} custom-call(s32[7,64]{1,0:T(8,128)S(1)} %copy.65.take_ref, s32[7,64]{1,0:T(8,128)S(1)} %copy.67.slot_ref, bf16[32,32,128]{2,1,0:T(8,128)(2,1)S(1)} %all_to_all.44.got_ref, bf16[8,32,64,128]{3,2,1,0:T(8,128)(2,1)} %bitcast.60, bf16[8,16,32,128]{3,2,1,0:T(8,128)(2,1)} %copy-done.1), custom_call_target="tpu_custom_call" | custom-call | tf_op jit(solution)/shard_map/hop/pallas_call | solution.py:374
  153.4 13.9 %all_to_all.45.rest_9_ = bf16[32,32,128]{2,1,0:T(8,128)(2,1)S(1)} all-to-all(bf16[32,32,128]{2,1,0:T(8,128)(2,1)S(1)} %hop.11), channel_id=1, replica_groups=mesh['level'=8,'grp'=32] {'grp'}, dimensions={0} | all-to-all | bytes 524288 | tf_op jit(solution)/shard_map/all_to_all | solution.py:390
  167.3 1.3 collective-permute-start.6
  168.6 1.3 collective-permute-start.5
  169.9 1.3 collective-permute-start.4
  171.2 1.3 collective-permute-start.3
  172.5 1.3 collective-permute-start.2
  173.8 4.0 %collective-permute-done.6.rest_8_ = bf16[32,32,128]{2,1,0:T(8,128)(2,1)S(1)} collective-permute-done((bf16[32,32,128]{2,1,0:T(8,128)(2,1)S(1)}, bf16[32,32,128]{2,1,0:T(8,128)(2,1)S(1)}, u32[]{:S(2)}, u32[]{:S(2)}) %collective-permute-start.6) | collective-permute-done | bytes 262176 | tf_op jit(solution)/shard_map/ppermute | solution.py:402
  177.8 1.3 collective-permute-start.1
  179.1 3.1 %collective-permute-done.5.rest_7_ = bf16[32,32,128]{2,1,0:T(8,128)(2,1)S(1)} collective-permute-done((bf16[32,32,128]{2,1,0:T(8,128)(2,1)S(1)}, bf16[32,32,128]{2,1,0:T(8,128)(2,1)S(1)}, u32[]{:S(2)}, u32[]{:S(2)}) %collective-permute-start.5) | collective-permute-done | bytes 262176 | tf_op jit(solution)/shard_map/ppermute | solution.py:402
  182.2 1.3 collective-permute-start
  183.5 5.6 %collective-permute-done.4.rest_6_ = bf16[32,32,128]{2,1,0:T(8,128)(2,1)S(1)} collective-permute-done((bf16[32,32,128]{2,1,0:T(8,128)(2,1)S(1)}, bf16[32,32,128]{2,1,0:T(8,128)(2,1)S(1)}, u32[]{:S(2)}, u32[]{:S(2)}) %collective-permute-start.4) | collective-permute-done | bytes 262176 | tf_op jit(solution)/shard_map/ppermute | solution.py:402
  189.1 2.9 %collective-permute-done.2.rest_4_ = bf16[32,32,128]{2,1,0:T(8,128)(2,1)S(1)} collective-permute-done((bf16[32,32,128]{2,1,0:T(8,128)(2,1)S(1)}, bf16[32,32,128]{2,1,0:T(8,128)(2,1)S(1)}, u32[]{:S(2)}, u32[]{:S(2)}) %collective-permute-start.2) | collective-permute-done | bytes 262176 | tf_op jit(solution)/shard_map/ppermute | solution.py:402
  192.0 5.4 %collective-permute-done.1.rest_3_ = bf16[32,32,128]{2,1,0:T(8,128)(2,1)S(1)} collective-permute-done((bf16[32,32,128]{2,1,0:T(8,128)(2,1)S(1)}, bf16[32,32,128]{2,1,0:T(8,128)(2,1)S(1)}, u32[]{:S(2)}, u32[]{:S(2)}) %collective-permute-start.1) | collective-permute-done | bytes 262176 | tf_op jit(solution)/shard_map/ppermute | solution.py:402
  197.4 0.7 copy-done.9
  198.1 2.1 collective-permute-done.rest_2_
  200.2 5.1 %all-gather.11.cloned.1.call-done = bf16[24,32,32,128]{3,2,1,0:T(8,128)(2,1)} async-done(((bf16[3,32,32,128]{3,2,1,0:T(8,128)(2,1)}), bf16[24,32,32,128]{3,2,1,0:T(8,128)(2,1)}) %all-gather.11.cloned.1.call-update) | async-done | bytes 6291472 | tf_op jit(solution)/shard_map/all_gather | solution.py:393
  205.3 7.3 %finish.1 = (bf16[1,32,128,256]{3,2,1,0:T(8,128)(2,1)}, bf16[1,32,64,256]{3,2,1,0:T(8,128)(2,1)}) custom-call(s32[1]{0:T(128)} %bitcast.level_ref, s32[64]{0:T(128)} %select_reduce_fusion.8.slot_ref, s32[32,128]{1,0:T(8,128)} %add_bitcast_fusion.rows_ref, bf16[32,128,256]{2,1,0:T(8,128)(2,1)} %bitcast.62, bf16[32,128,128]{2,1,0:T(8,128)(2,1)} %bitcast.66, ...), custom_call_target="tpu_custom_call" | custom-call | tf_op jit(solution)/shard_map/finish/pallas_call | solution.py:408
  (42 shorter events, 0.7 us)
Async XLA Ops:
  7.2 2.9 %copy-start = (s32[8,64,1024]{2,1,0:T(8,128)S(1)}, s32[8,64,1024]{2,1,0:T(8,128)}, u32[]{:S(2)}) copy-start(s32[8,64,1024]{2,1,0:T(8,128)} %param.11) | copy-start | bytes 6291460
  7.2 54.1 %all-gather.7.cloned.1.call-start = ((), (), s32[]{:S(2)}) async-start(), calls=%async_computation.8 | async-start | bytes 4718592 | tf_op jit(solution)/shard_map/all_gather | solution.py:354
  18.4 19.9 %all-to-all-start = ((bf16[8,16,32,128]{3,2,1,0:T(8,128)(2,1)}), bf16[8,16,32,128]{3,2,1,0:T(8,128)(2,1)S(1)}, u32[]{:S(2)}, u32[]{:S(2)}) async-start(bf16[8,16,32,128]{3,2,1,0:T(8,128)(2,1)} %get-tuple-element.4), calls=%async_computation | async-start | bytes 2097152 | tf_op jit(solution)/shard_map/all_to_all | solution.py:355
  38.3 23.0 %copy-start.1 = (bf16[8,16,32,128]{3,2,1,0:T(8,128)(2,1)}, bf16[8,16,32,128]{3,2,1,0:T(8,128)(2,1)S(1)}, u32[]{:S(2)}) copy-start(bf16[8,16,32,128]{3,2,1,0:T(8,128)(2,1)S(1)} %all-to-all-done.load_ref.all_load_ref) | copy-start | bytes 3145732
  39.1 0.7 copy-start.2
  39.8 21.5 %all-to-all-start.1 = ((bf16[32,32,128]{2,1,0:T(8,128)(2,1)}), bf16[32,32,128]{2,1,0:T(8,128)(2,1)S(1)}, u32[]{:S(2)}, u32[]{:S(2)}) async-start(bf16[32,32,128]{2,1,0:T(8,128)(2,1)} %copy-done.2), calls=%async_computation.1 | async-start | bytes 524288 | tf_op jit(solution)/shard_map/all_to_all | solution.py:390
  50.9 149.3 %all-gather.9.cloned.1.call-start = ((), (), s32[]{:S(2)}) async-start(), calls=%async_computation.9 | async-start | bytes 7077888 | tf_op jit(solution)/shard_map/all_gather | solution.py:393
  98.9 106.4 %all-gather.11.cloned.1.call-start = ((), (), s32[]{:S(2)}) async-start(), calls=%async_computation.10 | async-start | bytes 7077888 | tf_op jit(solution)/shard_map/all_gather | solution.py:393
  167.3 37.9 %copy-start.3 = (bf16[32,32,128]{2,1,0:T(8,128)(2,1)}, bf16[32,32,128]{2,1,0:T(8,128)(2,1)S(1)}, u32[]{:S(2)}) copy-start(bf16[32,32,128]{2,1,0:T(8,128)(2,1)S(1)} %all_to_all.45.rest_9_) | copy-start | bytes 786436
  167.3 10.5 %collective-permute-start.6 = (bf16[32,32,128]{2,1,0:T(8,128)(2,1)S(1)}, bf16[32,32,128]{2,1,0:T(8,128)(2,1)S(1)}, u32[]{:S(2)}, u32[]{:S(2)}) collective-permute-start(bf16[32,32,128]{2,1,0:T(8,128)(2,1)S(1)} %all_to_all.45.rest_9_), channel_id=1, source_target_pairs={{192,224},{193,225},{194,226},{195,227},{196,228},{197,229},{198,2... | collective-permute-start | bytes 786440 | tf_op jit(solution)/shard_map/ppermute | solution.py:402
  168.6 13.6 %collective-permute-start.5 = (bf16[32,32,128]{2,1,0:T(8,128)(2,1)S(1)}, bf16[32,32,128]{2,1,0:T(8,128)(2,1)S(1)}, u32[]{:S(2)}, u32[]{:S(2)}) collective-permute-start(bf16[32,32,128]{2,1,0:T(8,128)(2,1)S(1)} %all_to_all.45.rest_9_), channel_id=1, source_target_pairs={{160,224},{161,225},{162,226},{163,227},{164,228},{165,229},{166,2... | collective-permute-start | bytes 786440 | tf_op jit(solution)/shard_map/ppermute | solution.py:402
  169.9 19.2 %collective-permute-start.4 = (bf16[32,32,128]{2,1,0:T(8,128)(2,1)S(1)}, bf16[32,32,128]{2,1,0:T(8,128)(2,1)S(1)}, u32[]{:S(2)}, u32[]{:S(2)}) collective-permute-start(bf16[32,32,128]{2,1,0:T(8,128)(2,1)S(1)} %all_to_all.45.rest_9_), channel_id=1, source_target_pairs={{128,224},{129,225},{130,226},{131,227},{132,228},{133,229},{134,2... | collective-permute-start | bytes 786440 | tf_op jit(solution)/shard_map/ppermute | solution.py:402
  171.2 17.9 %collective-permute-start.3 = (bf16[32,32,128]{2,1,0:T(8,128)(2,1)S(1)}, bf16[32,32,128]{2,1,0:T(8,128)(2,1)S(1)}, u32[]{:S(2)}, u32[]{:S(2)}) collective-permute-start(bf16[32,32,128]{2,1,0:T(8,128)(2,1)S(1)} %all_to_all.45.rest_9_), channel_id=1, source_target_pairs={{96,224},{97,225},{98,226},{99,227},{100,228},{101,229},{102,230},... | collective-permute-start | bytes 786440 | tf_op jit(solution)/shard_map/ppermute | solution.py:402
  172.5 19.5 %collective-permute-start.2 = (bf16[32,32,128]{2,1,0:T(8,128)(2,1)S(1)}, bf16[32,32,128]{2,1,0:T(8,128)(2,1)S(1)}, u32[]{:S(2)}, u32[]{:S(2)}) collective-permute-start(bf16[32,32,128]{2,1,0:T(8,128)(2,1)S(1)} %all_to_all.45.rest_9_), channel_id=1, source_target_pairs={{64,224},{65,225},{66,226},{67,227},{68,228},{69,229},{70,230},{71... | collective-permute-start | bytes 786440 | tf_op jit(solution)/shard_map/ppermute | solution.py:402
  177.8 27.4 %copy-start.4 = (bf16[32,32,128]{2,1,0:T(8,128)(2,1)}, bf16[32,32,128]{2,1,0:T(8,128)(2,1)S(1)}, u32[]{:S(2)}) copy-start(bf16[32,32,128]{2,1,0:T(8,128)(2,1)S(1)} %collective-permute-done.6.rest_8_) | copy-start | bytes 786436
  177.8 19.6 %collective-permute-start.1 = (bf16[32,32,128]{2,1,0:T(8,128)(2,1)S(1)}, bf16[32,32,128]{2,1,0:T(8,128)(2,1)S(1)}, u32[]{:S(2)}, u32[]{:S(2)}) collective-permute-start(bf16[32,32,128]{2,1,0:T(8,128)(2,1)S(1)} %all_to_all.45.rest_9_), channel_id=1, source_target_pairs={{32,224},{33,225},{34,226},{35,227},{36,228},{37,229},{38,230},{39... | collective-permute-start | bytes 786440 | tf_op jit(solution)/shard_map/ppermute | solution.py:402
  182.2 23.0 %copy-start.5 = (bf16[32,32,128]{2,1,0:T(8,128)(2,1)}, bf16[32,32,128]{2,1,0:T(8,128)(2,1)S(1)}, u32[]{:S(2)}) copy-start(bf16[32,32,128]{2,1,0:T(8,128)(2,1)S(1)} %collective-permute-done.5.rest_7_) | copy-start | bytes 786436
  182.2 18.0 %collective-permute-start = (bf16[32,32,128]{2,1,0:T(8,128)(2,1)S(1)}, bf16[32,32,128]{2,1,0:T(8,128)(2,1)}, u32[]{:S(2)}, u32[]{:S(2)}) collective-permute-start(bf16[32,32,128]{2,1,0:T(8,128)(2,1)S(1)} %all_to_all.45.rest_9_), channel_id=1, source_target_pairs={{0,224},{1,225},{2,226},{3,227},{4,228},{5,229},{6,230},{7,231},{8... | collective-permute-start | bytes 786440 | tf_op jit(solution)/shard_map/ppermute | solution.py:402
  189.1 16.1 %copy-start.6 = (bf16[32,32,128]{2,1,0:T(8,128)(2,1)}, bf16[32,32,128]{2,1,0:T(8,128)(2,1)S(1)}, u32[]{:S(2)}) copy-start(bf16[32,32,128]{2,1,0:T(8,128)(2,1)S(1)} %collective-permute-done.4.rest_6_) | copy-start | bytes 786436
  189.1 16.1 %copy-start.7 = (bf16[32,32,128]{2,1,0:T(8,128)(2,1)}, bf16[32,32,128]{2,1,0:T(8,128)(2,1)S(1)}, u32[]{:S(2)}) copy-start(bf16[32,32,128]{2,1,0:T(8,128)(2,1)S(1)} %collective-permute-done.3.rest_5_) | copy-start | bytes 786436
  192.0 5.4 %copy-start.8 = (bf16[32,32,128]{2,1,0:T(8,128)(2,1)}, bf16[32,32,128]{2,1,0:T(8,128)(2,1)S(1)}, u32[]{:S(2)}) copy-start(bf16[32,32,128]{2,1,0:T(8,128)(2,1)S(1)} %collective-permute-done.2.rest_4_) | copy-start | bytes 786436
  197.4 0.7 copy-start.9
Sparse Core Ops, SparseCore 0:
  18.5 38.0 all-gather.6
  99.0 40.1 all-gather.8
  150.7 54.4 all-gather.10

commit v5 on v4

--- a/solution.py
+++ b/solution.py
@@ -119,33 +119,41 @@
 
 def hop_kernel(
     level,
+    have,
+    ahead,
     take_ref,
     slot_ref,
     got_ref,
     all_op_ref,
     all_load_ref,
-    send_ref,
-    ops,
-    load,
-    total,
-    values,
-    ready,
-    loaded,
+    *rest,
 ):
+    ops, load, total, values, ready, loaded = rest[-6:]
+    send_ref = rest[1] if have else rest[0]
     senders, span, lanes = got_ref.shape
     pairs = load.shape[0]
     half = lanes // 2
     parts = ready.shape[0]
     share = senders // parts
-    copies = [
-        pltpu.make_async_copy(
-            all_op_ref.at[level, pl.ds(i * share, share)],
-            ops.at[pl.ds(i * share, share)],
-            ready.at[i],
-        )
-        for i in range(parts)
-    ]
-    for copy in copies:
+
+    def bring(source, target):
+        return [
+            pltpu.make_async_copy(
+                source.at[pl.ds(i * share, share)],
+                target.at[pl.ds(i * share, share)],
+                ready.at[i],
+            )
+            for i in range(parts)
+        ]
+
+    copies, following = [], []
+    if have:
+        ops = rest[0]
+    else:
+        copies = bring(all_op_ref.at[level], ops)
+    if ahead:
+        following = bring(all_op_ref.at[level + 1], rest[-7])
+    for copy in copies if copies else following:
         copy.start()
     loading = pltpu.make_async_copy(all_load_ref.at[level], load, loaded.at[0])
     loading.start()
@@ -159,6 +167,8 @@
         elif s == senders // 2:
             for copy in copies[parts // 2 :]:
                 copy.wait()
+            for copy in following if copies else []:
+                copy.start()
         op = ops[s]
         zero = jnp.zeros_like(op)
         split = jnp.concatenate(
@@ -179,6 +189,8 @@
             values[node] = (both_halves(value, odd, low, half) - come).astype(BF16)
     values[2 * pairs] = jnp.zeros((span, lanes), BF16)
     pack(values, take_ref, level, send_ref)
+    for copy in following:
+        copy.wait()
 
 
 def finish_kernel(
@@ -357,6 +369,8 @@
     message = jax.ShapeDtypeStruct((group, span, lanes), BF16)
     values_shape = pltpu.VMEM((nodes + 1, span, lanes), BF16)
     arrived = [None]
+    brought = (2, 4, 5)
+    following = []
     early_counts = (hops // 2, hops - 1 - hops // 2)
     early = []
     for level in range(hops):
@@ -371,11 +385,14 @@
                 name="first",
             )(take, loads)
         else:
-            send = pl.pallas_call(
-                functools.partial(hop_kernel, level),
-                in_specs=[SMEM_SPEC, SMEM_SPEC, VMEM_SPEC, HBM_SPEC, HBM_SPEC],
-                out_specs=VMEM_SPEC,
-                out_shape=message,
+            have, ahead = level in brought, level + 1 in brought
+            operator = jax.ShapeDtypeStruct((group, rows, lanes), BF16)
+            send, *following = pl.pallas_call(
+                functools.partial(hop_kernel, level, have, ahead),
+                in_specs=[SMEM_SPEC, SMEM_SPEC, VMEM_SPEC, HBM_SPEC, HBM_SPEC]
+                + [VMEM_SPEC] * have,
+                out_specs=[VMEM_SPEC] * (1 + ahead),
+                out_shape=[message] + [operator] * ahead,
                 scratch_shapes=[
                     pltpu.VMEM((group, rows, lanes), BF16),
                     pltpu.VMEM((pairs, span, lanes), BF16),
@@ -384,9 +401,9 @@
                     pltpu.SemaphoreType.DMA((8,)),
                     pltpu.SemaphoreType.DMA((1,)),
                 ],
-                compiler_params=params(53),
+                compiler_params=params(51),
                 name="hop",
-            )(take, slot, arrived[-1], operators, loads)
+            )(take, slot, arrived[-1], operators, loads, *following)
         arrived.append(lax.all_to_all(send, "grp", split_axis=0, concat_axis=0, tiled=True))
         if len(arrived) == 1 + sum(early_counts[: len(early) + 1]) and len(early) < 2:
             ready = jnp.stack(arrived[1 + sum(early_counts[: len(early)]) :])
@@ -403,7 +420,7 @@
             for c in range(levels)
         ]
 
-    step = 8
+    step = 16
     tail = lambda i: jnp.maximum(i - 1, 0)
     return pl.pallas_call(
         functools.partial(finish_kernel, early_counts),
@@ -425,7 +442,7 @@
             pltpu.VMEM((nodes, rows, block), BF16),
             pltpu.VMEM((nodes + 1, block, columns), F32),
             pltpu.SemaphoreType.DMA((3,)),
-            pltpu.SemaphoreType.DMA((levels, parts)),
+            pltpu.SemaphoreType.DMA((levels, 2)),
         ],
         compiler_params=params(58, "arbitrary"),
         name="finish",

time: 220 us -> 220 us (level)
  Pallas kernels: 31.4 us -> 29 us
  transfers between devices with their start and end apart: 12 -> 12, of which waited for: 9 -> 9; matrix products, arithmetic and copies ran while one was open for 1% -> 1% of each run, Pallas kernels for 6% -> 5%
where the time goes in v5:
time: 220 us; the launch traced here: 218 us
  blocking collectives  86.7 us (39%)
  waiting for transfers between devices  52.3 us (24%)
  Pallas kernels  29 us (13%)
  starting transfers between devices  26 us (12%)
  between operations  14.1 us (6%)
  local copies, waits for them, and re-layouts  5.56 us (3%)
  other arithmetic  4.8 us (2%)
    all_to_all x6, blocking collectives, shards(): lax.all_to_all(send, 'grp', split_axis=0, concat_axis=0, tiled=True)  86.7 us
    ppermute x7, waiting for transfers between devices, shards(): lax.ppermute(arrived[level], 'level', [(c, level)])  23.1 us
    pallas_call x6, Pallas kernels, shards(): pl.pallas_call(functools.partial(hop_kernel, level, have, ahead), in_spec...  15.5 us
    all_to_all x1, waiting for transfers between devices, shards(): lax.all_to_all(load, 'level', split_axis=0, concat_axis=0, tiled=True)  13.6 us
    all_to_all x1, starting transfers between devices, shards(): lax.all_to_all(send, 'grp', split_axis=0, concat_axis=0, tiled=True)  11 us
    all_to_all x1, waiting for transfers between devices, shards(): lax.all_to_all(send, 'grp', split_axis=0, concat_axis=0, tiled=True)  10.3 us
    ppermute x7, starting transfers between devices, shards(): lax.ppermute(arrived[level], 'level', [(c, level)])  9.01 us
    pallas_call x1, Pallas kernels, shards(): pl.pallas_call(functools.partial(finish_kernel, early_counts), grid=(1 +...  6.4 us
  transfers between devices with their start and end apart: 12, of which 9 were waited for; matrix products, arithmetic and copies ran while one was open for 1% of the time, Pallas kernels for 5%

profile of v5, /device:TPU:25, one launch (start us, length us, event | category | flops | bytes accessed | tf_op | source)
XLA Modules:
  0.0 218.4 jit_solution(4051176945838321071)
XLA Ops:
  7.2 0.9 slice_reduce_fusion
  8.3 0.3 select_reduce_fusion.7
  8.6 0.8 reshape.109
  9.5 0.4 select_reduce_fusion.6
  10.1 0.2 copy.79
  10.3 0.7 select_reduce_fusion.8.slot_ref
  11.0 0.3 select_reduce_fusion.1
  11.4 0.7 add_bitcast_fusion.rows_ref
  12.1 6.3 %prepare.1 = (bf16[32,64,128]{2,1,0:T(8,128)(2,1)}, bf16[8,16,32,128]{3,2,1,0:T(8,128)(2,1)}) custom-call(s32[64]{0:T(128)} %select_reduce_fusion.8.slot_ref, s32[32,128]{1,0:T(8,128)} %add_bitcast_fusion.rows_ref, bf16[32,128,256]{2,1,0:T(8,128)(2,1)} %bitcast.61, bf16[32,128,128]{2,1,0:T(8,128)(2,1)} %bitcast.65, bf16[32,64,128]{2,1,0:T(8,128)(2,1)} %bitcast.67), custom_call_target="tpu_custom_call" | custom-call | tf_op jit(solution)/shard_map/prepare/pallas_call | solution.py:345
  18.4 5.8 %all-to-all-start = ((bf16[8,16,32,128]{3,2,1,0:T(8,128)(2,1)}), bf16[8,16,32,128]{3,2,1,0:T(8,128)(2,1)S(1)}, u32[]{:S(2)}, u32[]{:S(2)}) async-start(bf16[8,16,32,128]{3,2,1,0:T(8,128)(2,1)} %get-tuple-element.10), calls=%async_computation | async-start | bytes 2097152 | tf_op jit(solution)/shard_map/all_to_all | solution.py:367
  24.2 0.3 select_reduce_fusion.3
  24.7 13.6 %all-to-all-done.load_ref.all_load_ref = bf16[8,16,32,128]{3,2,1,0:T(8,128)(2,1)S(1)} async-done(((bf16[8,16,32,128]{3,2,1,0:T(8,128)(2,1)}), bf16[8,16,32,128]{3,2,1,0:T(8,128)(2,1)S(1)}, u32[]{:S(2)}, u32[]{:S(2)}) %all-to-all-start) | async-done | bytes 1048608 | tf_op jit(solution)/shard_map/all_to_all | solution.py:367
  38.3 0.8 first.1
  39.1 0.7 copy-done.3
  39.8 11.0 %all-to-all-start.1 = ((bf16[32,32,128]{2,1,0:T(8,128)(2,1)}), bf16[32,32,128]{2,1,0:T(8,128)(2,1)S(1)}, u32[]{:S(2)}, u32[]{:S(2)}) async-start(bf16[32,32,128]{2,1,0:T(8,128)(2,1)} %copy-done.3), calls=%async_computation.1 | async-start | bytes 524288 | tf_op jit(solution)/shard_map/all_to_all | solution.py:407
  50.9 10.3 %all-to-all-done.1.got_ref = bf16[32,32,128]{2,1,0:T(8,128)(2,1)S(1)} async-done(((bf16[32,32,128]{2,1,0:T(8,128)(2,1)}), bf16[32,32,128]{2,1,0:T(8,128)(2,1)S(1)}, u32[]{:S(2)}, u32[]{:S(2)}) %all-to-all-start.1) | async-done | bytes 262176 | tf_op jit(solution)/shard_map/all_to_all | solution.py:407
  61.2 3.4 %hop.6 = (bf16[32,32,128]{2,1,0:T(8,128)(2,1)S(1)}, bf16[32,64,128]{2,1,0:T(8,128)(2,1)S(1)}) custom-call(s32[7,64]{1,0:T(8,128)S(1)} %copy.65.take_ref, s32[7,64]{1,0:T(8,128)S(1)} %copy.67.slot_ref, bf16[32,32,128]{2,1,0:T(8,128)(2,1)S(1)} %all-to-all-done.1.got_ref, bf16[8,32,64,128]{3,2,1,0:T(8,128)(2,1)} %bitcast.55, ...), custom_call_target="tpu_custom_call" | custom-call | tf_op jit(solution)/shard_map/hop/pallas_call | solution.py:390
  64.6 15.8 %all_to_all.40.got_ref = bf16[32,32,128]{2,1,0:T(8,128)(2,1)S(1)} all-to-all(bf16[32,32,128]{2,1,0:T(8,128)(2,1)S(1)} %get-tuple-element.12), channel_id=1, replica_groups=mesh['level'=8,'grp'=32] {'grp'}, dimensions={0} | all-to-all | bytes 524288 | tf_op jit(solution)/shard_map/all_to_all | solution.py:407
  80.5 1.9 hop.7
  82.4 15.1 %all_to_all.41.got_ref = bf16[32,32,128]{2,1,0:T(8,128)(2,1)S(1)} all-to-all(bf16[32,32,128]{2,1,0:T(8,128)(2,1)S(1)} %hop.7), channel_id=1, replica_groups=mesh['level'=8,'grp'=32] {'grp'}, dimensions={0} | all-to-all | bytes 524288 | tf_op jit(solution)/shard_map/all_to_all | solution.py:407
  97.5 1.0 pad_maximum_fusion
  98.5 0.7 copy-done.1
  99.2 0.9 copy-done.2
  100.2 3.4 %hop.8 = (bf16[32,32,128]{2,1,0:T(8,128)(2,1)S(1)}, bf16[32,64,128]{2,1,0:T(8,128)(2,1)S(1)}) custom-call(s32[7,64]{1,0:T(8,128)S(1)} %copy.65.take_ref, s32[7,64]{1,0:T(8,128)S(1)} %copy.67.slot_ref, bf16[32,32,128]{2,1,0:T(8,128)(2,1)S(1)} %copy-done.2, bf16[8,32,64,128]{3,2,1,0:T(8,128)(2,1)} %bitcast.57, ...), custom_call_target="tpu_custom_call" | custom-call | tf_op jit(solution)/shard_map/hop/pallas_call | solution.py:390
  103.6 14.0 %all_to_all.42.got_ref = bf16[32,32,128]{2,1,0:T(8,128)(2,1)S(1)} all-to-all(bf16[32,32,128]{2,1,0:T(8,128)(2,1)S(1)} %get-tuple-element.14), channel_id=1, replica_groups=mesh['level'=8,'grp'=32] {'grp'}, dimensions={0} | all-to-all | bytes 524288 | tf_op jit(solution)/shard_map/all_to_all | solution.py:407
  117.7 2.0 hop.9
  119.6 14.0 %all_to_all.43.got_ref = bf16[32,32,128]{2,1,0:T(8,128)(2,1)S(1)} all-to-all(bf16[32,32,128]{2,1,0:T(8,128)(2,1)S(1)} %get-tuple-element.16), channel_id=1, replica_groups=mesh['level'=8,'grp'=32] {'grp'}, dimensions={0} | all-to-all | bytes 524288 | tf_op jit(solution)/shard_map/all_to_all | solution.py:407
  133.7 1.9 hop.10
  135.6 14.0 %all_to_all.44.got_ref = bf16[32,32,128]{2,1,0:T(8,128)(2,1)S(1)} all-to-all(bf16[32,32,128]{2,1,0:T(8,128)(2,1)S(1)} %hop.10), channel_id=1, replica_groups=mesh['level'=8,'grp'=32] {'grp'}, dimensions={0} | all-to-all | bytes 524288 | tf_op jit(solution)/shard_map/all_to_all | solution.py:407
  149.6 1.0 pad_maximum_fusion.1
  150.6 2.8 %hop.11 = bf16[32,32,128]{2,1,0:T(8,128)(2,1)S(1)} custom-call(s32[7,64]{1,0:T(8,128)S(1)} %copy.65.take_ref, s32[7,64]{1,0:T(8,128)S(1)} %copy.67.slot_ref, bf16[32,32,128]{2,1,0:T(8,128)(2,1)S(1)} %all_to_all.44.got_ref, bf16[8,32,64,128]{3,2,1,0:T(8,128)(2,1)} %bitcast.60, bf16[8,16,32,128]{3,2,1,0:T(8,128)(2,1)S(1)} %all-to-all-done.load_ref.all_load_ref), custom_call_target="tpu_custom_call" | custom-call | tf_op jit(solution)/shard_map/hop/pallas_call | solution.py:390
  153.4 13.7 %all_to_all.45.rest_9_ = bf16[32,32,128]{2,1,0:T(8,128)(2,1)S(1)} all-to-all(bf16[32,32,128]{2,1,0:T(8,128)(2,1)S(1)} %hop.11), channel_id=1, replica_groups=mesh['level'=8,'grp'=32] {'grp'}, dimensions={0} | all-to-all | bytes 524288 | tf_op jit(solution)/shard_map/all_to_all | solution.py:407
  167.2 1.3 collective-permute-start.6
  168.4 1.3 collective-permute-start.5
  169.7 1.3 collective-permute-start.4
  171.0 1.3 collective-permute-start.3
  172.3 1.3 collective-permute-start.2
  173.6 4.2 %collective-permute-done.6.rest_8_ = bf16[32,32,128]{2,1,0:T(8,128)(2,1)S(1)} collective-permute-done((bf16[32,32,128]{2,1,0:T(8,128)(2,1)S(1)}, bf16[32,32,128]{2,1,0:T(8,128)(2,1)S(1)}, u32[]{:S(2)}, u32[]{:S(2)}) %collective-permute-start.6) | collective-permute-done | bytes 262176 | tf_op jit(solution)/shard_map/ppermute | solution.py:419
  177.8 1.3 collective-permute-start.1
  179.1 2.9 %collective-permute-done.5.rest_7_ = bf16[32,32,128]{2,1,0:T(8,128)(2,1)S(1)} collective-permute-done((bf16[32,32,128]{2,1,0:T(8,128)(2,1)S(1)}, bf16[32,32,128]{2,1,0:T(8,128)(2,1)S(1)}, u32[]{:S(2)}, u32[]{:S(2)}) %collective-permute-start.5) | collective-permute-done | bytes 262176 | tf_op jit(solution)/shard_map/ppermute | solution.py:419
  182.0 1.3 collective-permute-start
  183.3 5.9 %collective-permute-done.4.rest_6_ = bf16[32,32,128]{2,1,0:T(8,128)(2,1)S(1)} collective-permute-done((bf16[32,32,128]{2,1,0:T(8,128)(2,1)S(1)}, bf16[32,32,128]{2,1,0:T(8,128)(2,1)S(1)}, u32[]{:S(2)}, u32[]{:S(2)}) %collective-permute-start.4) | collective-permute-done | bytes 262176 | tf_op jit(solution)/shard_map/ppermute | solution.py:419
  189.1 2.8 %collective-permute-done.2.rest_4_ = bf16[32,32,128]{2,1,0:T(8,128)(2,1)S(1)} collective-permute-done((bf16[32,32,128]{2,1,0:T(8,128)(2,1)S(1)}, bf16[32,32,128]{2,1,0:T(8,128)(2,1)S(1)}, u32[]{:S(2)}, u32[]{:S(2)}) %collective-permute-start.2) | collective-permute-done | bytes 262176 | tf_op jit(solution)/shard_map/ppermute | solution.py:419
  192.0 5.4 %collective-permute-done.1.rest_3_ = bf16[32,32,128]{2,1,0:T(8,128)(2,1)S(1)} collective-permute-done((bf16[32,32,128]{2,1,0:T(8,128)(2,1)S(1)}, bf16[32,32,128]{2,1,0:T(8,128)(2,1)S(1)}, u32[]{:S(2)}, u32[]{:S(2)}) %collective-permute-start.1) | collective-permute-done | bytes 262176 | tf_op jit(solution)/shard_map/ppermute | solution.py:419
  197.4 0.7 copy-done.10
  198.1 2.0 collective-permute-done.rest_2_
  200.0 5.3 %all-gather.11.cloned.1.call-done = bf16[24,32,32,128]{3,2,1,0:T(8,128)(2,1)} async-done(((bf16[3,32,32,128]{3,2,1,0:T(8,128)(2,1)}), bf16[24,32,32,128]{3,2,1,0:T(8,128)(2,1)}) %all-gather.11.cloned.1.call-update) | async-done | bytes 6291472 | tf_op jit(solution)/shard_map/all_gather | solution.py:410
  205.4 6.4 %finish.1 = (bf16[1,32,128,256]{3,2,1,0:T(8,128)(2,1)}, bf16[1,32,64,256]{3,2,1,0:T(8,128)(2,1)}) custom-call(s32[1]{0:T(128)} %bitcast.level_ref, s32[64]{0:T(128)} %select_reduce_fusion.8.slot_ref, s32[32,128]{1,0:T(8,128)} %add_bitcast_fusion.rows_ref, bf16[32,128,256]{2,1,0:T(8,128)(2,1)} %bitcast.62, bf16[32,128,128]{2,1,0:T(8,128)(2,1)} %bitcast.66, ...), custom_call_target="tpu_custom_call" | custom-call | tf_op jit(solution)/shard_map/finish/pallas_call | solution.py:425
  (44 shorter events, 0.9 us)
Async XLA Ops:
  7.2 2.9 %copy-start = (s32[8,64,1024]{2,1,0:T(8,128)S(1)}, s32[8,64,1024]{2,1,0:T(8,128)}, u32[]{:S(2)}) copy-start(s32[8,64,1024]{2,1,0:T(8,128)} %param.11) | copy-start | bytes 6291460
  7.2 54.0 %all-gather.7.cloned.1.call-start = ((), (), s32[]{:S(2)}) async-start(), calls=%async_computation.8 | async-start | bytes 4718592 | tf_op jit(solution)/shard_map/all_gather | solution.py:366
  18.4 19.9 %all-to-all-start = ((bf16[8,16,32,128]{3,2,1,0:T(8,128)(2,1)}), bf16[8,16,32,128]{3,2,1,0:T(8,128)(2,1)S(1)}, u32[]{:S(2)}, u32[]{:S(2)}) async-start(bf16[8,16,32,128]{3,2,1,0:T(8,128)(2,1)} %get-tuple-element.10), calls=%async_computation | async-start | bytes 2097152 | tf_op jit(solution)/shard_map/all_to_all | solution.py:367
  39.1 0.7 copy-start.3
  39.8 21.4 %all-to-all-start.1 = ((bf16[32,32,128]{2,1,0:T(8,128)(2,1)}), bf16[32,32,128]{2,1,0:T(8,128)(2,1)S(1)}, u32[]{:S(2)}, u32[]{:S(2)}) async-start(bf16[32,32,128]{2,1,0:T(8,128)(2,1)} %copy-done.3), calls=%async_computation.1 | async-start | bytes 524288 | tf_op jit(solution)/shard_map/all_to_all | solution.py:407
  50.8 149.2 %all-gather.9.cloned.1.call-start = ((), (), s32[]{:S(2)}) async-start(), calls=%async_computation.9 | async-start | bytes 7077888 | tf_op jit(solution)/shard_map/all_gather | solution.py:410
  98.5 0.7 copy-start.1
  99.2 106.2 %all-gather.11.cloned.1.call-start = ((), (), s32[]{:S(2)}) async-start(), calls=%async_computation.10 | async-start | bytes 7077888 | tf_op jit(solution)/shard_map/all_gather | solution.py:410
  99.2 1.0 copy-start.2
  167.2 38.2 %copy-start.4 = (bf16[32,32,128]{2,1,0:T(8,128)(2,1)}, bf16[32,32,128]{2,1,0:T(8,128)(2,1)S(1)}, u32[]{:S(2)}) copy-start(bf16[32,32,128]{2,1,0:T(8,128)(2,1)S(1)} %all_to_all.45.rest_9_) | copy-start | bytes 786436
  167.2 10.7 %collective-permute-start.6 = (bf16[32,32,128]{2,1,0:T(8,128)(2,1)S(1)}, bf16[32,32,128]{2,1,0:T(8,128)(2,1)S(1)}, u32[]{:S(2)}, u32[]{:S(2)}) collective-permute-start(bf16[32,32,128]{2,1,0:T(8,128)(2,1)S(1)} %all_to_all.45.rest_9_), channel_id=1, source_target_pairs={{192,224},{193,225},{194,226},{195,227},{196,228},{197,229},{198,2... | collective-permute-start | bytes 786440 | tf_op jit(solution)/shard_map/ppermute | solution.py:419
  168.4 13.5 %collective-permute-start.5 = (bf16[32,32,128]{2,1,0:T(8,128)(2,1)S(1)}, bf16[32,32,128]{2,1,0:T(8,128)(2,1)S(1)}, u32[]{:S(2)}, u32[]{:S(2)}) collective-permute-start(bf16[32,32,128]{2,1,0:T(8,128)(2,1)S(1)} %all_to_all.45.rest_9_), channel_id=1, source_target_pairs={{160,224},{161,225},{162,226},{163,227},{164,228},{165,229},{166,2... | collective-permute-start | bytes 786440 | tf_op jit(solution)/shard_map/ppermute | solution.py:419
  169.7 19.4 %collective-permute-start.4 = (bf16[32,32,128]{2,1,0:T(8,128)(2,1)S(1)}, bf16[32,32,128]{2,1,0:T(8,128)(2,1)S(1)}, u32[]{:S(2)}, u32[]{:S(2)}) collective-permute-start(bf16[32,32,128]{2,1,0:T(8,128)(2,1)S(1)} %all_to_all.45.rest_9_), channel_id=1, source_target_pairs={{128,224},{129,225},{130,226},{131,227},{132,228},{133,229},{134,2... | collective-permute-start | bytes 786440 | tf_op jit(solution)/shard_map/ppermute | solution.py:419
  171.0 18.1 %collective-permute-start.3 = (bf16[32,32,128]{2,1,0:T(8,128)(2,1)S(1)}, bf16[32,32,128]{2,1,0:T(8,128)(2,1)S(1)}, u32[]{:S(2)}, u32[]{:S(2)}) collective-permute-start(bf16[32,32,128]{2,1,0:T(8,128)(2,1)S(1)} %all_to_all.45.rest_9_), channel_id=1, source_target_pairs={{96,224},{97,225},{98,226},{99,227},{100,228},{101,229},{102,230},... | collective-permute-start | bytes 786440 | tf_op jit(solution)/shard_map/ppermute | solution.py:419
  172.3 19.6 %collective-permute-start.2 = (bf16[32,32,128]{2,1,0:T(8,128)(2,1)S(1)}, bf16[32,32,128]{2,1,0:T(8,128)(2,1)S(1)}, u32[]{:S(2)}, u32[]{:S(2)}) collective-permute-start(bf16[32,32,128]{2,1,0:T(8,128)(2,1)S(1)} %all_to_all.45.rest_9_), channel_id=1, source_target_pairs={{64,224},{65,225},{66,226},{67,227},{68,228},{69,229},{70,230},{71... | collective-permute-start | bytes 786440 | tf_op jit(solution)/shard_map/ppermute | solution.py:419
  177.8 27.6 %copy-start.5 = (bf16[32,32,128]{2,1,0:T(8,128)(2,1)}, bf16[32,32,128]{2,1,0:T(8,128)(2,1)S(1)}, u32[]{:S(2)}) copy-start(bf16[32,32,128]{2,1,0:T(8,128)(2,1)S(1)} %collective-permute-done.6.rest_8_) | copy-start | bytes 786436
  177.8 19.5 %collective-permute-start.1 = (bf16[32,32,128]{2,1,0:T(8,128)(2,1)S(1)}, bf16[32,32,128]{2,1,0:T(8,128)(2,1)S(1)}, u32[]{:S(2)}, u32[]{:S(2)}) collective-permute-start(bf16[32,32,128]{2,1,0:T(8,128)(2,1)S(1)} %all_to_all.45.rest_9_), channel_id=1, source_target_pairs={{32,224},{33,225},{34,226},{35,227},{36,228},{37,229},{38,230},{39... | collective-permute-start | bytes 786440 | tf_op jit(solution)/shard_map/ppermute | solution.py:419
  182.0 23.4 %copy-start.6 = (bf16[32,32,128]{2,1,0:T(8,128)(2,1)}, bf16[32,32,128]{2,1,0:T(8,128)(2,1)S(1)}, u32[]{:S(2)}) copy-start(bf16[32,32,128]{2,1,0:T(8,128)(2,1)S(1)} %collective-permute-done.5.rest_7_) | copy-start | bytes 786436
  182.0 18.1 %collective-permute-start = (bf16[32,32,128]{2,1,0:T(8,128)(2,1)S(1)}, bf16[32,32,128]{2,1,0:T(8,128)(2,1)}, u32[]{:S(2)}, u32[]{:S(2)}) collective-permute-start(bf16[32,32,128]{2,1,0:T(8,128)(2,1)S(1)} %all_to_all.45.rest_9_), channel_id=1, source_target_pairs={{0,224},{1,225},{2,226},{3,227},{4,228},{5,229},{6,230},{7,231},{8... | collective-permute-start | bytes 786440 | tf_op jit(solution)/shard_map/ppermute | solution.py:419
  189.1 16.3 %copy-start.7 = (bf16[32,32,128]{2,1,0:T(8,128)(2,1)}, bf16[32,32,128]{2,1,0:T(8,128)(2,1)S(1)}, u32[]{:S(2)}) copy-start(bf16[32,32,128]{2,1,0:T(8,128)(2,1)S(1)} %collective-permute-done.4.rest_6_) | copy-start | bytes 786436
  189.1 16.3 %copy-start.8 = (bf16[32,32,128]{2,1,0:T(8,128)(2,1)}, bf16[32,32,128]{2,1,0:T(8,128)(2,1)S(1)}, u32[]{:S(2)}) copy-start(bf16[32,32,128]{2,1,0:T(8,128)(2,1)S(1)} %collective-permute-done.3.rest_5_) | copy-start | bytes 786436
  192.0 5.4 %copy-start.9 = (bf16[32,32,128]{2,1,0:T(8,128)(2,1)}, bf16[32,32,128]{2,1,0:T(8,128)(2,1)S(1)}, u32[]{:S(2)}) copy-start(bf16[32,32,128]{2,1,0:T(8,128)(2,1)S(1)} %collective-permute-done.2.rest_4_) | copy-start | bytes 786436
  197.4 0.7 copy-start.10
Sparse Core Ops, SparseCore 0:
  18.5 38.0 all-gather.6
  99.3 40.2 all-gather.8
  150.7 54.6 all-gather.10

commit v6 on v4

--- a/solution.py
+++ b/solution.py
@@ -298,36 +298,24 @@
     slots = parent_slot[:hops].reshape(hops, group, nodes)
     place = lax.broadcasted_iota(jnp.int32, (hops, group, nodes), 2)
 
-    def ends(named):
+    def ends(named, place):
         first = jnp.min(jnp.where(named, place, nodes), axis=-1)
         last = jnp.max(jnp.where(named, place, -1), axis=-1)
         return first, jnp.where(last > first, last, nodes)
 
-    first, last = ends(devices == member)
-    own = lax.dynamic_index_in_dim(devices, member, 1, keepdims=True)
-    take = jnp.stack(ends(own == lax.broadcasted_iota(jnp.int32, (hops, group, nodes), 1)), -1)
-    take = take.reshape(hops, 2 * group)
-
-    def slot_of(which):
-        hit = place == which[..., None]
-        found = jnp.sum(jnp.where(hit, slots, 0), axis=-1)
-        return jnp.where(which < nodes, found, nodes)
-
-    slot = jnp.stack([slot_of(first), slot_of(last)], -1).reshape(hops, 2 * group)
-
     before = jnp.maximum(level_id - 1, 0)
-    home_slot = lax.dynamic_index_in_dim(slot, before, 0, keepdims=False)
-    home_slot = jnp.where(level_id > 0, home_slot, nodes)
-    landing = lax.dynamic_index_in_dim(row_index, before, 0, keepdims=False)
-    landing = landing.reshape(rows, group, nodes)
-
-    def rows_of(which):
-        which = lax.dynamic_index_in_dim(which, before, 0, keepdims=False)[None, :, None]
-        hit = lax.broadcasted_iota(jnp.int32, (rows, group, nodes), 2) == which
-        found = jnp.sum(jnp.where(hit, landing, 0), axis=-1)
-        return jnp.where(which[..., 0] < nodes, found, -1)
-
-    home_rows = jnp.concatenate([rows_of(first), rows_of(last)], axis=0).T
+
+    def at_home(array):
+        return lax.dynamic_index_in_dim(array, before, 0, keepdims=False)
+
+    named = at_home(parent_device).reshape(group, nodes) == member
+    which = jnp.where(level_id > 0, jnp.stack(ends(named, place[0])), nodes)
+    hit = place[:1] == which[..., None]
+    home_slot = jnp.sum(jnp.where(hit, at_home(parent_slot).reshape(group, nodes) - nodes, 0), -1)
+    home_slot = (home_slot + nodes).T.reshape(-1)
+    landing = at_home(row_index).reshape(rows, group, nodes) + 1
+    home_rows = jnp.sum(jnp.where(hit[:, None], landing, 0), -1) - 1
+    home_rows = home_rows.reshape(lanes, group).T
 
     parts = 4
     operators, load = pl.pallas_call(
@@ -354,10 +342,21 @@
     operators = lax.all_gather(operators, "level", axis=0)
     loads = lax.all_to_all(load, "level", split_axis=0, concat_axis=0, tiled=True)
 
+    first, last = ends(devices == member, place)
+    own = lax.dynamic_index_in_dim(devices, member, 1, keepdims=True)
+    receiver = lax.broadcasted_iota(jnp.int32, (hops, group, nodes), 1)
+    take = jnp.stack(ends(own == receiver, place), -1).reshape(hops, 2 * group)
+
+    def slot_of(which):
+        hit = place == which[..., None]
+        return jnp.sum(jnp.where(hit, slots - nodes, 0), axis=-1) + nodes
+
+    slot = jnp.stack([slot_of(first), slot_of(last)], -1).reshape(hops, 2 * group)
+
     message = jax.ShapeDtypeStruct((group, span, lanes), BF16)
     values_shape = pltpu.VMEM((nodes + 1, span, lanes), BF16)
     arrived = [None]
-    early_counts = (hops // 2, hops - 1 - hops // 2)
+    early_counts = (hops // 2, hops - 2 - hops // 2)
     early = []
     for level in range(hops):
         if level == 0:
@@ -395,15 +394,13 @@
             arrived[-1], early[0] = lax.optimization_barrier((arrived[-1], early[0]))
 
     late = []
+    after = lax.optimization_barrier((arrived[-2], arrived[-1]))
     for level in range(1 + sum(early_counts), levels):
-        late += [
-            arrived[level]
-            if c == level
-            else lax.ppermute(arrived[level], "level", [(c, level)])
-            for c in range(levels)
-        ]
-
-    step = 8
+        for c in range(levels):
+            value = arrived[level] if c < 5 and level < hops else after[level - levels]
+            late.append(value if c == level else lax.ppermute(value, "level", [(c, level)]))
+
+    step = 16
     tail = lambda i: jnp.maximum(i - 1, 0)
     return pl.pallas_call(
         functools.partial(finish_kernel, early_counts),
@@ -425,7 +422,7 @@
             pltpu.VMEM((nodes, rows, block), BF16),
             pltpu.VMEM((nodes + 1, block, columns), F32),
             pltpu.SemaphoreType.DMA((3,)),
-            pltpu.SemaphoreType.DMA((levels, parts)),
+            pltpu.SemaphoreType.DMA((levels, 2)),
         ],
         compiler_params=params(58, "arbitrary"),
         name="finish",

time: 220 us -> 216 us (0.982)
  starting transfers between devices: 26 us -> 46.2 us
  blocking collectives: 86.9 us -> 72.9 us
  waiting for transfers between devices: 52 us -> 39.9 us
    ppermute x7 -> x14, starting transfers between devices: 9.01 us -> 25.4 us  [shards(): lax.ppermute(value, 'level', [(c, level)])]
    all_to_all x6 -> x5, blocking collectives: 86.9 us -> 72.9 us  [shards(): lax.all_to_all(send, 'grp', split_axis=0, concat_axis=0, tiled=True)]
    ppermute x7 -> x14, waiting for transfers between devices: 23.1 us -> 12.8 us  [shards(): lax.ppermute(value, 'level', [(c, level)])]
    all_gather x2, waiting for transfers between devices: 5.07 us -> 0.02 us  [shards(): early.append(lax.all_gather(ready, 'level', axis=0))]
    all_to_all x1 -> x2, waiting for transfers between devices: 10.3 us -> 14.6 us  [shards(): lax.all_to_all(send, 'grp', split_axis=0, concat_axis=0, tiled=True)]
    all_to_all x1 -> x2, starting transfers between devices: 11.1 us -> 14.9 us  [shards(): lax.all_to_all(send, 'grp', split_axis=0, concat_axis=0, tiled=True)]
  transfers between devices with their start and end apart: 12 -> 20, of which waited for: 9 -> 7; matrix products, arithmetic and copies ran while one was open for 1% -> 2% of each run, Pallas kernels for 6% -> 6%
where the time goes in v6:
time: 216 us; the launch traced here: 215 us
  blocking collectives  72.9 us (34%)
  starting transfers between devices  46.2 us (21%)
  waiting for transfers between devices  39.9 us (18%)
  Pallas kernels  31.1 us (14%)
  between operations  14.3 us (7%)
  other arithmetic  5.85 us (3%)
  local copies, waits for them, and re-layouts  4.63 us (2%)
    all_to_all x5, blocking collectives, shards(): lax.all_to_all(send, 'grp', split_axis=0, concat_axis=0, tiled=True)  72.9 us
    ppermute x14, starting transfers between devices, shards(): lax.ppermute(value, 'level', [(c, level)])  25.4 us
    pallas_call x6, Pallas kernels, shards(): pl.pallas_call(functools.partial(hop_kernel, level), in_specs=[SMEM_SPEC,...  17.7 us
    all_to_all x2, starting transfers between devices, shards(): lax.all_to_all(send, 'grp', split_axis=0, concat_axis=0, tiled=True)  14.9 us
    all_to_all x2, waiting for transfers between devices, shards(): lax.all_to_all(send, 'grp', split_axis=0, concat_axis=0, tiled=True)  14.6 us
    ppermute x14, waiting for transfers between devices, shards(): lax.ppermute(value, 'level', [(c, level)])  12.8 us
    all_to_all x1, waiting for transfers between devices, shards(): lax.all_to_all(load, 'level', split_axis=0, concat_axis=0, tiled=True)  12.5 us
    pallas_call x1, Pallas kernels, shards(): pl.pallas_call(functools.partial(finish_kernel, early_counts), grid=(1 +...  6.43 us
  transfers between devices with their start and end apart: 20, of which 7 were waited for; matrix products, arithmetic and copies ran while one was open for 2% of the time, Pallas kernels for 6%

profile of v6, /device:TPU:25, one launch (start us, length us, event | category | flops | bytes accessed | tf_op | source)
XLA Modules:
  0.0 215.0 jit_solution(10927304645697999865)
XLA Ops:
  7.2 0.8 compare_reduce_fusion
  8.3 0.8 add_reduce_fusion
  9.4 0.7 reshape.116.slot_ref
  10.8 0.7 sub.25
  11.5 6.3 %prepare.1 = (bf16[32,64,128]{2,1,0:T(8,128)(2,1)}, bf16[8,16,32,128]{3,2,1,0:T(8,128)(2,1)}) custom-call(s32[64]{0:T(128)} %reshape.116.slot_ref, s32[32,128]{1,0:T(8,128)} %bitcast.61, bf16[32,128,256]{2,1,0:T(8,128)(2,1)} %bitcast.52, bf16[32,128,128]{2,1,0:T(8,128)(2,1)} %bitcast.56, bf16[32,64,128]{2,1,0:T(8,128)(2,1)} %bitcast.58), custom_call_target="tpu_custom_call" | custom-call | tf_op jit(solution)/shard_map/prepare/pallas_call | solution.py:321
  17.8 5.8 %all-to-all-start = ((bf16[8,16,32,128]{3,2,1,0:T(8,128)(2,1)}), bf16[8,16,32,128]{3,2,1,0:T(8,128)(2,1)S(1)}, u32[]{:S(2)}, u32[]{:S(2)}) async-start(bf16[8,16,32,128]{3,2,1,0:T(8,128)(2,1)} %get-tuple-element.8), calls=%async_computation | async-start | bytes 2097152 | tf_op jit(solution)/shard_map/all_to_all | solution.py:343
  24.6 0.6 slice_add_fusion
  25.2 12.5 %all-to-all-done.load_ref.all_load_ref = bf16[8,16,32,128]{3,2,1,0:T(8,128)(2,1)S(1)} async-done(((bf16[8,16,32,128]{3,2,1,0:T(8,128)(2,1)}), bf16[8,16,32,128]{3,2,1,0:T(8,128)(2,1)S(1)}, u32[]{:S(2)}, u32[]{:S(2)}) %all-to-all-start) | async-done | bytes 1048608 | tf_op jit(solution)/shard_map/all_to_all | solution.py:343
  37.7 0.8 first.1
  38.5 0.7 copy-done.3
  39.2 11.0 %all-to-all-start.1 = ((bf16[32,32,128]{2,1,0:T(8,128)(2,1)}), bf16[32,32,128]{2,1,0:T(8,128)(2,1)S(1)}, u32[]{:S(2)}, u32[]{:S(2)}) async-start(bf16[32,32,128]{2,1,0:T(8,128)(2,1)} %copy-done.3), calls=%async_computation.1 | async-start | bytes 524288 | tf_op jit(solution)/shard_map/all_to_all | solution.py:389
  50.3 0.8 sub.27
  51.8 8.9 %all-to-all-done.1.got_ref = bf16[32,32,128]{2,1,0:T(8,128)(2,1)S(1)} async-done(((bf16[32,32,128]{2,1,0:T(8,128)(2,1)}), bf16[32,32,128]{2,1,0:T(8,128)(2,1)S(1)}, u32[]{:S(2)}, u32[]{:S(2)}) %all-to-all-start.1) | async-done | bytes 262176 | tf_op jit(solution)/shard_map/all_to_all | solution.py:389
  60.7 2.8 %hop.6 = bf16[32,32,128]{2,1,0:T(8,128)(2,1)S(1)} custom-call(s32[7,64]{1,0:T(8,128)S(1)} %copy.60.take_ref, s32[7,64]{1,0:T(8,128)S(1)} %copy.61.slot_ref, bf16[32,32,128]{2,1,0:T(8,128)(2,1)S(1)} %all-to-all-done.1.got_ref, bf16[8,32,64,128]{3,2,1,0:T(8,128)(2,1)} %bitcast.46, bf16[8,16,32,128]{3,2,1,0:T(8,128)(2,1)} %copy-done.1), custom_call_target="tpu_custom_call" | custom-call | tf_op jit(solution)/shard_map/hop/pallas_call | solution.py:373
  63.5 15.8 %all_to_all.40.got_ref = bf16[32,32,128]{2,1,0:T(8,128)(2,1)S(1)} all-to-all(bf16[32,32,128]{2,1,0:T(8,128)(2,1)S(1)} %hop.6), channel_id=1, replica_groups=mesh['level'=8,'grp'=32] {'grp'}, dimensions={0} | all-to-all | bytes 524288 | tf_op jit(solution)/shard_map/all_to_all | solution.py:389
  79.3 2.8 %hop.7 = bf16[32,32,128]{2,1,0:T(8,128)(2,1)S(1)} custom-call(s32[7,64]{1,0:T(8,128)S(1)} %copy.60.take_ref, s32[7,64]{1,0:T(8,128)S(1)} %copy.61.slot_ref, bf16[32,32,128]{2,1,0:T(8,128)(2,1)S(1)} %all_to_all.40.got_ref, bf16[8,32,64,128]{3,2,1,0:T(8,128)(2,1)} %bitcast.47, bf16[8,16,32,128]{3,2,1,0:T(8,128)(2,1)} %copy-done.1), custom_call_target="tpu_custom_call" | custom-call | tf_op jit(solution)/shard_map/hop/pallas_call | solution.py:373
  82.1 15.0 %all_to_all.41.got_ref = bf16[32,32,128]{2,1,0:T(8,128)(2,1)S(1)} all-to-all(bf16[32,32,128]{2,1,0:T(8,128)(2,1)S(1)} %hop.7), channel_id=1, replica_groups=mesh['level'=8,'grp'=32] {'grp'}, dimensions={0} | all-to-all | bytes 524288 | tf_op jit(solution)/shard_map/all_to_all | solution.py:389
  97.1 1.0 pad_maximum_fusion
  98.2 2.8 %hop.8 = bf16[32,32,128]{2,1,0:T(8,128)(2,1)S(1)} custom-call(s32[7,64]{1,0:T(8,128)S(1)} %copy.60.take_ref, s32[7,64]{1,0:T(8,128)S(1)} %copy.61.slot_ref, bf16[32,32,128]{2,1,0:T(8,128)(2,1)S(1)} %all_to_all.41.got_ref, bf16[8,32,64,128]{3,2,1,0:T(8,128)(2,1)} %bitcast.48, bf16[8,16,32,128]{3,2,1,0:T(8,128)(2,1)} %copy-done.1), custom_call_target="tpu_custom_call" | custom-call | tf_op jit(solution)/shard_map/hop/pallas_call | solution.py:373
  101.0 14.1 %all_to_all.42.got_ref = bf16[32,32,128]{2,1,0:T(8,128)(2,1)S(1)} all-to-all(bf16[32,32,128]{2,1,0:T(8,128)(2,1)S(1)} %hop.8), channel_id=1, replica_groups=mesh['level'=8,'grp'=32] {'grp'}, dimensions={0} | all-to-all | bytes 524288 | tf_op jit(solution)/shard_map/all_to_all | solution.py:389
  115.1 2.9 %hop.9 = bf16[32,32,128]{2,1,0:T(8,128)(2,1)S(1)} custom-call(s32[7,64]{1,0:T(8,128)S(1)} %copy.60.take_ref, s32[7,64]{1,0:T(8,128)S(1)} %copy.61.slot_ref, bf16[32,32,128]{2,1,0:T(8,128)(2,1)S(1)} %all_to_all.42.got_ref, bf16[8,32,64,128]{3,2,1,0:T(8,128)(2,1)} %bitcast.49, bf16[8,16,32,128]{3,2,1,0:T(8,128)(2,1)} %copy-done.1), custom_call_target="tpu_custom_call" | custom-call | tf_op jit(solution)/shard_map/hop/pallas_call | solution.py:373
  117.9 14.1 %all_to_all.43.got_ref = bf16[32,32,128]{2,1,0:T(8,128)(2,1)S(1)} all-to-all(bf16[32,32,128]{2,1,0:T(8,128)(2,1)S(1)} %hop.9), channel_id=1, replica_groups=mesh['level'=8,'grp'=32] {'grp'}, dimensions={0} | all-to-all | bytes 524288 | tf_op jit(solution)/shard_map/all_to_all | solution.py:389
  132.0 0.8 pad_maximum_fusion.1
  132.8 2.8 %hop.10 = bf16[32,32,128]{2,1,0:T(8,128)(2,1)S(1)} custom-call(s32[7,64]{1,0:T(8,128)S(1)} %copy.60.take_ref, s32[7,64]{1,0:T(8,128)S(1)} %copy.61.slot_ref, bf16[32,32,128]{2,1,0:T(8,128)(2,1)S(1)} %all_to_all.43.got_ref, bf16[8,32,64,128]{3,2,1,0:T(8,128)(2,1)} %bitcast.50, bf16[8,16,32,128]{3,2,1,0:T(8,128)(2,1)} %copy-done.1), custom_call_target="tpu_custom_call" | custom-call | tf_op jit(solution)/shard_map/hop/pallas_call | solution.py:373
  135.7 14.0 %all_to_all.44.got_ref.rest_8_ = bf16[32,32,128]{2,1,0:T(8,128)(2,1)S(1)} all-to-all(bf16[32,32,128]{2,1,0:T(8,128)(2,1)S(1)} %hop.10), channel_id=1, replica_groups=mesh['level'=8,'grp'=32] {'grp'}, dimensions={0} | all-to-all | bytes 524288 | tf_op jit(solution)/shard_map/all_to_all | solution.py:389
  149.7 3.5 %hop.11 = bf16[32,32,128]{2,1,0:T(8,128)(2,1)} custom-call(s32[7,64]{1,0:T(8,128)S(1)} %copy.60.take_ref, s32[7,64]{1,0:T(8,128)S(1)} %copy.61.slot_ref, bf16[32,32,128]{2,1,0:T(8,128)(2,1)S(1)} %all_to_all.44.got_ref.rest_8_, bf16[8,32,64,128]{3,2,1,0:T(8,128)(2,1)} %bitcast.51, bf16[8,16,32,128]{3,2,1,0:T(8,128)(2,1)} %copy-done.1), custom_call_target="tpu_custom_call" | custom-call | tf_op jit(solution)/shard_map/hop/pallas_call | solution.py:373
  153.2 3.9 %all-to-all-start.7 = ((bf16[32,32,128]{2,1,0:T(8,128)(2,1)}), bf16[32,32,128]{2,1,0:T(8,128)(2,1)S(1)}, u32[]{:S(2)}, u32[]{:S(2)}) async-start(bf16[32,32,128]{2,1,0:T(8,128)(2,1)} %hop.11), calls=%async_computation.7 | async-start | bytes 524288 | tf_op jit(solution)/shard_map/all_to_all | solution.py:389
  157.1 0.7 collective-permute-start.4
  157.8 0.7 collective-permute-start.3
  158.5 0.7 collective-permute-start.2
  159.2 1.4 collective-permute-start.1
  160.6 1.4 collective-permute-start
  161.9 5.8 %all-to-all-done.7.rest_17_ = bf16[32,32,128]{2,1,0:T(8,128)(2,1)S(1)} async-done(((bf16[32,32,128]{2,1,0:T(8,128)(2,1)}), bf16[32,32,128]{2,1,0:T(8,128)(2,1)S(1)}, u32[]{:S(2)}, u32[]{:S(2)}) %all-to-all-start.7) | async-done | bytes 262176 | tf_op jit(solution)/shard_map/all_to_all | solution.py:389
  167.7 10.9 %collective-permute-start.6 = (bf16[32,32,128]{2,1,0:T(8,128)(2,1)S(1)}, bf16[32,32,128]{2,1,0:T(8,128)(2,1)S(1)}, u32[]{:S(2)}, u32[]{:S(2)}) collective-permute-start(bf16[32,32,128]{2,1,0:T(8,128)(2,1)S(1)} %all_to_all.44.got_ref.rest_8_), channel_id=1, source_target_pairs={{224,192},{225,193},{226,194},{227,195},{228,196},{229,197},{230,1... | collective-permute-start | bytes 786440 | tf_op jit(solution)/shard_map/ppermute | solution.py:401
  178.6 0.7 collective-permute-start.5
  179.3 1.3 collective-permute-start.13
  180.6 1.3 collective-permute-start.12
  181.9 1.3 collective-permute-start.11
  183.3 1.3 collective-permute-start.10
  184.6 1.3 collective-permute-start.9
  185.9 1.3 collective-permute-start.8
  187.2 5.1 %collective-permute-done.12.rest_15_ = bf16[32,32,128]{2,1,0:T(8,128)(2,1)S(1)} collective-permute-done((bf16[32,32,128]{2,1,0:T(8,128)(2,1)S(1)}, bf16[32,32,128]{2,1,0:T(8,128)(2,1)S(1)}, u32[]{:S(2)}, u32[]{:S(2)}) %collective-permute-start.12) | collective-permute-done | bytes 262176 | tf_op jit(solution)/shard_map/ppermute | solution.py:401
  192.3 0.7 copy-done.11
  193.0 1.3 collective-permute-start.7
  194.3 0.5 collective-permute-done.9.rest_12_
  194.8 2.8 %collective-permute-done.8.rest_11_ = bf16[32,32,128]{2,1,0:T(8,128)(2,1)} collective-permute-done((bf16[32,32,128]{2,1,0:T(8,128)(2,1)S(1)}, bf16[32,32,128]{2,1,0:T(8,128)(2,1)}, u32[]{:S(2)}, u32[]{:S(2)}) %collective-permute-start.8) | collective-permute-done | bytes 262176 | tf_op jit(solution)/shard_map/ppermute | solution.py:401
  197.6 4.4 %collective-permute-done.7.rest_10_ = bf16[32,32,128]{2,1,0:T(8,128)(2,1)} collective-permute-done((bf16[32,32,128]{2,1,0:T(8,128)(2,1)S(1)}, bf16[32,32,128]{2,1,0:T(8,128)(2,1)}, u32[]{:S(2)}, u32[]{:S(2)}) %collective-permute-start.7) | collective-permute-done | bytes 262176 | tf_op jit(solution)/shard_map/ppermute | solution.py:401
  202.0 6.4 %finish.1 = (bf16[1,32,128,256]{3,2,1,0:T(8,128)(2,1)}, bf16[1,32,64,256]{3,2,1,0:T(8,128)(2,1)}) custom-call(s32[1]{0:T(128)} %bitcast.level_ref, s32[64]{0:T(128)} %reshape.116.slot_ref, s32[32,128]{1,0:T(8,128)} %bitcast.62, bf16[32,128,256]{2,1,0:T(8,128)(2,1)} %bitcast.53, bf16[32,128,128]{2,1,0:T(8,128)(2,1)} %bitcast.57, ...), custom_call_target="tpu_custom_call" | custom-call | tf_op jit(solution)/shard_map/finish/pallas_call | solution.py:405
  (78 shorter events, 3.1 us)
Async XLA Ops:
  7.2 2.9 %copy-start = (s32[8,64,1024]{2,1,0:T(8,128)S(1)}, s32[8,64,1024]{2,1,0:T(8,128)}, u32[]{:S(2)}) copy-start(s32[8,64,1024]{2,1,0:T(8,128)} %param.11) | copy-start | bytes 6291460
  7.2 53.5 %all-gather.7.cloned.1.call-start = ((), (), s32[]{:S(2)}) async-start(), calls=%async_computation.8 | async-start | bytes 4718592 | tf_op jit(solution)/shard_map/all_gather | solution.py:342
  17.8 5.8 %copy-start.14 = (s32[8,1024,1]{1,2,0:T(1,128)S(1)}, s32[8,1024,1]{1,2,0:T(1,128)}, u32[]{:S(2)}) copy-start(s32[8,1024,1]{1,2,0:T(1,128)} %param.9) | copy-start | bytes 98308
  17.8 6.8 %copy-start.13 = (s32[8,1024]{1,0:T(8,128)S(1)}, s32[8,1024]{1,0:T(8,128)}, u32[]{:S(2)}) copy-start(s32[8,1024]{1,0:T(8,128)} %param.10) | copy-start | bytes 98308
  17.8 19.9 %all-to-all-start = ((bf16[8,16,32,128]{3,2,1,0:T(8,128)(2,1)}), bf16[8,16,32,128]{3,2,1,0:T(8,128)(2,1)S(1)}, u32[]{:S(2)}, u32[]{:S(2)}) async-start(bf16[8,16,32,128]{3,2,1,0:T(8,128)(2,1)} %get-tuple-element.8), calls=%async_computation | async-start | bytes 2097152 | tf_op jit(solution)/shard_map/all_to_all | solution.py:343
  37.7 23.0 %copy-start.1 = (bf16[8,16,32,128]{3,2,1,0:T(8,128)(2,1)}, bf16[8,16,32,128]{3,2,1,0:T(8,128)(2,1)S(1)}, u32[]{:S(2)}) copy-start(bf16[8,16,32,128]{3,2,1,0:T(8,128)(2,1)S(1)} %all-to-all-done.load_ref.all_load_ref) | copy-start | bytes 3145732
  38.5 0.7 copy-start.3
  39.2 21.5 %all-to-all-start.1 = ((bf16[32,32,128]{2,1,0:T(8,128)(2,1)}), bf16[32,32,128]{2,1,0:T(8,128)(2,1)S(1)}, u32[]{:S(2)}, u32[]{:S(2)}) async-start(bf16[32,32,128]{2,1,0:T(8,128)(2,1)} %copy-done.3), calls=%async_computation.1 | async-start | bytes 524288 | tf_op jit(solution)/shard_map/all_to_all | solution.py:389
  50.3 99.4 %all-gather.9.cloned.1.call-start = ((), (), s32[]{:S(2)}) async-start(), calls=%async_computation.9 | async-start | bytes 7077888 | tf_op jit(solution)/shard_map/all_gather | solution.py:392
  98.1 96.2 %all-gather.11.cloned.1.call-start = ((), (), s32[]{:S(2)}) async-start(), calls=%async_computation.10 | async-start | bytes 4718592 | tf_op jit(solution)/shard_map/all_gather | solution.py:392
  149.7 28.9 %copy-start.2 = (bf16[32,32,128]{2,1,0:T(8,128)(2,1)}, bf16[32,32,128]{2,1,0:T(8,128)(2,1)S(1)}, u32[]{:S(2)}) copy-start(bf16[32,32,128]{2,1,0:T(8,128)(2,1)S(1)} %all_to_all.44.got_ref.rest_8_) | copy-start | bytes 786436
  153.2 14.5 %all-to-all-start.7 = ((bf16[32,32,128]{2,1,0:T(8,128)(2,1)}), bf16[32,32,128]{2,1,0:T(8,128)(2,1)S(1)}, u32[]{:S(2)}, u32[]{:S(2)}) async-start(bf16[32,32,128]{2,1,0:T(8,128)(2,1)} %hop.11), calls=%async_computation.7 | async-start | bytes 524288 | tf_op jit(solution)/shard_map/all_to_all | solution.py:389
  157.1 10.6 %collective-permute-start.4 = (bf16[32,32,128]{2,1,0:T(8,128)(2,1)S(1)}, bf16[32,32,128]{2,1,0:T(8,128)(2,1)S(1)}, u32[]{:S(2)}, u32[]{:S(2)}) collective-permute-start(bf16[32,32,128]{2,1,0:T(8,128)(2,1)S(1)} %all_to_all.44.got_ref.rest_8_), channel_id=1, source_target_pairs={{128,192},{129,193},{130,194},{131,195},{132,196},{133,197},{134,1... | collective-permute-start | bytes 786440 | tf_op jit(solution)/shard_map/ppermute | solution.py:401
  157.8 20.8 %collective-permute-start.3 = (bf16[32,32,128]{2,1,0:T(8,128)(2,1)S(1)}, bf16[32,32,128]{2,1,0:T(8,128)(2,1)S(1)}, u32[]{:S(2)}, u32[]{:S(2)}) collective-permute-start(bf16[32,32,128]{2,1,0:T(8,128)(2,1)S(1)} %all_to_all.44.got_ref.rest_8_), channel_id=1, source_target_pairs={{96,192},{97,193},{98,194},{99,195},{100,196},{101,197},{102,198},... | collective-permute-start | bytes 786440 | tf_op jit(solution)/shard_map/ppermute | solution.py:401
  158.5 20.8 %collective-permute-start.2 = (bf16[32,32,128]{2,1,0:T(8,128)(2,1)S(1)}, bf16[32,32,128]{2,1,0:T(8,128)(2,1)S(1)}, u32[]{:S(2)}, u32[]{:S(2)}) collective-permute-start(bf16[32,32,128]{2,1,0:T(8,128)(2,1)S(1)} %all_to_all.44.got_ref.rest_8_), channel_id=1, source_target_pairs={{64,192},{65,193},{66,194},{67,195},{68,196},{69,197},{70,198},{71... | collective-permute-start | bytes 786440 | tf_op jit(solution)/shard_map/ppermute | solution.py:401
  159.2 21.4 %collective-permute-start.1 = (bf16[32,32,128]{2,1,0:T(8,128)(2,1)S(1)}, bf16[32,32,128]{2,1,0:T(8,128)(2,1)}, u32[]{:S(2)}, u32[]{:S(2)}) collective-permute-start(bf16[32,32,128]{2,1,0:T(8,128)(2,1)S(1)} %all_to_all.44.got_ref.rest_8_), channel_id=1, source_target_pairs={{32,192},{33,193},{34,194},{35,195},{36,196},{37,197},{38,198},{39... | collective-permute-start | bytes 786440 | tf_op jit(solution)/shard_map/ppermute | solution.py:401
  160.6 21.4 %collective-permute-start = (bf16[32,32,128]{2,1,0:T(8,128)(2,1)S(1)}, bf16[32,32,128]{2,1,0:T(8,128)(2,1)}, u32[]{:S(2)}, u32[]{:S(2)}) collective-permute-start(bf16[32,32,128]{2,1,0:T(8,128)(2,1)S(1)} %all_to_all.44.got_ref.rest_8_), channel_id=1, source_target_pairs={{0,192},{1,193},{2,194},{3,195},{4,196},{5,197},{6,198},{7,199},{8... | collective-permute-start | bytes 786440 | tf_op jit(solution)/shard_map/ppermute | solution.py:401
  167.7 34.3 %copy-start.4 = (bf16[32,32,128]{2,1,0:T(8,128)(2,1)}, bf16[32,32,128]{2,1,0:T(8,128)(2,1)S(1)}, u32[]{:S(2)}) copy-start(bf16[32,32,128]{2,1,0:T(8,128)(2,1)S(1)} %all-to-all-done.7.rest_17_) | copy-start | bytes 786436
  167.7 34.3 %copy-start.5 = (bf16[32,32,128]{2,1,0:T(8,128)(2,1)}, bf16[32,32,128]{2,1,0:T(8,128)(2,1)S(1)}, u32[]{:S(2)}) copy-start(bf16[32,32,128]{2,1,0:T(8,128)(2,1)S(1)} %collective-permute-done.4.rest_6_) | copy-start | bytes 786436
  167.7 15.5 %collective-permute-start.6 = (bf16[32,32,128]{2,1,0:T(8,128)(2,1)S(1)}, bf16[32,32,128]{2,1,0:T(8,128)(2,1)S(1)}, u32[]{:S(2)}, u32[]{:S(2)}) collective-permute-start(bf16[32,32,128]{2,1,0:T(8,128)(2,1)S(1)} %all_to_all.44.got_ref.rest_8_), channel_id=1, source_target_pairs={{224,192},{225,193},{226,194},{227,195},{228,196},{229,197},{230,1... | collective-permute-start | bytes 786440 | tf_op jit(solution)/shard_map/ppermute | solution.py:401
  178.6 23.4 %copy-start.6 = (bf16[32,32,128]{2,1,0:T(8,128)(2,1)}, bf16[32,32,128]{2,1,0:T(8,128)(2,1)S(1)}, u32[]{:S(2)}) copy-start(bf16[32,32,128]{2,1,0:T(8,128)(2,1)S(1)} %collective-permute-done.3.rest_5_) | copy-start | bytes 786436
  178.6 6.0 %collective-permute-start.5 = (bf16[32,32,128]{2,1,0:T(8,128)(2,1)S(1)}, bf16[32,32,128]{2,1,0:T(8,128)(2,1)S(1)}, u32[]{:S(2)}, u32[]{:S(2)}) collective-permute-start(bf16[32,32,128]{2,1,0:T(8,128)(2,1)S(1)} %all_to_all.44.got_ref.rest_8_), channel_id=1, source_target_pairs={{160,192},{161,193},{162,194},{163,195},{164,196},{165,197},{166,1... | collective-permute-start | bytes 786440 | tf_op jit(solution)/shard_map/ppermute | solution.py:401
  179.3 22.7 %copy-start.7 = (bf16[32,32,128]{2,1,0:T(8,128)(2,1)}, bf16[32,32,128]{2,1,0:T(8,128)(2,1)S(1)}, u32[]{:S(2)}) copy-start(bf16[32,32,128]{2,1,0:T(8,128)(2,1)S(1)} %collective-permute-done.2.rest_4_) | copy-start | bytes 786436
  179.3 6.6 %collective-permute-start.13 = (bf16[32,32,128]{2,1,0:T(8,128)(2,1)S(1)}, bf16[32,32,128]{2,1,0:T(8,128)(2,1)S(1)}, u32[]{:S(2)}, u32[]{:S(2)}) collective-permute-start(bf16[32,32,128]{2,1,0:T(8,128)(2,1)S(1)} %all-to-all-done.7.rest_17_), channel_id=1, source_target_pairs={{192,224},{193,225},{194,226},{195,227},{196,228},{197,229},{198,2... | collective-permute-start | bytes 786440 | tf_op jit(solution)/shard_map/ppermute | solution.py:401
  180.6 11.7 %collective-permute-start.12 = (bf16[32,32,128]{2,1,0:T(8,128)(2,1)S(1)}, bf16[32,32,128]{2,1,0:T(8,128)(2,1)S(1)}, u32[]{:S(2)}, u32[]{:S(2)}) collective-permute-start(bf16[32,32,128]{2,1,0:T(8,128)(2,1)S(1)} %all-to-all-done.7.rest_17_), channel_id=1, source_target_pairs={{160,224},{161,225},{162,226},{163,227},{164,228},{165,229},{166,2... | collective-permute-start | bytes 786440 | tf_op jit(solution)/shard_map/ppermute | solution.py:401
  181.9 12.4 %collective-permute-start.11 = (bf16[32,32,128]{2,1,0:T(8,128)(2,1)S(1)}, bf16[32,32,128]{2,1,0:T(8,128)(2,1)}, u32[]{:S(2)}, u32[]{:S(2)}) collective-permute-start(bf16[32,32,128]{2,1,0:T(8,128)(2,1)S(1)} %all-to-all-done.7.rest_17_), channel_id=1, source_target_pairs={{128,224},{129,225},{130,226},{131,227},{132,228},{133,229},{134,2... | collective-permute-start | bytes 786440 | tf_op jit(solution)/shard_map/ppermute | solution.py:401
  183.2 9.0 %copy-start.8 = (bf16[32,32,128]{2,1,0:T(8,128)(2,1)}, bf16[32,32,128]{2,1,0:T(8,128)(2,1)S(1)}, u32[]{:S(2)}) copy-start(bf16[32,32,128]{2,1,0:T(8,128)(2,1)S(1)} %collective-permute-done.6.rest_9_) | copy-start | bytes 786436
  183.3 11.1 %collective-permute-start.10 = (bf16[32,32,128]{2,1,0:T(8,128)(2,1)S(1)}, bf16[32,32,128]{2,1,0:T(8,128)(2,1)}, u32[]{:S(2)}, u32[]{:S(2)}) collective-permute-start(bf16[32,32,128]{2,1,0:T(8,128)(2,1)S(1)} %all-to-all-done.7.rest_17_), channel_id=1, source_target_pairs={{96,224},{97,225},{98,226},{99,227},{100,228},{101,229},{102,230},... | collective-permute-start | bytes 786440 | tf_op jit(solution)/shard_map/ppermute | solution.py:401
  184.6 7.7 %copy-start.9 = (bf16[32,32,128]{2,1,0:T(8,128)(2,1)}, bf16[32,32,128]{2,1,0:T(8,128)(2,1)S(1)}, u32[]{:S(2)}) copy-start(bf16[32,32,128]{2,1,0:T(8,128)(2,1)S(1)} %collective-permute-done.5.rest_7_) | copy-start | bytes 786436
  184.6 10.2 %collective-permute-start.9 = (bf16[32,32,128]{2,1,0:T(8,128)(2,1)S(1)}, bf16[32,32,128]{2,1,0:T(8,128)(2,1)S(1)}, u32[]{:S(2)}, u32[]{:S(2)}) collective-permute-start(bf16[32,32,128]{2,1,0:T(8,128)(2,1)S(1)} %all-to-all-done.7.rest_17_), channel_id=1, source_target_pairs={{64,224},{65,225},{66,226},{67,227},{68,228},{69,229},{70,230},{71... | collective-permute-start | bytes 786440 | tf_op jit(solution)/shard_map/ppermute | solution.py:401
  185.9 6.4 %copy-start.10 = (bf16[32,32,128]{2,1,0:T(8,128)(2,1)}, bf16[32,32,128]{2,1,0:T(8,128)(2,1)S(1)}, u32[]{:S(2)}) copy-start(bf16[32,32,128]{2,1,0:T(8,128)(2,1)S(1)} %collective-permute-done.13.rest_16_) | copy-start | bytes 786436
  185.9 11.7 %collective-permute-start.8 = (bf16[32,32,128]{2,1,0:T(8,128)(2,1)S(1)}, bf16[32,32,128]{2,1,0:T(8,128)(2,1)}, u32[]{:S(2)}, u32[]{:S(2)}) collective-permute-start(bf16[32,32,128]{2,1,0:T(8,128)(2,1)S(1)} %all-to-all-done.7.rest_17_), channel_id=1, source_target_pairs={{32,224},{33,225},{34,226},{35,227},{36,228},{37,229},{38,230},{39... | collective-permute-start | bytes 786440 | tf_op jit(solution)/shard_map/ppermute | solution.py:401
  192.3 0.7 copy-start.11
  193.0 9.0 %collective-permute-start.7 = (bf16[32,32,128]{2,1,0:T(8,128)(2,1)S(1)}, bf16[32,32,128]{2,1,0:T(8,128)(2,1)}, u32[]{:S(2)}, u32[]{:S(2)}) collective-permute-start(bf16[32,32,128]{2,1,0:T(8,128)(2,1)S(1)} %all-to-all-done.7.rest_17_), channel_id=1, source_target_pairs={{0,224},{1,225},{2,226},{3,227},{4,228},{5,229},{6,230},{7,231},{8... | collective-permute-start | bytes 786440 | tf_op jit(solution)/shard_map/ppermute | solution.py:401
  194.8 7.2 %copy-start.12 = (bf16[32,32,128]{2,1,0:T(8,128)(2,1)}, bf16[32,32,128]{2,1,0:T(8,128)(2,1)S(1)}, u32[]{:S(2)}) copy-start(bf16[32,32,128]{2,1,0:T(8,128)(2,1)S(1)} %collective-permute-done.9.rest_12_) | copy-start | bytes 786436
Sparse Core Ops, SparseCore 0:
  17.9 38.0 all-gather.6
  98.2 40.2 all-gather.8
  140.5 37.0 all-gather.10

commit v7 on v6

--- a/solution.py
+++ b/solution.py
@@ -393,12 +393,23 @@
         elif len(arrived) == hops:
             arrived[-1], early[0] = lax.optimization_barrier((arrived[-1], early[0]))
 
-    late = []
-    after = lax.optimization_barrier((arrived[-2], arrived[-1]))
-    for level in range(1 + sum(early_counts), levels):
-        for c in range(levels):
-            value = arrived[level] if c < 5 and level < hops else after[level - levels]
-            late.append(value if c == level else lax.ppermute(value, "level", [(c, level)]))
+    sixth, seventh = arrived[-2:]
+    second = levels - 2
+    shared = {0: levels - 3, 1: levels - 1}
+    early_sent = {
+        c: lax.ppermute(sixth, "level", [(c, second)]) for c in range(levels - 3)
+    }
+    last_sent = {}
+    for c in range(levels - 1):
+        if c in shared:
+            mixed = jnp.where(level_id == shared[c], sixth, seventh)
+            pairs_sent = [(c, levels - 1), (shared[c], second)]
+            last_sent[c] = lax.ppermute(mixed, "level", pairs_sent)
+        else:
+            last_sent[c] = lax.ppermute(seventh, "level", [(c, levels - 1)])
+    own_sent = {second: sixth} | {source: last_sent[c] for c, source in shared.items()}
+    late = [(early_sent | own_sent)[c] for c in range(levels)]
+    late += [(last_sent | {levels - 1: seventh})[c] for c in range(levels)]
 
     step = 16
     tail = lambda i: jnp.maximum(i - 1, 0)

time: 216 us -> 216 us (level)
  waiting for transfers between devices: 39.9 us -> 37.4 us
    ppermute x14 -> x12, waiting for transfers between devices: 12.8 us -> 10.3 us  [the longest x5 7.69 us: shards(): last_sent[c] = lax.ppermute(seventh, 'level', [(c, levels - 1)])]
    ppermute x14 -> x12, starting transfers between devices: 25.4 us -> 25.2 us  [the longest x2 14 us: shards(): last_sent[c] = lax.ppermute(mixed, 'level', pairs_sent)]
  transfers between devices with their start and end apart: 20 -> 18, of which waited for: 7 -> 7; matrix products, arithmetic and copies ran while one was open for 2% -> 2% of each run, Pallas kernels for 6% -> 6%
where the time goes in v7:
time: 216 us; the launch traced here: 214 us
  blocking collectives  73 us (34%)
  starting transfers between devices  46.1 us (21%)
  waiting for transfers between devices  37.4 us (17%)
  Pallas kernels  31.2 us (14%)
  between operations  14.2 us (7%)
  other arithmetic  6.72 us (3%)
  local copies, waits for them, and re-layouts  5.25 us (2%)
    all_to_all x5, blocking collectives, shards(): lax.all_to_all(send, 'grp', split_axis=0, concat_axis=0, tiled=True)  73 us
    pallas_call x6, Pallas kernels, shards(): pl.pallas_call(functools.partial(hop_kernel, level), in_specs=[SMEM_SPEC,...  17.8 us
    all_to_all x2, starting transfers between devices, shards(): lax.all_to_all(send, 'grp', split_axis=0, concat_axis=0, tiled=True)  15 us
    all_to_all x2, waiting for transfers between devices, shards(): lax.all_to_all(send, 'grp', split_axis=0, concat_axis=0, tiled=True)  14.6 us
    ppermute x2, starting transfers between devices, shards(): last_sent[c] = lax.ppermute(mixed, 'level', pairs_sent)  14 us
    all_to_all x1, waiting for transfers between devices, shards(): lax.all_to_all(load, 'level', split_axis=0, concat_axis=0, tiled=True)  12.4 us
    ppermute x5, waiting for transfers between devices, shards(): last_sent[c] = lax.ppermute(seventh, 'level', [(c, levels - 1)])  7.69 us
    ppermute x5, starting transfers between devices, shards(): last_sent[c] = lax.ppermute(seventh, 'level', [(c, levels - 1)])  6.45 us
  transfers between devices with their start and end apart: 18, of which 7 were waited for; matrix products, arithmetic and copies ran while one was open for 2% of the time, Pallas kernels for 6%

profile of v7, /device:TPU:25, one launch (start us, length us, event | category | flops | bytes accessed | tf_op | source)
XLA Modules:
  0.0 213.9 jit_solution(9981657365861278891)
XLA Ops:
  7.2 0.8 compare_reduce_fusion
  8.3 0.8 add_reduce_fusion
  9.4 0.6 reshape.116.slot_ref
  10.8 0.7 sub.25
  11.4 6.2 %prepare.1 = (bf16[32,64,128]{2,1,0:T(8,128)(2,1)}, bf16[8,16,32,128]{3,2,1,0:T(8,128)(2,1)}) custom-call(s32[64]{0:T(128)} %reshape.116.slot_ref, s32[32,128]{1,0:T(8,128)} %bitcast.61, bf16[32,128,256]{2,1,0:T(8,128)(2,1)} %bitcast.52, bf16[32,128,128]{2,1,0:T(8,128)(2,1)} %bitcast.56, bf16[32,64,128]{2,1,0:T(8,128)(2,1)} %bitcast.58), custom_call_target="tpu_custom_call" | custom-call | tf_op jit(solution)/shard_map/prepare/pallas_call | solution.py:321
  17.7 5.8 %all-to-all-start = ((bf16[8,16,32,128]{3,2,1,0:T(8,128)(2,1)}), bf16[8,16,32,128]{3,2,1,0:T(8,128)(2,1)S(1)}, u32[]{:S(2)}, u32[]{:S(2)}) async-start(bf16[8,16,32,128]{3,2,1,0:T(8,128)(2,1)} %get-tuple-element.6), calls=%async_computation | async-start | bytes 2097152 | tf_op jit(solution)/shard_map/all_to_all | solution.py:343
  24.6 0.6 slice_add_fusion
  25.2 12.4 %all-to-all-done.load_ref.all_load_ref = bf16[8,16,32,128]{3,2,1,0:T(8,128)(2,1)S(1)} async-done(((bf16[8,16,32,128]{3,2,1,0:T(8,128)(2,1)}), bf16[8,16,32,128]{3,2,1,0:T(8,128)(2,1)S(1)}, u32[]{:S(2)}, u32[]{:S(2)}) %all-to-all-start) | async-done | bytes 1048608 | tf_op jit(solution)/shard_map/all_to_all | solution.py:343
  37.6 0.8 first.1
  38.4 0.7 copy-done.3
  39.1 11.1 %all-to-all-start.1 = ((bf16[32,32,128]{2,1,0:T(8,128)(2,1)}), bf16[32,32,128]{2,1,0:T(8,128)(2,1)S(1)}, u32[]{:S(2)}, u32[]{:S(2)}) async-start(bf16[32,32,128]{2,1,0:T(8,128)(2,1)} %copy-done.3), calls=%async_computation.1 | async-start | bytes 524288 | tf_op jit(solution)/shard_map/all_to_all | solution.py:389
  50.3 0.8 sub.27
  51.7 8.9 %all-to-all-done.1.got_ref = bf16[32,32,128]{2,1,0:T(8,128)(2,1)S(1)} async-done(((bf16[32,32,128]{2,1,0:T(8,128)(2,1)}), bf16[32,32,128]{2,1,0:T(8,128)(2,1)S(1)}, u32[]{:S(2)}, u32[]{:S(2)}) %all-to-all-start.1) | async-done | bytes 262176 | tf_op jit(solution)/shard_map/all_to_all | solution.py:389
  60.6 2.8 %hop.6 = bf16[32,32,128]{2,1,0:T(8,128)(2,1)S(1)} custom-call(s32[7,64]{1,0:T(8,128)S(1)} %copy.60.take_ref, s32[7,64]{1,0:T(8,128)S(1)} %copy.61.slot_ref, bf16[32,32,128]{2,1,0:T(8,128)(2,1)S(1)} %all-to-all-done.1.got_ref, bf16[8,32,64,128]{3,2,1,0:T(8,128)(2,1)} %bitcast.46, bf16[8,16,32,128]{3,2,1,0:T(8,128)(2,1)} %copy-done.1), custom_call_target="tpu_custom_call" | custom-call | tf_op jit(solution)/shard_map/hop/pallas_call | solution.py:373
  63.5 15.8 %all_to_all.40.got_ref = bf16[32,32,128]{2,1,0:T(8,128)(2,1)S(1)} all-to-all(bf16[32,32,128]{2,1,0:T(8,128)(2,1)S(1)} %hop.6), channel_id=1, replica_groups=mesh['level'=8,'grp'=32] {'grp'}, dimensions={0} | all-to-all | bytes 524288 | tf_op jit(solution)/shard_map/all_to_all | solution.py:389
  79.3 2.8 %hop.7 = bf16[32,32,128]{2,1,0:T(8,128)(2,1)S(1)} custom-call(s32[7,64]{1,0:T(8,128)S(1)} %copy.60.take_ref, s32[7,64]{1,0:T(8,128)S(1)} %copy.61.slot_ref, bf16[32,32,128]{2,1,0:T(8,128)(2,1)S(1)} %all_to_all.40.got_ref, bf16[8,32,64,128]{3,2,1,0:T(8,128)(2,1)} %bitcast.47, bf16[8,16,32,128]{3,2,1,0:T(8,128)(2,1)} %copy-done.1), custom_call_target="tpu_custom_call" | custom-call | tf_op jit(solution)/shard_map/hop/pallas_call | solution.py:373
  82.1 15.1 %all_to_all.41.got_ref = bf16[32,32,128]{2,1,0:T(8,128)(2,1)S(1)} all-to-all(bf16[32,32,128]{2,1,0:T(8,128)(2,1)S(1)} %hop.7), channel_id=1, replica_groups=mesh['level'=8,'grp'=32] {'grp'}, dimensions={0} | all-to-all | bytes 524288 | tf_op jit(solution)/shard_map/all_to_all | solution.py:389
  97.2 1.0 pad_maximum_fusion
  98.2 2.8 %hop.8 = bf16[32,32,128]{2,1,0:T(8,128)(2,1)S(1)} custom-call(s32[7,64]{1,0:T(8,128)S(1)} %copy.60.take_ref, s32[7,64]{1,0:T(8,128)S(1)} %copy.61.slot_ref, bf16[32,32,128]{2,1,0:T(8,128)(2,1)S(1)} %all_to_all.41.got_ref, bf16[8,32,64,128]{3,2,1,0:T(8,128)(2,1)} %bitcast.48, bf16[8,16,32,128]{3,2,1,0:T(8,128)(2,1)} %copy-done.1), custom_call_target="tpu_custom_call" | custom-call | tf_op jit(solution)/shard_map/hop/pallas_call | solution.py:373
  101.1 14.1 %all_to_all.42.got_ref = bf16[32,32,128]{2,1,0:T(8,128)(2,1)S(1)} all-to-all(bf16[32,32,128]{2,1,0:T(8,128)(2,1)S(1)} %hop.8), channel_id=1, replica_groups=mesh['level'=8,'grp'=32] {'grp'}, dimensions={0} | all-to-all | bytes 524288 | tf_op jit(solution)/shard_map/all_to_all | solution.py:389
  115.1 2.9 %hop.9 = bf16[32,32,128]{2,1,0:T(8,128)(2,1)S(1)} custom-call(s32[7,64]{1,0:T(8,128)S(1)} %copy.60.take_ref, s32[7,64]{1,0:T(8,128)S(1)} %copy.61.slot_ref, bf16[32,32,128]{2,1,0:T(8,128)(2,1)S(1)} %all_to_all.42.got_ref, bf16[8,32,64,128]{3,2,1,0:T(8,128)(2,1)} %bitcast.49, bf16[8,16,32,128]{3,2,1,0:T(8,128)(2,1)} %copy-done.1), custom_call_target="tpu_custom_call" | custom-call | tf_op jit(solution)/shard_map/hop/pallas_call | solution.py:373
  118.0 14.1 %all_to_all.43.got_ref = bf16[32,32,128]{2,1,0:T(8,128)(2,1)S(1)} all-to-all(bf16[32,32,128]{2,1,0:T(8,128)(2,1)S(1)} %hop.9), channel_id=1, replica_groups=mesh['level'=8,'grp'=32] {'grp'}, dimensions={0} | all-to-all | bytes 524288 | tf_op jit(solution)/shard_map/all_to_all | solution.py:389
  132.1 0.9 pad_maximum_fusion.1
  133.0 2.8 %hop.10 = bf16[32,32,128]{2,1,0:T(8,128)(2,1)S(1)} custom-call(s32[7,64]{1,0:T(8,128)S(1)} %copy.60.take_ref, s32[7,64]{1,0:T(8,128)S(1)} %copy.61.slot_ref, bf16[32,32,128]{2,1,0:T(8,128)(2,1)S(1)} %all_to_all.43.got_ref, bf16[8,32,64,128]{3,2,1,0:T(8,128)(2,1)} %bitcast.50, bf16[8,16,32,128]{3,2,1,0:T(8,128)(2,1)} %copy-done.1), custom_call_target="tpu_custom_call" | custom-call | tf_op jit(solution)/shard_map/hop/pallas_call | solution.py:373
  135.9 14.0 %all_to_all.44.got_ref.rest_8_ = bf16[32,32,128]{2,1,0:T(8,128)(2,1)S(1)} all-to-all(bf16[32,32,128]{2,1,0:T(8,128)(2,1)S(1)} %hop.10), channel_id=1, replica_groups=mesh['level'=8,'grp'=32] {'grp'}, dimensions={0} | all-to-all | bytes 524288 | tf_op jit(solution)/shard_map/all_to_all | solution.py:389
  149.8 3.5 %hop.11 = bf16[32,32,128]{2,1,0:T(8,128)(2,1)} custom-call(s32[7,64]{1,0:T(8,128)S(1)} %copy.60.take_ref, s32[7,64]{1,0:T(8,128)S(1)} %copy.61.slot_ref, bf16[32,32,128]{2,1,0:T(8,128)(2,1)S(1)} %all_to_all.44.got_ref.rest_8_, bf16[8,32,64,128]{3,2,1,0:T(8,128)(2,1)} %bitcast.51, bf16[8,16,32,128]{3,2,1,0:T(8,128)(2,1)} %copy-done.1), custom_call_target="tpu_custom_call" | custom-call | tf_op jit(solution)/shard_map/hop/pallas_call | solution.py:373
  153.4 3.9 %all-to-all-start.7 = ((bf16[32,32,128]{2,1,0:T(8,128)(2,1)}), bf16[32,32,128]{2,1,0:T(8,128)(2,1)S(1)}, u32[]{:S(2)}, u32[]{:S(2)}) async-start(bf16[32,32,128]{2,1,0:T(8,128)(2,1)} %hop.11), calls=%async_computation.7 | async-start | bytes 524288 | tf_op jit(solution)/shard_map/all_to_all | solution.py:389
  157.3 0.7 collective-permute-start.4
  158.0 0.7 collective-permute-start.3
  158.7 0.7 collective-permute-start.2
  159.3 1.4 collective-permute-start.1
  160.7 1.4 collective-permute-start
  162.1 5.8 %all-to-all-done.7.rest_17_ = bf16[32,32,128]{2,1,0:T(8,128)(2,1)S(1)} async-done(((bf16[32,32,128]{2,1,0:T(8,128)(2,1)}), bf16[32,32,128]{2,1,0:T(8,128)(2,1)S(1)}, u32[]{:S(2)}, u32[]{:S(2)}) %all-to-all-start.7) | async-done | bytes 262176 | tf_op jit(solution)/shard_map/all_to_all | solution.py:389
  167.9 1.3 collective-permute-start.11
  169.2 1.3 collective-permute-start.10
  170.5 0.8 broadcast_select_fusion
  171.3 0.7 copy-done.9
  172.0 12.7 %collective-permute-start.6 = (bf16[32,32,128]{2,1,0:T(8,128)(2,1)}, bf16[32,32,128]{2,1,0:T(8,128)(2,1)S(1)}, u32[]{:S(2)}, u32[]{:S(2)}) collective-permute-start(bf16[32,32,128]{2,1,0:T(8,128)(2,1)} %get-tuple-element.20), channel_id=1, source_target_pairs={{32,224},{224,192},{33,225},{225,193},{34,226},{226,194},{35,227},... | collective-permute-start | bytes 786440 | tf_op jit(solution)/shard_map/ppermute | solution.py:407
  184.7 1.3 collective-permute-start.9
  186.0 1.3 collective-permute-start.8
  187.4 1.3 collective-permute-start.7
  188.7 1.3 collective-permute-start.5
  190.0 2.5 %collective-permute-done.9.rest_14_ = bf16[32,32,128]{2,1,0:T(8,128)(2,1)} collective-permute-done((bf16[32,32,128]{2,1,0:T(8,128)(2,1)S(1)}, bf16[32,32,128]{2,1,0:T(8,128)(2,1)}, u32[]{:S(2)}, u32[]{:S(2)}) %collective-permute-start.9) | collective-permute-done | bytes 262176 | tf_op jit(solution)/shard_map/ppermute | solution.py:409
  192.5 3.2 %collective-permute-done.8.rest_13_ = bf16[32,32,128]{2,1,0:T(8,128)(2,1)} collective-permute-done((bf16[32,32,128]{2,1,0:T(8,128)(2,1)S(1)}, bf16[32,32,128]{2,1,0:T(8,128)(2,1)}, u32[]{:S(2)}, u32[]{:S(2)}) %collective-permute-start.8) | collective-permute-done | bytes 262176 | tf_op jit(solution)/shard_map/ppermute | solution.py:409
  195.7 2.0 collective-permute-done.7.rest_12_
  197.7 2.6 %collective-permute-done.5.rest_7_.rest_10_ = bf16[32,32,128]{2,1,0:T(8,128)(2,1)S(1)} collective-permute-done((bf16[32,32,128]{2,1,0:T(8,128)(2,1)}, bf16[32,32,128]{2,1,0:T(8,128)(2,1)S(1)}, u32[]{:S(2)}, u32[]{:S(2)}) %collective-permute-start.5) | collective-permute-done | bytes 262176 | tf_op jit(solution)/shard_map/ppermute | solution.py:407
  200.3 0.7 copy-done.6
  201.0 6.4 %finish.1 = (bf16[1,32,128,256]{3,2,1,0:T(8,128)(2,1)}, bf16[1,32,64,256]{3,2,1,0:T(8,128)(2,1)}) custom-call(s32[1]{0:T(128)} %bitcast.level_ref, s32[64]{0:T(128)} %reshape.116.slot_ref, s32[32,128]{1,0:T(8,128)} %bitcast.62, bf16[32,128,256]{2,1,0:T(8,128)(2,1)} %bitcast.53, bf16[32,128,128]{2,1,0:T(8,128)(2,1)} %bitcast.57, ...), custom_call_target="tpu_custom_call" | custom-call | tf_op jit(solution)/shard_map/finish/pallas_call | solution.py:416
  (69 shorter events, 3.1 us)
Async XLA Ops:
  7.2 2.9 %copy-start = (s32[8,64,1024]{2,1,0:T(8,128)S(1)}, s32[8,64,1024]{2,1,0:T(8,128)}, u32[]{:S(2)}) copy-start(s32[8,64,1024]{2,1,0:T(8,128)} %param.11) | copy-start | bytes 6291460
  7.2 53.4 %all-gather.7.cloned.1.call-start = ((), (), s32[]{:S(2)}) async-start(), calls=%async_computation.8 | async-start | bytes 4718592 | tf_op jit(solution)/shard_map/all_gather | solution.py:342
  17.7 5.8 %copy-start.11 = (s32[8,1024,1]{1,2,0:T(1,128)S(1)}, s32[8,1024,1]{1,2,0:T(1,128)}, u32[]{:S(2)}) copy-start(s32[8,1024,1]{1,2,0:T(1,128)} %param.9) | copy-start | bytes 98308
  17.7 6.9 %copy-start.10 = (s32[8,1024]{1,0:T(8,128)S(1)}, s32[8,1024]{1,0:T(8,128)}, u32[]{:S(2)}) copy-start(s32[8,1024]{1,0:T(8,128)} %param.10) | copy-start | bytes 98308
  17.7 19.9 %all-to-all-start = ((bf16[8,16,32,128]{3,2,1,0:T(8,128)(2,1)}), bf16[8,16,32,128]{3,2,1,0:T(8,128)(2,1)S(1)}, u32[]{:S(2)}, u32[]{:S(2)}) async-start(bf16[8,16,32,128]{3,2,1,0:T(8,128)(2,1)} %get-tuple-element.6), calls=%async_computation | async-start | bytes 2097152 | tf_op jit(solution)/shard_map/all_to_all | solution.py:343
  37.6 23.0 %copy-start.1 = (bf16[8,16,32,128]{3,2,1,0:T(8,128)(2,1)}, bf16[8,16,32,128]{3,2,1,0:T(8,128)(2,1)S(1)}, u32[]{:S(2)}) copy-start(bf16[8,16,32,128]{3,2,1,0:T(8,128)(2,1)S(1)} %all-to-all-done.load_ref.all_load_ref) | copy-start | bytes 3145732
  38.4 0.7 copy-start.3
  39.1 21.5 %all-to-all-start.1 = ((bf16[32,32,128]{2,1,0:T(8,128)(2,1)}), bf16[32,32,128]{2,1,0:T(8,128)(2,1)S(1)}, u32[]{:S(2)}, u32[]{:S(2)}) async-start(bf16[32,32,128]{2,1,0:T(8,128)(2,1)} %copy-done.3), calls=%async_computation.1 | async-start | bytes 524288 | tf_op jit(solution)/shard_map/all_to_all | solution.py:389
  50.2 99.6 %all-gather.9.cloned.1.call-start = ((), (), s32[]{:S(2)}) async-start(), calls=%async_computation.9 | async-start | bytes 7077888 | tf_op jit(solution)/shard_map/all_gather | solution.py:392
  98.2 91.8 %all-gather.11.cloned.1.call-start = ((), (), s32[]{:S(2)}) async-start(), calls=%async_computation.10 | async-start | bytes 4718592 | tf_op jit(solution)/shard_map/all_gather | solution.py:392
  149.8 20.6 %copy-start.2 = (bf16[32,32,128]{2,1,0:T(8,128)(2,1)}, bf16[32,32,128]{2,1,0:T(8,128)(2,1)S(1)}, u32[]{:S(2)}) copy-start(bf16[32,32,128]{2,1,0:T(8,128)(2,1)S(1)} %all_to_all.44.got_ref.rest_8_) | copy-start | bytes 786436
  153.4 14.5 %all-to-all-start.7 = ((bf16[32,32,128]{2,1,0:T(8,128)(2,1)}), bf16[32,32,128]{2,1,0:T(8,128)(2,1)S(1)}, u32[]{:S(2)}, u32[]{:S(2)}) async-start(bf16[32,32,128]{2,1,0:T(8,128)(2,1)} %hop.11), calls=%async_computation.7 | async-start | bytes 524288 | tf_op jit(solution)/shard_map/all_to_all | solution.py:389
  157.3 4.8 %collective-permute-start.4 = (bf16[32,32,128]{2,1,0:T(8,128)(2,1)S(1)}, bf16[32,32,128]{2,1,0:T(8,128)(2,1)S(1)}, u32[]{:S(2)}, u32[]{:S(2)}) collective-permute-start(bf16[32,32,128]{2,1,0:T(8,128)(2,1)S(1)} %all_to_all.44.got_ref.rest_8_), channel_id=1, source_target_pairs={{128,192},{129,193},{130,194},{131,195},{132,196},{133,197},{134,1... | collective-permute-start | bytes 786440 | tf_op jit(solution)/shard_map/ppermute | solution.py:400
  158.0 11.2 %collective-permute-start.3 = (bf16[32,32,128]{2,1,0:T(8,128)(2,1)S(1)}, bf16[32,32,128]{2,1,0:T(8,128)(2,1)S(1)}, u32[]{:S(2)}, u32[]{:S(2)}) collective-permute-start(bf16[32,32,128]{2,1,0:T(8,128)(2,1)S(1)} %all_to_all.44.got_ref.rest_8_), channel_id=1, source_target_pairs={{96,192},{97,193},{98,194},{99,195},{100,196},{101,197},{102,198},... | collective-permute-start | bytes 786440 | tf_op jit(solution)/shard_map/ppermute | solution.py:400
  158.7 12.7 %collective-permute-start.2 = (bf16[32,32,128]{2,1,0:T(8,128)(2,1)S(1)}, bf16[32,32,128]{2,1,0:T(8,128)(2,1)S(1)}, u32[]{:S(2)}, u32[]{:S(2)}) collective-permute-start(bf16[32,32,128]{2,1,0:T(8,128)(2,1)S(1)} %all_to_all.44.got_ref.rest_8_), channel_id=1, source_target_pairs={{64,192},{65,193},{66,194},{67,195},{68,196},{69,197},{70,198},{71... | collective-permute-start | bytes 786440 | tf_op jit(solution)/shard_map/ppermute | solution.py:400
  159.3 25.4 %collective-permute-start.1 = (bf16[32,32,128]{2,1,0:T(8,128)(2,1)S(1)}, bf16[32,32,128]{2,1,0:T(8,128)(2,1)}, u32[]{:S(2)}, u32[]{:S(2)}) collective-permute-start(bf16[32,32,128]{2,1,0:T(8,128)(2,1)S(1)} %all_to_all.44.got_ref.rest_8_), channel_id=1, source_target_pairs={{32,192},{33,193},{34,194},{35,195},{36,196},{37,197},{38,198},{39... | collective-permute-start | bytes 786440 | tf_op jit(solution)/shard_map/ppermute | solution.py:400
  160.7 25.3 %collective-permute-start = (bf16[32,32,128]{2,1,0:T(8,128)(2,1)S(1)}, bf16[32,32,128]{2,1,0:T(8,128)(2,1)}, u32[]{:S(2)}, u32[]{:S(2)}) collective-permute-start(bf16[32,32,128]{2,1,0:T(8,128)(2,1)S(1)} %all_to_all.44.got_ref.rest_8_), channel_id=1, source_target_pairs={{0,192},{1,193},{2,194},{3,195},{4,196},{5,197},{6,198},{7,199},{8... | collective-permute-start | bytes 786440 | tf_op jit(solution)/shard_map/ppermute | solution.py:400
  162.1 38.2 %copy-start.7 = (bf16[32,32,128]{2,1,0:T(8,128)(2,1)}, bf16[32,32,128]{2,1,0:T(8,128)(2,1)S(1)}, u32[]{:S(2)}) copy-start(bf16[32,32,128]{2,1,0:T(8,128)(2,1)S(1)} %collective-permute-done.4.rest_6_) | copy-start | bytes 786436
  167.9 32.4 %copy-start.4 = (bf16[32,32,128]{2,1,0:T(8,128)(2,1)}, bf16[32,32,128]{2,1,0:T(8,128)(2,1)S(1)}, u32[]{:S(2)}) copy-start(bf16[32,32,128]{2,1,0:T(8,128)(2,1)S(1)} %all-to-all-done.7.rest_17_) | copy-start | bytes 786436
  167.9 19.5 %collective-permute-start.11 = (bf16[32,32,128]{2,1,0:T(8,128)(2,1)S(1)}, bf16[32,32,128]{2,1,0:T(8,128)(2,1)}, u32[]{:S(2)}, u32[]{:S(2)}) collective-permute-start(bf16[32,32,128]{2,1,0:T(8,128)(2,1)S(1)} %all-to-all-done.7.rest_17_), channel_id=1, source_target_pairs={{192,224},{193,225},{194,226},{195,227},{196,228},{197,229},{198,2... | collective-permute-start | bytes 786440 | tf_op jit(solution)/shard_map/ppermute | solution.py:409
  169.2 31.1 %copy-start.8 = (bf16[32,32,128]{2,1,0:T(8,128)(2,1)}, bf16[32,32,128]{2,1,0:T(8,128)(2,1)S(1)}, u32[]{:S(2)}) copy-start(bf16[32,32,128]{2,1,0:T(8,128)(2,1)S(1)} %collective-permute-done.3.rest_5_) | copy-start | bytes 786436
  169.2 19.5 %collective-permute-start.10 = (bf16[32,32,128]{2,1,0:T(8,128)(2,1)S(1)}, bf16[32,32,128]{2,1,0:T(8,128)(2,1)}, u32[]{:S(2)}, u32[]{:S(2)}) collective-permute-start(bf16[32,32,128]{2,1,0:T(8,128)(2,1)S(1)} %all-to-all-done.7.rest_17_), channel_id=1, source_target_pairs={{160,224},{161,225},{162,226},{163,227},{164,228},{165,229},{166,2... | collective-permute-start | bytes 786440 | tf_op jit(solution)/shard_map/ppermute | solution.py:409
  171.3 0.7 copy-start.9
  172.0 25.7 %collective-permute-start.6 = (bf16[32,32,128]{2,1,0:T(8,128)(2,1)}, bf16[32,32,128]{2,1,0:T(8,128)(2,1)S(1)}, u32[]{:S(2)}, u32[]{:S(2)}) collective-permute-start(bf16[32,32,128]{2,1,0:T(8,128)(2,1)} %get-tuple-element.20), channel_id=1, source_target_pairs={{32,224},{224,192},{33,225},{225,193},{34,226},{226,194},{35,227},... | collective-permute-start | bytes 786440 | tf_op jit(solution)/shard_map/ppermute | solution.py:407
  184.7 7.8 %collective-permute-start.9 = (bf16[32,32,128]{2,1,0:T(8,128)(2,1)S(1)}, bf16[32,32,128]{2,1,0:T(8,128)(2,1)}, u32[]{:S(2)}, u32[]{:S(2)}) collective-permute-start(bf16[32,32,128]{2,1,0:T(8,128)(2,1)S(1)} %all-to-all-done.7.rest_17_), channel_id=1, source_target_pairs={{128,224},{129,225},{130,226},{131,227},{132,228},{133,229},{134,2... | collective-permute-start | bytes 786440 | tf_op jit(solution)/shard_map/ppermute | solution.py:409
  186.0 9.6 %collective-permute-start.8 = (bf16[32,32,128]{2,1,0:T(8,128)(2,1)S(1)}, bf16[32,32,128]{2,1,0:T(8,128)(2,1)}, u32[]{:S(2)}, u32[]{:S(2)}) collective-permute-start(bf16[32,32,128]{2,1,0:T(8,128)(2,1)S(1)} %all-to-all-done.7.rest_17_), channel_id=1, source_target_pairs={{96,224},{97,225},{98,226},{99,227},{100,228},{101,229},{102,230},... | collective-permute-start | bytes 786440 | tf_op jit(solution)/shard_map/ppermute | solution.py:409
  187.4 10.3 %collective-permute-start.7 = (bf16[32,32,128]{2,1,0:T(8,128)(2,1)S(1)}, bf16[32,32,128]{2,1,0:T(8,128)(2,1)}, u32[]{:S(2)}, u32[]{:S(2)}) collective-permute-start(bf16[32,32,128]{2,1,0:T(8,128)(2,1)S(1)} %all-to-all-done.7.rest_17_), channel_id=1, source_target_pairs={{64,224},{65,225},{66,226},{67,227},{68,228},{69,229},{70,230},{71... | collective-permute-start | bytes 786440 | tf_op jit(solution)/shard_map/ppermute | solution.py:409
  188.7 11.6 %collective-permute-start.5 = (bf16[32,32,128]{2,1,0:T(8,128)(2,1)}, bf16[32,32,128]{2,1,0:T(8,128)(2,1)S(1)}, u32[]{:S(2)}, u32[]{:S(2)}) collective-permute-start(bf16[32,32,128]{2,1,0:T(8,128)(2,1)} %get-tuple-element.21), channel_id=1, source_target_pairs={{0,224},{160,192},{1,225},{161,193},{2,226},{162,194},{3,227},{163... | collective-permute-start | bytes 786440 | tf_op jit(solution)/shard_map/ppermute | solution.py:407
  197.7 2.6 %copy-start.5 = (bf16[32,32,128]{2,1,0:T(8,128)(2,1)}, bf16[32,32,128]{2,1,0:T(8,128)(2,1)S(1)}, u32[]{:S(2)}) copy-start(bf16[32,32,128]{2,1,0:T(8,128)(2,1)S(1)} %collective-permute-done.6.rest_9_.rest_11_) | copy-start | bytes 786436
  200.3 0.7 copy-start.6
Sparse Core Ops, SparseCore 0:
  17.9 38.0 all-gather.6
  98.3 40.1 all-gather.8
  140.4 37.7 all-gather.10
